TPU v7x, 32 devices: a whole 2x2x4 slice. The times are simulated.
32 devices in a mesh: dp: 2 (over y), mp: 16 (over z, x, core).
Axes of the slice: x: 2, y: 2, z: 4, core: 2. Of those that a mesh axis runs over, the one named last changes fastest.
Arguments:
- table_rows: bfloat16 [2, 16, 4608, 128], P('dp', 'mp'), may hold values from -6 to 6
- bag_ids: int32 [2, 16, 4608], P('dp', 'mp'), may hold values from 0 to 4095, never falling along the last dimension, each value on 1 to 8 neighbouring positions
- slot_feature: int32 [512], replicated, may hold values from 0 to 511, each once
- block_exponent: int32 [512, 4], replicated, may hold values from 0 to 3
- fm_project: bfloat16 [2, 512, 32], P(None, 'dp'), may hold values from -0.25 to 0.25
- fm_output: bfloat16 [2, 32, 128], P(None, 'dp'), may hold values from -0.09375 to 0.09375
- mix_weight: bfloat16 [2, 512, 512], P(None, 'dp'), may hold values from -0.25 to 0.25
- norm_gain: bfloat16 [2, 128], P(None, 'dp'), may hold values from 0.25 to 1.75
- out_cotangent: bfloat16 [256, 512, 128], P(('dp', 'mp')), may hold values from -6 to 6
Outputs:
- features_out: bfloat16 [256, 512, 128], P(('dp', 'mp'))
- row_grads: bfloat16 [2, 16, 4608, 128], P('dp', 'mp')
- grad_project: float32 [2, 512, 32], P(None, 'dp')
- grad_output: float32 [2, 32, 128], P(None, 'dp')
- grad_mix: float32 [2, 512, 512], P(None, 'dp')
- grad_gain: float32 [2, 128], P(None, 'dp')
Inputs may be any that keep to these rules, and one draw needn't show every extreme that they name: `bag_ids`: on each device the bag numbers never fall along the rows; every one of the 4096 bags has 1 to 8 rows, some bag exactly 8. `slot_feature`: each feature stands in exactly one slot.
All inputs are finite; a program needn't handle non-finite values.
Results may differ from a plain program's by a relative error of at most 0.013.
Values may be sent and summed in bfloat16 or wider, within the bound.
No kernel may reach another device: no remote copies, remote signals or barrier semaphores. Data moves between devices by JAX's collectives and lax.ppermute only.
A program may use at most 64 MiB of HBM per device.

v0:
```python
import jax
import jax.numpy as jnp
from jax import lax
from jax.sharding import PartitionSpec as P

F = 512
E = 128
LAYERS = 2
SAMP_DEV = 8
BAGS = 4096


EPS = 1e-05


def for_sending(x):

    def short(part):
        return part.astype(jnp.bfloat16) if part.dtype == jnp.float32 else part

    return jax.tree.map(short, x)


def product(form, left, right):
    return jnp.einsum(form, left, right, preferred_element_type=jnp.float32)


def layer_forward(acts, project, output, mixing, gain_row):
    projected = product("sfe,fk->sek", acts, project).astype(jnp.bfloat16)
    paired = product("sfe,sek->sfk", acts, projected).astype(jnp.bfloat16)
    total = (
        acts.astype(jnp.float32)
        + product("sfk,ke->sfe", paired, output)
        + product("gf,sfe->sge", mixing, acts)
    )
    centred = total - jnp.mean(total, axis=-1, keepdims=True)
    inverse_std = lax.rsqrt(jnp.mean(centred * centred, axis=-1, keepdims=True) + EPS)
    normed = centred * inverse_std
    result = (normed * gain_row.astype(jnp.float32)).astype(jnp.bfloat16)
    return (result, (projected, paired, normed, inverse_std))


def layer_backward(upstream, acts, project, output, mixing, gain_row, saved):
    projected, paired, normed, inverse_std = saved
    upper = upstream.astype(jnp.float32)
    grad_gain = jnp.sum(upper * normed, axis=(0, 1))
    scaled = upper * gain_row.astype(jnp.float32)
    grad_total = inverse_std * (
        scaled
        - jnp.mean(scaled, axis=-1, keepdims=True)
        - normed * jnp.mean(scaled * normed, axis=-1, keepdims=True)
    )
    total_low = grad_total.astype(jnp.bfloat16)
    grad_output = product("sfk,sfe->ke", paired, total_low)
    grad_paired = product("sfe,ke->sfk", total_low, output).astype(jnp.bfloat16)
    grad_mixing = product("sge,sfe->gf", total_low, acts)
    grad_projected = product("sfk,sfe->sek", grad_paired, acts).astype(jnp.bfloat16)
    grad_project = product("sfe,sek->fk", acts, grad_projected)
    grad_acts = (
        grad_total
        + product("gf,sge->sfe", mixing, total_low)
        + product("sfk,sek->sfe", grad_paired, projected)
        + product("fk,sek->sfe", project, grad_projected)
    )
    return (grad_acts.astype(jnp.bfloat16), (grad_project, grad_output, grad_mixing, grad_gain))


def per_device(
    table_rows,
    bag_ids,
    slot_feature,
    block_exponent,
    fm_project,
    fm_output,
    mix_weight,
    norm_gain,
    out_cotangent,
):
    tables = lax.axis_size("mp")
    f_dev = F // tables
    own_ids = bag_ids[0, 0]
    pooled = jax.ops.segment_sum(
        table_rows[0, 0].astype(jnp.float32), own_ids, num_segments=BAGS, indices_are_sorted=True
    )
    pooled = pooled.astype(jnp.bfloat16).reshape(-1, f_dev, E)
    slot_acts = lax.all_to_all(pooled, "mp", split_axis=0, concat_axis=1, tiled=True)
    inverse = jnp.zeros((F,), jnp.int32).at[slot_feature].set(jnp.arange(F, dtype=jnp.int32))
    scales = jnp.repeat(jnp.exp2((block_exponent - 2).astype(jnp.float32)), 32, axis=1)
    acts = (jnp.take(slot_acts, inverse, axis=1).astype(jnp.float32) * scales[None]).astype(
        jnp.bfloat16
    )
    project_all, output_all, mixing_all, gain_all = (
        lax.all_gather(fm_project, "dp", axis=1, tiled=True),
        lax.all_gather(fm_output, "dp", axis=1, tiled=True),
        lax.all_gather(mix_weight, "dp", axis=1, tiled=True),
        lax.all_gather(norm_gain, "dp", axis=1, tiled=True),
    )
    saved_all = []
    for layer in range(LAYERS):
        before = acts
        acts, saved = layer_forward(
            acts, project_all[layer], output_all[layer], mixing_all[layer], gain_all[layer]
        )
        saved_all.append((before, saved))
    upstream = out_cotangent
    collected = []
    for layer in reversed(range(LAYERS)):
        before, saved = saved_all[layer]
        upstream, grads = layer_backward(
            upstream,
            before,
            project_all[layer],
            output_all[layer],
            mixing_all[layer],
            gain_all[layer],
            saved,
        )
        collected.append(grads)
    collected = collected[::-1]
    partial_grads = tuple((jnp.stack([entry[index] for entry in collected]) for index in range(4)))
    slot_grads = (
        jnp.take(upstream, slot_feature, axis=1).astype(jnp.float32)
        * jnp.take(scales, slot_feature, axis=0)[None]
    ).astype(jnp.bfloat16)
    owner_grads = lax.all_to_all(slot_grads, "mp", split_axis=1, concat_axis=0, tiled=True)
    row_grads = owner_grads.reshape(BAGS, E)[own_ids].reshape(1, 1, -1, E)
    summed = lax.psum(partial_grads, "mp")
    shares = jax.tree.map(
        lambda part: part.astype(jnp.float32),
        lax.psum_scatter(for_sending(summed), "dp", scatter_dimension=1, tiled=True),
    )
    samples_all = SAMP_DEV * tables * lax.axis_size("dp")
    factor = 1.0 / jnp.sqrt(jnp.float32(samples_all))
    return (
        acts,
        row_grads,
        shares[0] * factor,
        shares[1] * factor,
        shares[2] * factor,
        shares[3] * factor,
    )


def solution(mesh):
    placed = (
        P("dp", "mp", None, None),
        P("dp", "mp", None),
        P(),
        P(),
        P(None, "dp", None),
        P(None, "dp", None),
        P(None, "dp", None),
        P(None, "dp"),
        P(("dp", "mp"), None, None),
    )
    return jax.shard_map(
        per_device,
        mesh=mesh,
        in_specs=placed,
        out_specs=(
            P(("dp", "mp"), None, None),
            P("dp", "mp", None, None),
            P(None, "dp", None),
            P(None, "dp", None),
            P(None, "dp", None),
            P(None, "dp"),
        ),
        check_vma=False,
    )
```

profile of v0, /device:TPU:0, one launch (start us, length us, event | category | flops | bytes accessed | tf_op | source)
XLA Modules:
  0.0 237.5 jit_solution(16351685328636935528)
XLA Ops:
  7.9 26.0 %scatter_custom_fusion = f32[4096,128]{1,0:T(8,128)S(1)} fusion(s32[4608]{0:T(1024)S(1)} %reduce, bf16[1,1,4608,128]{3,2,1,0:T(8,128)(2,1)} %param.11, f32[]{:T(128)} %constant.19.clone.1), kind=kCustom, calls=%fused_computation.16 | custom fusion | flops 1179648 | bytes 3276804 | tf_op jit(solution)/shard_map/scatter-add | solution.py:82
  33.9 1.1 convert_element_type.126
  35.0 7.5 %all-to-all-start = ((bf16[128,32,128]{2,1,0:T(8,128)(2,1)}), bf16[128,32,128]{2,1,0:T(8,128)(2,1)S(1)}, u32[]{:S(2)}, u32[]{:S(2)}) async-start(bf16[128,32,128]{2,1,0:T(8,128)(2,1)} %bitcast.1), calls=%async_computation | async-start | bytes 2097152 | tf_op jit(solution)/shard_map/all_to_all | solution.py:86
  43.3 4.2 %all-gather = bf16[2,64,2]{1,2,0:T(2,128)(2,1)S(1)} all-gather(bf16[1,64,2]{1,2,0:T(2,128)(2,1)S(1)} %bitcast.175), channel_id=1, replica_groups=mesh['dp'=2,'mp'=16] {'dp'}, dimensions={0}, use_global_device_ids=true | all-gather | bytes 768 | tf_op jit(solution)/shard_map/all_gather | solution.py:96
  47.7 2.4 %scatter_custom_fusion.1 = s32[512]{0:T(512)S(1)} fusion(s32[512]{0:T(512)S(1)} %compare_select_fusion.2, s32[512]{0:T(512)S(1)} %iota.3, s32[]{:T(128)} %constant.26.clone.1), kind=kCustom, calls=%fused_computation.99 | custom fusion | bytes 2052 | tf_op jit(solution)/shard_map/scatter | solution.py:87
  50.1 4.6 %all_gather.12 = bf16[2,512,32]{1,2,0:T(8,128)(2,1)S(1)} all-gather(bf16[2,256,32]{1,2,0:T(8,128)(2,1)S(1)} %copy-done.21), channel_id=1, replica_groups=mesh['dp'=2,'mp'=16] {'dp'}, dimensions={1}, use_global_device_ids=true | all-gather | bytes 98304 | tf_op jit(solution)/shard_map/all_gather | solution.py:93
  55.4 4.5 %all_gather.13 = bf16[2,32,128]{2,1,0:T(8,128)(2,1)S(1)} all-gather(bf16[2,16,128]{2,1,0:T(8,128)(2,1)S(1)} %copy-done.24), channel_id=1, replica_groups=mesh['dp'=2,'mp'=16] {'dp'}, dimensions={1}, use_global_device_ids=true | all-gather | bytes 24576 | tf_op jit(solution)/shard_map/all_gather | solution.py:94
  59.9 1.5 copy.99
  61.6 1.0 gather_fusion
  63.5 2.0 all-to-all-done
  66.3 1.8 gather_fusion.2
  69.9 1.8 fusion.27
  71.8 3.3 %fusion.31 = (f32[8,512]{1,0:T(8,128)S(1)}, f32[8,512,128]{1,2,0:T(8,128)S(1)}) fusion(bf16[2,512,512]{2,1,0:T(8,128)(2,1)} %all-gather.3.cloned.1.call-done, bf16[512,8,128]{0,2,1:T(8,128)(2,1)} %copy-done.3, f32[512,128]{0,1:T(8,128)S(1)} %bitcast.166, pred[512]{0:T(512)(128)(4,1)S(1)} %compare_and_fusion.1, f32[8,512,128]{1,2,0:T(8,128)} %fusion.27), kind=kOutput, calls=%fused_computation.103 | convolution fusion | flops 543158272 | bytes 7357440 | tf_op jit(solution)/shard_map/gf,sfe->sge/dot_general | solution.py:25
  80.3 1.8 fusion.23
  84.5 1.9 fusion.15
  90.4 1.5 pad_maximum_fusion
  94.8 78.1 %all-reduce.2 = (bf16[2,512,32]{1,2,0:T(8,128)(2,1)}, bf16[2,32,128]{2,1,0:T(8,128)(2,1)}, bf16[2,512,512]{2,1,0:T(8,128)(2,1)}, bf16[2,128]{1,0:T(2,128)(2,1)}) all-reduce(f32[2,512,32]{1,2,0:T(8,128)S(1)} %pad_maximum_fusion.1, f32[2,32,128]{2,1,0:T(8,128)} %pad_maximum_fusion.2, ...), channel_id=1, replica_groups=mesh['dp'=2,'mp'=16] {'mp'}, use_global_device_ids=true, to_apply=%region_10.12 | all-reduce | flops 565504 | bytes 3393024 | tf_op jit(solution)/shard_map/psum | solution.py:127
  173.0 1.4 copy.136
  174.5 2.7 %fusion.34 = f32[8,512,128]{1,2,0:T(8,128)} fusion(bf16[8,512,32]{1,2,0:T(8,128)(2,1)S(1)} %convolution_convert_fusion, bf16[8,128,32]{1,2,0:T(8,128)(2,1)} %copy-done.19), kind=kOutput, calls=%fused_computation.106 | convolution fusion | flops 33554432 | bytes 2424832 | tf_op jit(solution)/shard_map/sfk,sek->sfe/dot_general | solution.py:25
  177.2 2.6 %fusion.24 = f32[8,128,512]{2,1,0:T(8,128)} fusion(bf16[8,128,32]{1,2,0:T(8,128)(2,1)} %copy-done.20, bf16[2,512,32]{1,2,0:T(8,128)(2,1)S(1)} %copy-done.11), kind=kOutput, calls=%fused_computation.73 | convolution fusion | flops 33554432 | bytes 2195456 | tf_op jit(solution)/shard_map/fk,sek->sfe/dot_general | solution.py:25
  180.0 4.8 %fusion.16 = bf16[8,512,128]{1,2,0:T(8,128)(2,1)} fusion(f32[8,128,512]{2,1,0:T(8,128)} %fusion.24, f32[8,512,128]{1,2,0:T(8,128)} %fusion.34, bf16[8,512,128]{1,2,0:T(8,128)(2,1)S(1)} %fusion.22, bf16[2,512,512]{2,1,0:T(8,128)(2,1)} %all-gather.3.cloned.1.call-done, f32[8,512]{1,0:T(8,128)S(1)} %copy-done.15, f32[8,512,128]{1,2,0:T(8,128)S(1)} %get-tuple-element.46, ...), kind=kOutput, calls=%fused_computation.28 | convolution fusion | flops 543162368 | bytes 10027520 | tf_op jit(solution)/shard_map/gf,sge->sfe/dot_general | solution.py:25
  184.8 1.7 copy.105
  186.5 1.8 gather_fusion.3
  188.4 3.5 %multiply_convert_fusion = bf16[8,512,128]{2,0,1:T(8,128)(2,1)} fusion(bf16[512,8,128]{2,1,0:T(8,128)(2,1)S(1)} %gather_fusion.3, f32[512,128]{1,0:T(8,128)S(1)} %copy-done.2, pred[512]{0:T(512)(128)(4,1)S(1)} %copy-done.30), kind=kLoop, calls=%fused_computation.37 | loop fusion | flops 2097152 | bytes 2359808 | tf_op jit(solution)/shard_map/convert_element_type | solution.py:124
  191.9 3.7 %all-to-all-start.1 = ((bf16[8,512,128]{2,0,1:T(8,128)(2,1)}), bf16[8,512,128]{2,0,1:T(8,128)(2,1)S(1)}, u32[]{:S(2)}, u32[]{:S(2)}) async-start(bf16[8,512,128]{2,0,1:T(8,128)(2,1)} %multiply_convert_fusion), calls=%async_computation.1 | async-start | bytes 2097152 | tf_op jit(solution)/shard_map/all_to_all | solution.py:125
  195.6 1.3 copy.117
  198.3 1.3 convert_multiply_fusion.6
  199.6 6.0 %reduce-scatter.7.cloned.1.call-done = bf16[2,256,32]{1,2,0:T(8,128)(2,1)} async-done(((bf16[2,512,32]{1,2,0:T(8,128)(2,1)}), bf16[2,256,32]{1,2,0:T(8,128)(2,1)}) %reduce-scatter.7.cloned.1.call-update) | async-done | bytes 32784 | tf_op jit(solution)/shard_map/reduce_scatter | solution.py:130
  205.6 1.4 convert_multiply_fusion.5
  207.0 11.4 %all-to-all-done.1 = bf16[8,512,128]{2,0,1:T(8,128)(2,1)S(1)} async-done(((bf16[8,512,128]{2,0,1:T(8,128)(2,1)}), bf16[8,512,128]{2,0,1:T(8,128)(2,1)S(1)}, u32[]{:S(2)}, u32[]{:S(2)}) %all-to-all-start.1) | async-done | bytes 1048608 | tf_op jit(solution)/shard_map/all_to_all | solution.py:125
  218.7 10.2 %gather_fusion.1 = bf16[4608,128]{1,0:T(8,128)(2,1)} fusion(bf16[4096,128]{1,0:T(8,128)(2,1)S(1)} %bitcast.158, s32[5120]{0:T(1024)S(1)} %pad_clamp_fusion), kind=kCustom, calls=%fused_computation.3 | custom fusion | bytes 2377728 | tf_op jit(solution)/shard_map/gather | solution.py:126
  228.9 2.2 convert_multiply_fusion.4
  (140 shorter events, 22.0 us)
Async XLA Ops:
  35.0 8.3 %copy-start.34 = (bf16[2,64]{1,0:T(2,128)(2,1)S(1)}, bf16[2,64]{1,0:T(2,128)(2,1)}, u32[]{:S(2)}) copy-start(bf16[2,64]{1,0:T(2,128)(2,1)} %param.18) | copy-start | bytes 772
  35.0 12.6 %copy-start.25 = (s32[512]{0:T(512)S(1)}, s32[512]{0:T(512)}, u32[]{:S(2)}) copy-start(s32[512]{0:T(512)} %param.13) | copy-start | bytes 6148
  35.0 15.1 %copy-start.21 = (bf16[2,256,32]{1,2,0:T(8,128)(2,1)S(1)}, bf16[2,256,32]{1,2,0:T(8,128)(2,1)}, u32[]{:S(2)}) copy-start(bf16[2,256,32]{1,2,0:T(8,128)(2,1)} %param.15) | copy-start | bytes 98308
  35.0 20.3 %copy-start.26 = (s32[512,4]{0,1:T(4,128)S(1)}, s32[512,4]{0,1:T(4,128)}, u32[]{:S(2)}) copy-start(s32[512,4]{0,1:T(4,128)} %param.14) | copy-start | bytes 24580
  35.0 20.4 %copy-start.24 = (bf16[2,16,128]{2,1,0:T(8,128)(2,1)S(1)}, bf16[2,16,128]{2,1,0:T(8,128)(2,1)}, u32[]{:S(2)}) copy-start(bf16[2,16,128]{2,1,0:T(8,128)(2,1)} %param.16) | copy-start | bytes 24580
  35.0 30.5 %all-to-all-start = ((bf16[128,32,128]{2,1,0:T(8,128)(2,1)}), bf16[128,32,128]{2,1,0:T(8,128)(2,1)S(1)}, u32[]{:S(2)}, u32[]{:S(2)}) async-start(bf16[128,32,128]{2,1,0:T(8,128)(2,1)} %bitcast.1), calls=%async_computation | async-start | bytes 2097152 | tf_op jit(solution)/shard_map/all_to_all | solution.py:86
  42.5 29.2 %all-gather.3.cloned.1.call-start = ((), (), s32[]{:S(2)}) async-start(), calls=%async_computation.6 | async-start | bytes 1572864 | tf_op jit(solution)/shard_map/all_gather | solution.py:95
  43.3 153.7 %reduce-scatter.13.cloned.1.call-start = ((), (), s32[]{:S(2)}) async-start(), calls=%async_computation.10 | async-start | bytes 49152
  54.7 29.3 %copy-start.10 = (bf16[2,512,32]{1,2,0:T(8,128)(2,1)}, bf16[2,512,32]{1,2,0:T(8,128)(2,1)S(1)}, u32[]{:S(2)}) copy-start(bf16[2,512,32]{1,2,0:T(8,128)(2,1)S(1)} %all_gather.12) | copy-start | bytes 196612
  54.7 7.9 %copy-start.22 = (s32[1024]{0:T(1024)}, s32[1024]{0:T(1024)S(1)}, u32[]{:S(2)}) copy-start(s32[1024]{0:T(1024)S(1)} %pad_clamp_fusion.1) | copy-start | bytes 12292
  55.3 16.4 %copy-start.32 = (pred[512]{0:T(512)(128)(4,1)}, pred[512]{0:T(512)(128)(4,1)S(1)}, u32[]{:S(2)}) copy-start(pred[512]{0:T(512)(128)(4,1)S(1)} %compare_and_fusion.1) | copy-start | bytes 1540
  55.4 7.3 %copy-start.29 = (pred[512]{0:T(512)(128)(4,1)}, pred[512]{0:T(512)(128)(4,1)S(1)}, u32[]{:S(2)}) copy-start(pred[512]{0:T(512)(128)(4,1)S(1)} %compare_and_fusion) | copy-start | bytes 1540
  61.4 25.7 %copy-start.5 = (f32[512,4,32]{0,2,1:T(8,128)}, f32[512,4,32]{0,2,1:T(8,128)S(1)}, u32[]{:S(2)}) copy-start(f32[512,4,32]{0,2,1:T(8,128)S(1)} %broadcast_in_dim.27) | copy-start | bytes 786436
  69.4 2.4 %copy-start.19 = (bf16[8,128,32]{1,2,0:T(8,128)(2,1)}, bf16[8,128,32]{1,2,0:T(8,128)(2,1)S(1)}, u32[]{:S(2)}) copy-start(bf16[8,128,32]{1,2,0:T(8,128)(2,1)S(1)} %convolution_convert_fusion.7) | copy-start | bytes 196612
  69.9 1.8 copy-start.7
  75.4 11.0 %copy-start.12 = (f32[8,512]{1,0:T(8,128)}, f32[8,512]{1,0:T(8,128)S(1)}, u32[]{:S(2)}) copy-start(f32[8,512]{1,0:T(8,128)S(1)} %add_rsqrt_fusion.1) | copy-start | bytes 49156
  86.4 1.6 copy-start.4
  90.4 2.7 %copy-start.6 = (f32[512,4,32]{0,2,1:T(8,128)S(1)}, f32[512,4,32]{0,2,1:T(8,128)}, u32[]{:S(2)}) copy-start(f32[512,4,32]{0,2,1:T(8,128)} %copy-done.5) | copy-start | bytes 786436
  173.0 4.3 %copy-start.11 = (bf16[2,512,32]{1,2,0:T(8,128)(2,1)S(1)}, bf16[2,512,32]{1,2,0:T(8,128)(2,1)}, u32[]{:S(2)}) copy-start(bf16[2,512,32]{1,2,0:T(8,128)(2,1)} %copy-done.10) | copy-start | bytes 196612
  174.4 5.5 %copy-start.13 = (f32[8,512]{1,0:T(8,128)S(1)}, f32[8,512]{1,0:T(8,128)}, u32[]{:S(2)}) copy-start(f32[8,512]{1,0:T(8,128)} %copy-done.12) | copy-start | bytes 49156
  174.4 5.5 %copy-start.15 = (f32[8,512]{1,0:T(8,128)S(1)}, f32[8,512]{1,0:T(8,128)}, u32[]{:S(2)}) copy-start(f32[8,512]{1,0:T(8,128)} %copy-done.14) | copy-start | bytes 49156
  174.4 5.5 %copy-start.17 = (f32[8,512]{1,0:T(8,128)S(1)}, f32[8,512]{1,0:T(8,128)}, u32[]{:S(2)}) copy-start(f32[8,512]{1,0:T(8,128)} %copy-done.16) | copy-start | bytes 49156
  174.4 5.5 %copy-start.28 = (f32[128]{0:T(128)S(1)}, f32[128]{0:T(128)}, u32[]{:S(2)}) copy-start(f32[128]{0:T(128)} %get-tuple-element.44) | copy-start | bytes 1540
  174.4 23.9 %reduce-scatter.9.cloned.1.call-start = ((), (), s32[]{:S(2)}) async-start(), calls=%async_computation.8 | async-start | bytes 24576 | tf_op jit(solution)/shard_map/reduce_scatter | solution.py:130
  177.2 28.5 %reduce-scatter.7.cloned.1.call-start = ((), (), s32[]{:S(2)}) async-start(), calls=%async_computation.7 | async-start | bytes 98304 | tf_op jit(solution)/shard_map/reduce_scatter | solution.py:130
  179.9 49.0 %reduce-scatter.11.cloned.1.call-start = ((), (), s32[]{:S(2)}) async-start(), calls=%async_computation.9 | async-start | bytes 1572864 | tf_op jit(solution)/shard_map/reduce_scatter | solution.py:130
  184.8 1.7 copy-start.23
  186.5 1.9 copy-start.2
  186.5 1.9 copy-start.30
  188.4 7.2 %copy-start.18 = (s32[1,1,4608]{2,1,0:T(1,128)S(1)}, s32[1,1,4608]{2,1,0:T(1,128)}, u32[]{:S(2)}) copy-start(s32[1,1,4608]{2,1,0:T(1,128)} %param.12) | copy-start | bytes 55300
  188.4 7.2 %copy-start.1 = (bf16[8,512,128]{1,2,0:T(8,128)(2,1)S(1)}, bf16[8,512,128]{1,2,0:T(8,128)(2,1)}, u32[]{:S(2)}) copy-start(bf16[8,512,128]{1,2,0:T(8,128)(2,1)} %get-tuple-element.42) | copy-start | bytes 3145732
  191.9 26.6 %all-to-all-start.1 = ((bf16[8,512,128]{2,0,1:T(8,128)(2,1)}), bf16[8,512,128]{2,0,1:T(8,128)(2,1)S(1)}, u32[]{:S(2)}, u32[]{:S(2)}) async-start(bf16[8,512,128]{2,0,1:T(8,128)(2,1)} %multiply_convert_fusion), calls=%async_computation.1 | async-start | bytes 2097152 | tf_op jit(solution)/shard_map/all_to_all | solution.py:125
  (10 other events, 9.6 us)
Sparse Core Ops, SparseCore 0:
  44.9 22.8 all-gather.2
  174.5 7.1 reduce-scatter.12
  183.9 9.7 reduce-scatter.8
  195.7 9.8 reduce-scatter.6
  207.7 20.3 reduce-scatter.10
where the time goes:
time: 240 us; the launch traced here: 238 us
  blocking collectives  91.4 us (38%)
  other arithmetic  45.5 us (19%)
  local copies, waits for them, and re-layouts  29.1 us (12%)
  matrix products  25.4 us (11%)
  waiting for transfers between devices  20.2 us (8%)
  between operations  14.5 us (6%)
  starting transfers between devices  11.4 us (5%)
    psum x1, blocking collectives, per_device(): summed = lax.psum(partial_grads, 'mp')  78.1 us
    scatter-add x1, other arithmetic, per_device(): jax.ops.segment_sum(table_rows[0, 0].astype(jnp.float32), own_ids, num_se...  26 us
    dot_general x24, matrix products, product(): return jnp.einsum(form, left, right, preferred_element_type=jnp.float32)  25.4 us
    all_to_all x1, waiting for transfers between devices, per_device(): lax.all_to_all(slot_grads, 'mp', split_axis=1, concat_axis=0, tiled=True)  11.4 us
    gather x1, local copies, waits for them, and re-layouts, per_device(): row_grads = owner_grads.reshape(BAGS, E)[own_ids].reshape(1, 1, -1, E)  10.2 us
    unnamed x75, local copies, waits for them, and re-layouts  8.12 us
    all_to_all x1, starting transfers between devices, per_device(): lax.all_to_all(pooled, 'mp', split_axis=0, concat_axis=1, tiled=True)  7.5 us
    reduce_scatter x3, waiting for transfers between devices, per_device(): lax.psum_scatter(for_sending(summed), 'dp', scatter_dimension=1, tiled=True)  6.03 us
  transfers between devices with their start and end apart: 7, of which 3 were waited for; matrix products, arithmetic and copies ran while one was open for 19% of the time, Pallas kernels for 0%

commit v1 on v0

v1 whole, which is shorter than its diff:
```python
import functools

import jax
import jax.numpy as jnp
from jax import lax
from jax.experimental import pallas as pl
from jax.experimental.pallas import tpu as pltpu
from jax.sharding import PartitionSpec as P

F = 512
E = 128
K = 32
LAYERS = 2
SAMP_DEV = 8
PAIR = 2
PW = PAIR * E
EPS = 1e-05
VMEM_LIMIT = 56 * 1024 * 1024
PIECE = 144
BF = jnp.bfloat16
F32 = jnp.float32


def params():
    return pltpu.CompilerParams(vmem_limit_bytes=VMEM_LIMIT)


def dot(left, right):
    return jnp.dot(left, right, preferred_element_type=F32)


def dot_nt(left, right):
    return lax.dot_general(left, right, (((1,), (1,)), ((), ())), preferred_element_type=F32)


def dot_tn(left, right):
    return lax.dot_general(left, right, (((0,), (0,)), ((), ())), preferred_element_type=F32)


def pool_kernel(ids_ref, rows_ref, out_ref, *, block):
    bags, rows = out_ref.shape[0], rows_ref.shape[0]
    for low in range(0, bags, block):
        high = min(low + block + rows - bags, rows)
        bag = lax.broadcasted_iota(jnp.int32, (block, high - low), 0) + low
        hot = jnp.where(ids_ref[:, low:high] == bag, 1.0, 0.0).astype(BF)
        out_ref[low : low + block, :] = dot(hot, rows_ref[low:high, :]).astype(BF)


def pool(ids, rows, bags):
    return pl.pallas_call(
        functools.partial(pool_kernel, block=256),
        out_shape=jax.ShapeDtypeStruct((bags, E), BF),
        compiler_params=params(),
        name="pool",
    )(ids, rows)


def expand_kernel(ids_ref, bags_ref, out_ref, table, *, block):
    rows, bags = out_ref.shape[0], bags_ref.shape[0]
    table[...] = jnp.zeros_like(table)
    for part in range(rows // 128):
        table[part : part + 1, :] = ids_ref[:, part * 128 : (part + 1) * 128]
    columns = table[...].T
    for low in range(0, rows, block):
        first = max(low - (rows - bags), 0)
        last = min(low + block, bags)
        own = jnp.concatenate(
            [columns[:, part : part + 1] for part in range(low // 128, (low + block) // 128)], axis=0
        )
        bag = lax.broadcasted_iota(jnp.int32, (block, last - first), 1) + first
        hot = jnp.where(own == bag, 1.0, 0.0).astype(BF)
        out_ref[low : low + block, :] = dot(hot, bags_ref[first:last, :]).astype(BF)


def expand(ids, owner, rows):
    return pl.pallas_call(
        functools.partial(expand_kernel, block=256),
        out_shape=jax.ShapeDtypeStruct((rows, E), BF),
        scratch_shapes=[pltpu.VMEM((128, 128), jnp.int32)],
        compiler_params=params(),
        name="expand",
    )(ids, owner)


def prepare_kernel(
    slot_ref, expo_ref, project_ref, output_ref, mix_ref, left_ref, back_ref, diag_ref, scale_ref, perm_ref, unperm_ref
):
    for layer in range(LAYERS):
        left_ref[layer, :F, :] = mix_ref[layer]
        left_ref[layer, F:, :] = project_ref[layer].T
        back_ref[layer] = mix_ref[layer].T
        row = output_ref[layer]
        none = jnp.zeros_like(row)
        diag_ref[layer] = jnp.concatenate(
            [jnp.concatenate([row, none], axis=1), jnp.concatenate([none, row], axis=1)], axis=0
        )
    expo = expo_ref[...]
    small = jnp.where(
        expo == 0, 0.25, jnp.where(expo == 1, 0.5, jnp.where(expo == 2, 1.0, 2.0))
    ).astype(BF)
    blocks = expo.shape[1]
    spread = jnp.where(
        lax.broadcasted_iota(jnp.int32, (blocks, E), 1) // (E // blocks)
        == lax.broadcasted_iota(jnp.int32, (blocks, E), 0),
        1.0,
        0.0,
    ).astype(BF)
    scale_ref[...] = dot(small, spread)
    hot = jnp.where(slot_ref[...] == lax.broadcasted_iota(jnp.int32, (F, F), 0), 1.0, 0.0)
    perm_ref[...] = hot.astype(BF)
    unperm_ref[...] = hot.T.astype(BF)


def prepare(slot_feature, block_exponent, project, output, mix):
    return pl.pallas_call(
        prepare_kernel,
        out_shape=(
            jax.ShapeDtypeStruct((LAYERS, F + K, F), BF),
            jax.ShapeDtypeStruct((LAYERS, F, F), BF),
            jax.ShapeDtypeStruct((LAYERS, PAIR * K, PW), BF),
            jax.ShapeDtypeStruct((F, E), F32),
            jax.ShapeDtypeStruct((F, F), BF),
            jax.ShapeDtypeStruct((F, F), BF),
        ),
        compiler_params=params(),
        name="prepare",
    )(slot_feature.reshape(1, F), block_exponent, project, output, mix)


def unslot(block, f_dev):
    if f_dev % 16:
        block = block.astype(F32)
    parts = [block[:, t * f_dev : (t + 1) * f_dev, :].reshape(F, E) for t in range(PAIR)]
    return jnp.concatenate(parts, axis=1).astype(BF)


def layers_kernel(
    pos_ref,
    recv_ref,
    cot_ref,
    left_ref,
    back_ref,
    diag_ref,
    project_ref,
    gain_ref,
    scale_ref,
    perm_ref,
    unperm_ref,
    *refs,
    f_dev,
    packed,
):
    feats_ref, slots_ref = refs[:2]
    grad_refs = refs[2:4] if packed else refs[2:6]
    xs, ts, normed_s, inv_s, grad_s, next_s, wacc, gacc, dm, pj, ex = refs[-11:]
    step = pl.program_id(0)
    columns = pl.ds(pl.multiple_of(step * PW, PW), PW)
    scale = scale_ref[...]
    chunk = 128

    @pl.when(step == 0)
    def _():
        wacc[...] = jnp.zeros_like(wacc)
        gacc[...] = jnp.zeros_like(gacc)

    x = dot(perm_ref[...], unslot(recv_ref[...], f_dev))
    x = (x * jnp.concatenate([scale] * PAIR, axis=1)).astype(BF)
    same = (
        lax.broadcasted_iota(jnp.int32, (PAIR * K, PW), 0) // K
        == lax.broadcasted_iota(jnp.int32, (PAIR * K, PW), 1) // E
    )
    saved = []
    for layer in range(LAYERS):
        xs[layer, :, columns] = x
        mixed = dot(left_ref[layer], x)
        projected = jnp.concatenate([mixed[F:]] * PAIR, axis=0)
        projected = jnp.where(same, projected, 0.0).astype(BF)
        paired = dot_nt(x, projected).astype(BF)
        low = dot(paired, diag_ref[layer])
        gain = gain_ref[layer : layer + 1, :].astype(F32)
        saved.append((x, projected, paired))
        for t in range(PAIR):
            lanes = slice(t * E, (t + 1) * E)
            for r in range(0, F, chunk):
                rows = slice(r, r + chunk)
                total = x[rows, lanes].astype(F32) + mixed[rows, lanes] + low[rows, lanes]
                centred = total - jnp.sum(total, axis=-1, keepdims=True) * (1.0 / E)
                variance = jnp.sum(centred * centred, axis=-1, keepdims=True) * (1.0 / E)
                inverse = lax.rsqrt(variance + EPS)
                normed = centred * inverse
                normed_s[layer, rows, lanes] = normed
                inv_s[layer, rows, lanes] = jnp.broadcast_to(inverse, (chunk, E))
                out = (normed * gain).astype(BF)
                next_s[rows, lanes] = out
                if layer == LAYERS - 1:
                    feats_ref[t, rows, :] = out
        x = next_s[...]

    for layer in reversed(range(LAYERS)):
        x, projected, paired = saved[layer]
        gain = gain_ref[layer : layer + 1, :].astype(F32)
        dgain = jnp.zeros((8, E), F32)
        for t in range(PAIR):
            lanes = slice(t * E, (t + 1) * E)
            for r in range(0, F, chunk):
                rows = slice(r, r + chunk)
                if layer == LAYERS - 1:
                    upper = cot_ref[t, rows, :].astype(F32)
                else:
                    upper = next_s[rows, lanes].astype(F32)
                normed = normed_s[layer, rows, lanes]
                dgain = dgain + jnp.sum((upper * normed).reshape(chunk // 8, 8, E), axis=0)
                scaled = upper * gain
                first = jnp.sum(scaled, axis=-1, keepdims=True) * (1.0 / E)
                second = jnp.sum(scaled * normed, axis=-1, keepdims=True) * (1.0 / E)
                total = inv_s[layer, rows, lanes] * (scaled - first - normed * second)
                grad_s[rows, lanes] = total
                next_s[rows, lanes] = total.astype(BF)
        gacc[layer] += dgain
        total_low = next_s[...]
        ts[layer, :F, columns] = total_low
        grad_paired = dot_nt(total_low, diag_ref[layer]).astype(BF)
        wide = dot_tn(grad_paired, x)
        grad_projected = jnp.concatenate(
            [wide[t * K : (t + 1) * K, t * E : (t + 1) * E] for t in range(PAIR)], axis=1
        ).astype(BF)
        ts[layer, F:, columns] = grad_projected
        wide = dot_tn(paired, total_low)
        for t in range(PAIR):
            wacc[layer] += wide[t * K : (t + 1) * K, t * E : (t + 1) * E]
        upstream = dot(back_ref[layer], total_low) + dot(
            jnp.concatenate([grad_paired, project_ref[layer]], axis=1),
            jnp.concatenate([projected, grad_projected], axis=0),
        )
        for t in range(PAIR):
            lanes = slice(t * E, (t + 1) * E)
            for r in range(0, F, chunk):
                rows = slice(r, r + chunk)
                out = (grad_s[rows, lanes] + upstream[rows, lanes]).astype(BF)
                if layer == 0:
                    out = (out.astype(F32) * scale[rows]).astype(BF)
                next_s[rows, lanes] = out

    slots = dot(unperm_ref[...], next_s[...])
    if f_dev % 16 == 0:
        slots = slots.astype(BF)
    for t in range(PAIR):
        slots_ref[:, t * f_dev : (t + 1) * f_dev, :] = (
            slots[:, t * E : (t + 1) * E].reshape(F // f_dev, f_dev, E).astype(BF)
        )

    @pl.when(step == pl.num_programs(0) - 1)
    def _():
        for layer in range(LAYERS):
            dm[layer] = dot_nt(ts[layer], xs[layer])
        gains = [jnp.sum(gacc[layer], axis=0, keepdims=True) for layer in range(LAYERS)]
        if not packed:
            mix_ref, project_t_ref, output_ref, gain_out_ref = grad_refs
            mix_ref[...] = dm[:, :F, :]
            project_t_ref[...] = dm[:, F:, :]
            output_ref[...] = wacc[...]
            gain_out_ref[...] = jnp.concatenate(gains, axis=0)
            return
        half = F // 2
        for d in range(2):
            gain_row = jnp.concatenate([g[:, d * 64 : (d + 1) * 64] for g in gains], axis=1)
            for m in range(16):
                l, h, kb = m // 8, (m // 4) % 2, m % 4
                low = d * half + h * E
                pj[d, m] = dm[l, F + 8 * kb : F + 8 * kb + 8, low : low + E]
                if m < 4:
                    low = d * (K // 2) + 8 * (m % 2)
                    ex[d, m] = wacc[m // 2, low : low + 8, :]
                else:
                    ex[d, m] = jnp.broadcast_to(gain_row, (8, E))
        my_d, my_m = pos_ref[0], pos_ref[1]
        for core in range(2):
            for rx in range(2):
                for ry in range(2):
                    for rz in range(4):
                        m = my_m ^ (rz * 4 + rx * 2 + core)
                        d = my_d ^ ry
                        start = pl.multiple_of(d * half + (m % 8) * 32, 32)
                        block = dm[m // 8, pl.ds(start, 32), :]
                        pieces = [block[:, c * E : (c + 1) * E] for c in range(4)]
                        pieces += [pj[d, m], ex[d, m]]
                        grad_refs[core][(rx * 2 + ry) * 4 + rz] = jnp.concatenate(
                            pieces, axis=0
                        ).astype(BF)


def run_layers(pos, recv, cotangent, operands, project, gain, f_dev, packed):
    left, back, diag, scale, perm, unperm = operands
    tables = F // f_dev

    def whole(x):
        return pl.BlockSpec(x.shape, lambda i, pos: (0,) * x.ndim)

    def shape(dims, dtype=F32):
        return jax.ShapeDtypeStruct(dims, dtype)

    if packed:
        grads = [shape((16, PIECE, E), BF)] * 2
    else:
        grads = [
            shape((LAYERS, F, F)),
            shape((LAYERS, K, F)),
            shape((LAYERS, K, E)),
            shape((LAYERS, E)),
        ]
    cot_spec = pl.BlockSpec((PAIR, F, E), lambda i, pos: (i, 0, 0))
    slot_spec = pl.BlockSpec((tables, PAIR * f_dev, E), lambda i, pos: (0, i, 0))
    constants = [left, back, diag, project, gain, scale, perm, unperm]
    width = SAMP_DEV * E
    return pl.pallas_call(
        functools.partial(layers_kernel, f_dev=f_dev, packed=packed),
        out_shape=[
            shape((SAMP_DEV, F, E), BF),
            shape((tables, SAMP_DEV * f_dev, E), BF),
        ]
        + grads,
        grid_spec=pltpu.PrefetchScalarGridSpec(
            num_scalar_prefetch=1,
            grid=(SAMP_DEV // PAIR,),
            in_specs=[slot_spec, cot_spec] + [whole(x) for x in constants],
            out_specs=[cot_spec, slot_spec] + [whole(x) for x in grads],
            scratch_shapes=[
                pltpu.VMEM((LAYERS, F, width), BF),
                pltpu.VMEM((LAYERS, F + K, width), BF),
                pltpu.VMEM((LAYERS, F, PW), F32),
                pltpu.VMEM((LAYERS, F, PW), F32),
                pltpu.VMEM((F, PW), F32),
                pltpu.VMEM((F, PW), BF),
                pltpu.VMEM((LAYERS, K, E), F32),
                pltpu.VMEM((LAYERS, 8, E), F32),
                pltpu.VMEM((LAYERS, F + K, F), F32),
                pltpu.VMEM((2, 16, 8, E), F32),
                pltpu.VMEM((2, 16, 8, E), F32),
            ],
        ),
        compiler_params=params(),
        name="layers",
    )(pos, recv, cotangent, *constants)


def gather_dp(part, axis):
    if lax.axis_size("dp") != 2:
        return lax.all_gather(part, "dp", axis=axis, tiled=True)
    other = lax.ppermute(part, "dp", [(0, 1), (1, 0)])
    return jnp.where(
        lax.axis_index("dp") == 0,
        jnp.concatenate([part, other], axis=axis),
        jnp.concatenate([other, part], axis=axis),
    )


def across(x, d, m):
    pairs = [(i, i ^ (d * 16 + m)) for i in range(32)]
    return lax.ppermute(x, ("dp", "mp"), pairs)


def sum_kernel(*refs, parts):
    total = sum(ref[...].astype(F32) for ref in refs[:parts]).astype(BF)
    outs = refs[parts:]
    size = total.shape[0] // len(outs)
    for i, out in enumerate(outs):
        out[...] = total[i * size : (i + 1) * size]


def sum_parts(parts, outs):
    size = parts[0].shape[0] // outs
    return pl.pallas_call(
        functools.partial(sum_kernel, parts=len(parts)),
        out_shape=[jax.ShapeDtypeStruct((size,) + parts[0].shape[1:], BF)] * outs,
        compiler_params=params(),
        name="sum_parts",
    )(*parts)


def finish_kernel(pos_ref, *refs, factor):
    parts = refs[:4]
    mix_ref, project_ref, output_ref, gain_ref, pj, ex = refs[4:]
    my_m = pos_ref[1]
    for c in range(2):
        for rx in range(2):
            for rz in range(4):
                m = my_m ^ (rz * 4 + rx * 2 + c)
                piece = parts[c * 2 + rx][rz].astype(F32) * factor
                start = pl.multiple_of((m % 8) * 32, 32)
                for n in range(4):
                    mix_ref[m // 8, pl.ds(start, 32), n * E : (n + 1) * E] = piece[
                        n * 32 : (n + 1) * 32
                    ]
                pj[m] = piece[128:136]
                ex[m] = piece[136:144]
    for l in range(LAYERS):
        rows = [
            jnp.concatenate([pj[l * 8 + h * 4 + kb] for kb in range(4)], axis=0) for h in range(2)
        ]
        project_ref[l] = jnp.concatenate(rows, axis=1).T
        for b in range(2):
            output_ref[l, b * 8 : (b + 1) * 8, :] = ex[l * 2 + b]
        gain_ref[l : l + 1, :] = ex[4][0:1, l * 64 : (l + 1) * 64]


def finish(pos, parts, factor):
    vmem = pl.BlockSpec(memory_space=pltpu.VMEM)
    return pl.pallas_call(
        functools.partial(finish_kernel, factor=factor),
        out_shape=[
            jax.ShapeDtypeStruct((LAYERS, F // 2, F), F32),
            jax.ShapeDtypeStruct((LAYERS, F // 2, K), F32),
            jax.ShapeDtypeStruct((LAYERS, K // 2, E), F32),
            jax.ShapeDtypeStruct((LAYERS, E // 2), F32),
        ],
        in_specs=[pl.BlockSpec(memory_space=pltpu.SMEM)] + [vmem] * 4,
        out_specs=[vmem] * 4,
        scratch_shapes=[pltpu.VMEM((16, 8, E), F32)] * 2,
        compiler_params=params(),
        name="finish",
    )(pos, *parts)


def reduce_packed(pos, keep, send, factor):
    other = across(send, 0, 1)
    own, to_y, to_x, to_xy = sum_parts([keep, other], 4)
    parts = [own, across(to_y, 1, 0), across(to_x, 0, 2), across(to_xy, 1, 2)]
    quarters = sum_parts(parts, 4)
    parts = [quarters[0]] + [across(quarters[r], 0, 4 * r) for r in range(1, 4)]
    (piece,) = sum_parts(parts, 1)
    column = jnp.concatenate([piece] + [across(piece, 0, 4 * r) for r in range(1, 4)], axis=0)
    beside = across(column, 0, 2)
    return finish(pos, [column, beside, across(column, 0, 1), across(beside, 0, 1)], factor)


def per_device(
    table_rows,
    bag_ids,
    slot_feature,
    block_exponent,
    fm_project,
    fm_output,
    mix_weight,
    norm_gain,
    out_cotangent,
):
    tables, groups = lax.axis_size("mp"), lax.axis_size("dp")
    f_dev = F // tables
    bags = SAMP_DEV * tables * f_dev
    rows = table_rows.shape[2]
    ids = bag_ids.reshape(1, rows)
    factor = 1.0 / float(SAMP_DEV * tables * groups) ** 0.5
    pos = jnp.stack([lax.axis_index("dp"), lax.axis_index("mp")]).astype(jnp.int32)

    pooled = pool(ids, table_rows.reshape(rows, E), bags).reshape(tables, SAMP_DEV * f_dev, E)
    recv = lax.all_to_all(pooled, "mp", split_axis=0, concat_axis=0, tiled=True)
    project, output, mix, gain = (
        gather_dp(part, 1) for part in (fm_project, fm_output, mix_weight, norm_gain)
    )
    operands = prepare(slot_feature, block_exponent, project, output, mix)
    packed = (groups, tables) == (2, 16)
    feats, slots, *grads = run_layers(
        pos, recv, out_cotangent, operands, project, gain, f_dev, packed
    )
    owner = lax.all_to_all(slots, "mp", split_axis=0, concat_axis=0, tiled=True)
    row_grads = expand(ids, owner.reshape(bags, E), rows).reshape(1, 1, rows, E)
    if packed:
        mix_g, project_g, output_g, gain_g = reduce_packed(pos, grads[0], grads[1], factor)
        return feats, row_grads, project_g, output_g, mix_g, gain_g
    summed = lax.psum(tuple(grads), "mp")
    mix_g, project_t, output_g, gain_g = summed
    parts = (project_t.transpose(0, 2, 1), output_g, mix_g, gain_g)
    shares = [
        lax.psum_scatter(part.astype(BF), "dp", scatter_dimension=1, tiled=True).astype(F32)
        * factor
        for part in parts
    ]
    return feats, row_grads, *shares


def solution(mesh):
    placed = (
        P("dp", "mp", None, None),
        P("dp", "mp", None),
        P(),
        P(),
        P(None, "dp", None),
        P(None, "dp", None),
        P(None, "dp", None),
        P(None, "dp"),
        P(("dp", "mp"), None, None),
    )
    return jax.shard_map(
        per_device,
        mesh=mesh,
        in_specs=placed,
        out_specs=(
            P(("dp", "mp"), None, None),
            P("dp", "mp", None, None),
            P(None, "dp", None),
            P(None, "dp", None),
            P(None, "dp", None),
            P(None, "dp"),
        ),
        check_vma=False,
    )
```

time: 240 us -> 128 us (0.53)
  blocking collectives: 91.4 us -> 0 us
  Pallas kernels: 0 us -> 45.1 us
  other arithmetic: 45.5 us -> 4.79 us
  matrix products: 25.4 us -> 0 us
  starting transfers between devices: 11.4 us -> 33.9 us
  local copies, waits for them, and re-layouts: 29.1 us -> 7.65 us
  waiting for transfers between devices: 20.2 us -> 35.3 us
  between operations: 14.5 us -> 0.78 us
    psum x1 -> x0, blocking collectives: 78.1 us -> none  [per_device(): summed = lax.psum(partial_grads, 'mp')]
    pallas_call x0 -> x8, Pallas kernels: none -> 45.1 us  [the longest x1 25.4 us: run_layers(): pl.pallas_call(functools.partial(layers_kernel, f_dev=f_dev, packed=packe...]
    ppermute x0 -> x17, waiting for transfers between devices: none -> 34.6 us  [the longest x13 25.3 us: across(): return lax.ppermute(x, ('dp', 'mp'), pairs)]
    scatter-add x1 -> x0, other arithmetic: 26 us -> none  [per_device(): jax.ops.segment_sum(table_rows[0, 0].astype(jnp.float32), own_ids, num_se...]
    dot_general x24 -> x0, matrix products: 25.4 us -> none  [product(): return jnp.einsum(form, left, right, preferred_element_type=jnp.float32)]
    ppermute x0 -> x17, starting transfers between devices: none -> 19.4 us  [the longest x13 15.3 us: across(): return lax.ppermute(x, ('dp', 'mp'), pairs)]
    gather x5 -> x0, local copies, waits for them, and re-layouts: 15.7 us -> none  [the longest x1 10.2 us: per_device(): row_grads = owner_grads.reshape(BAGS, E)[own_ids].reshape(1, 1, -1, E)]
    all_gather x3 -> x0, blocking collectives: 13.3 us -> none  [the longest x1 4.59 us: per_device(): lax.all_gather(fm_project, 'dp', axis=1, tiled=True)]
  transfers between devices with their start and end apart: 7 -> 19, of which waited for: 3 -> 13; matrix products, arithmetic and copies ran while one was open for 19% -> 6% of each run, Pallas kernels for 0% -> 9%
where the time goes in v1:
time: 128 us
  Pallas kernels  45.1 us (35%)
  waiting for transfers between devices  35.3 us (28%)
  starting transfers between devices  33.9 us (26%)
  local copies, waits for them, and re-layouts  7.65 us (6%)
  other arithmetic  4.79 us (4%)
    pallas_call x1, Pallas kernels, run_layers(): pl.pallas_call(functools.partial(layers_kernel, f_dev=f_dev, packed=packe...  25.4 us
    ppermute x13, waiting for transfers between devices, across(): return lax.ppermute(x, ('dp', 'mp'), pairs)  25.3 us
    ppermute x13, starting transfers between devices, across(): return lax.ppermute(x, ('dp', 'mp'), pairs)  15.3 us
    ppermute x4, waiting for transfers between devices, gather_dp(): other = lax.ppermute(part, 'dp', [(0, 1), (1, 0)])  9.3 us
    all_to_all x1, starting transfers between devices, per_device(): recv = lax.all_to_all(pooled, 'mp', split_axis=0, concat_axis=0, tiled=True)  7.5 us
    unnamed x40, local copies, waits for them, and re-layouts  7.31 us
    all_to_all x1, starting transfers between devices, per_device(): owner = lax.all_to_all(slots, 'mp', split_axis=0, concat_axis=0, tiled=True)  7.01 us
    pallas_call x3, Pallas kernels, sum_parts(): pl.pallas_call(functools.partial(sum_kernel, parts=len(parts)), out_shape...  5.36 us
  transfers between devices with their start and end apart: 19, of which 13 were waited for; matrix products, arithmetic and copies ran while one was open for 6% of the time, Pallas kernels for 9%

profile of v1, /device:TPU:0, one launch (start us, length us, event | category | flops | bytes accessed | tf_op | source)
XLA Modules:
  0.0 127.5 jit_solution(15604076994339215836)
XLA Ops:
  0.6 4.0 %pool.1 = bf16[4096,128]{1,0:T(8,128)(2,1)} custom-call(s32[1,4608]{1,0:T(1,128)} %bitcast.12, bf16[4608,128]{1,0:T(8,128)(2,1)} %bitcast.10), custom_call_target="tpu_custom_call" | custom-call | tf_op jit(solution)/shard_map/pool/pallas_call | solution.py:50
  4.7 7.5 %all-to-all-start = ((bf16[16,256,128]{2,1,0:T(8,128)(2,1)}), bf16[16,256,128]{2,1,0:T(8,128)(2,1)S(1)}, u32[]{:S(2)}, u32[]{:S(2)}) async-start(bf16[16,256,128]{2,1,0:T(8,128)(2,1)} %bitcast.9), calls=%async_computation | async-start | bytes 2097152 | tf_op jit(solution)/shard_map/all_to_all | solution.py:456
  12.2 1.6 %collective-permute-start.3 = (bf16[2,64]{1,0:T(2,128)(2,1)S(1)}, bf16[2,64]{1,0:T(2,128)(2,1)S(1)}, u32[]{:S(2)}, u32[]{:S(2)}) collective-permute-start(bf16[2,64]{1,0:T(2,128)(2,1)S(1)} %copy-done.17), channel_id=1, source_target_pairs={{0,16},{16,0},{1,17},{17,1},{2,18},{18,2},{3,19},{19,3},{4,20},{20... | collective-permute-start | bytes 776 | tf_op jit(solution)/shard_map/ppermute | solution.py:349
  14.3 1.5 %collective-permute-start = (bf16[2,256,32]{1,2,0:T(8,128)(2,1)S(1)}, bf16[2,256,32]{1,2,0:T(8,128)(2,1)S(1)}, u32[]{:S(2)}, u32[]{:S(2)}) collective-permute-start(bf16[2,256,32]{1,2,0:T(8,128)(2,1)S(1)} %copy-done.14), channel_id=1, source_target_pairs={{0,16},{16,0},{1,17},{17,1},{2,18},{18,2},{3,19},{19,3},{4,20},{20... | collective-permute-start | bytes 98312 | tf_op jit(solution)/shard_map/ppermute | solution.py:349
  20.2 9.3 %collective-permute-done.2 = bf16[2,256,512]{2,1,0:T(8,128)(2,1)S(1)} collective-permute-done((bf16[2,256,512]{2,1,0:T(8,128)(2,1)S(1)}, bf16[2,256,512]{2,1,0:T(8,128)(2,1)S(1)}, u32[]{:S(2)}, u32[]{:S(2)}) %collective-permute-start.2) | collective-permute-done | bytes 524320 | tf_op jit(solution)/shard_map/ppermute | solution.py:349
  29.5 1.4 %maximum_select_fusion.mix_ref = bf16[2,512,512]{2,1,0:T(8,128)(2,1)} fusion(bf16[2,256,512]{2,1,0:T(8,128)(2,1)S(1)} %collective-permute-done.2, bf16[2,256,512]{2,1,0:T(8,128)(2,1)S(1)} %copy-done.4, pred[]{:T(512)S(6)} %eq.2), kind=kLoop, calls=%fused_computation | loop fusion | flops 4718592 | bytes 2097153 | tf_op jit(solution)/shard_map/jit(_where)/select_n | solution.py:350
  30.9 3.6 %prepare.1 = (bf16[2,544,512]{2,1,0:T(8,128)(2,1)}, bf16[2,512,512]{2,1,0:T(8,128)(2,1)}, bf16[2,64,256]{2,1,0:T(8,128)(2,1)}, f32[512,128]{1,0:T(8,128)}, bf16[...) custom-call(s32[1,512]{1,0:T(1,128)} %bitcast.14, s32[512,4]{1,0:T(8,128)} %copy.22.expo_ref, ...), custom_call_target="tpu_custom_call" | custom-call | tf_op jit(solution)/shard_map/prepare/pallas_call | solution.py:115
  36.1 25.4 %layers.1 = (bf16[8,512,128]{2,1,0:T(8,128)(2,1)}, bf16[16,256,128]{2,1,0:T(8,128)(2,1)}, bf16[16,144,128]{2,1,0:T(8,128)(2,1)}, bf16[16,144,128]{2,1,0:T(8,128)(2,1)}) custom-call(s32[2]{0:T(128)} %pad_add_fusion.pos_ref, bf16[16,256,128]{2,1,0:T(8,128)(2,1)} %copy-done, bf16[8,512,128]{2,1,0:T(8,128)(2,1)} %cot_ref.1, ...), custom_call_target="tpu_custom_call" | custom-call | tf_op jit(solution)/shard_map/layers/pallas_call | solution.py:315
  61.6 7.0 %all-to-all-start.1 = ((bf16[16,256,128]{2,1,0:T(8,128)(2,1)}), bf16[16,256,128]{2,1,0:T(8,128)(2,1)S(1)}, u32[]{:S(2)}, u32[]{:S(2)}) async-start(bf16[16,256,128]{2,1,0:T(8,128)(2,1)} %get-tuple-element.35), calls=%async_computation.1 | async-start | bytes 2097152 | tf_op jit(solution)/shard_map/all_to_all | solution.py:465
  69.1 1.6 %collective-permute-done.4.refs_1_ = bf16[16,144,128]{2,1,0:T(8,128)(2,1)S(1)} collective-permute-done((bf16[16,144,128]{2,1,0:T(8,128)(2,1)S(1)}, bf16[16,144,128]{2,1,0:T(8,128)(2,1)S(1)}, u32[]{:S(2)}, u32[]{:S(2)}) %collective-permute-start.4) | collective-permute-done | bytes 589856 | tf_op jit(solution)/shard_map/ppermute | solution.py:359
  71.5 2.1 %sum_parts.3 = (bf16[4,144,128]{2,1,0:T(8,128)(2,1)}, bf16[4,144,128]{2,1,0:T(8,128)(2,1)}, bf16[4,144,128]{2,1,0:T(8,128)(2,1)}, bf16[4,144,128]{2,1,0:T(8,128)(2,1)}) custom-call(bf16[16,144,128]{2,1,0:T(8,128)(2,1)} %get-tuple-element.36.refs_0_, bf16[16,144,128]{2,1,0:T(8,128)(2,1)} %copy-done.2), custom_call_target="tpu_custom_call" | custom-call | tf_op jit(solution)/shard_map/sum_parts/pallas_call | solution.py:372
  73.6 1.5 %collective-permute-start.5 = (bf16[4,144,128]{2,1,0:T(8,128)(2,1)}, bf16[4,144,128]{2,1,0:T(8,128)(2,1)S(1)}, u32[]{:S(2)}, u32[]{:S(2)}) collective-permute-start(bf16[4,144,128]{2,1,0:T(8,128)(2,1)} %get-tuple-element.39), channel_id=1, source_target_pairs={{0,16},{1,17},{2,18},{3,19},{4,20},{5,21},{6,22},{7,23},{8,24},{9,... | collective-permute-start | bytes 442376 | tf_op jit(solution)/shard_map/ppermute | solution.py:359
  75.1 1.9 %collective-permute-start.6 = (bf16[4,144,128]{2,1,0:T(8,128)(2,1)}, bf16[4,144,128]{2,1,0:T(8,128)(2,1)S(1)}, u32[]{:S(2)}, u32[]{:S(2)}) collective-permute-start(bf16[4,144,128]{2,1,0:T(8,128)(2,1)} %get-tuple-element.40), channel_id=1, source_target_pairs={{0,2},{1,3},{2,0},{3,1},{4,6},{5,7},{6,4},{7,5},{8,10},{9,11},{10,... | collective-permute-start | bytes 442376 | tf_op jit(solution)/shard_map/ppermute | solution.py:359
  77.1 2.8 %collective-permute-done.5.refs_1_ = bf16[4,144,128]{2,1,0:T(8,128)(2,1)S(1)} collective-permute-done((bf16[4,144,128]{2,1,0:T(8,128)(2,1)}, bf16[4,144,128]{2,1,0:T(8,128)(2,1)S(1)}, u32[]{:S(2)}, u32[]{:S(2)}) %collective-permute-start.5) | collective-permute-done | bytes 147488 | tf_op jit(solution)/shard_map/ppermute | solution.py:359
  79.9 5.6 %collective-permute-done.6.refs_2_ = bf16[4,144,128]{2,1,0:T(8,128)(2,1)S(1)} collective-permute-done((bf16[4,144,128]{2,1,0:T(8,128)(2,1)}, bf16[4,144,128]{2,1,0:T(8,128)(2,1)S(1)}, u32[]{:S(2)}, u32[]{:S(2)}) %collective-permute-start.6) | collective-permute-done | bytes 147488 | tf_op jit(solution)/shard_map/ppermute | solution.py:359
  85.5 2.6 %collective-permute-done.7.refs_3_ = bf16[4,144,128]{2,1,0:T(8,128)(2,1)S(1)} collective-permute-done((bf16[4,144,128]{2,1,0:T(8,128)(2,1)}, bf16[4,144,128]{2,1,0:T(8,128)(2,1)S(1)}, u32[]{:S(2)}, u32[]{:S(2)}) %collective-permute-start.7) | collective-permute-done | bytes 147488 | tf_op jit(solution)/shard_map/ppermute | solution.py:359
  88.8 1.8 %sum_parts.4 = (bf16[1,144,128]{2,1,0:T(8,128)(2,1)}, bf16[1,144,128]{2,1,0:T(8,128)(2,1)}, bf16[1,144,128]{2,1,0:T(8,128)(2,1)}, bf16[1,144,128]{2,1,0:T(8,128)(2,1)}) custom-call(bf16[4,144,128]{2,1,0:T(8,128)(2,1)} %get-tuple-element.38.refs_0_, bf16[4,144,128]{2,1,0:T(8,128)(2,1)} %copy-done.5, bf16[4,144,128]{2,1,0:T(8,128)(2,1)} %copy-done.6, ...), custom_call_target="tpu_custom_call" | custom-call | tf_op jit(solution)/shard_map/sum_parts/pallas_call | solution.py:372
  90.6 3.5 %collective-permute-start.8 = (bf16[1,144,128]{2,1,0:T(8,128)(2,1)}, bf16[1,144,128]{2,1,0:T(8,128)(2,1)S(1)}, u32[]{:S(2)}, u32[]{:S(2)}) collective-permute-start(bf16[1,144,128]{2,1,0:T(8,128)(2,1)} %get-tuple-element.43), channel_id=1, source_target_pairs={{0,4},{1,5},{2,6},{3,7},{4,0},{5,1},{6,2},{7,3},{8,12},{9,13},{10,... | collective-permute-start | bytes 110600 | tf_op jit(solution)/shard_map/ppermute | solution.py:359
  94.1 1.1 collective-permute-start.9
  95.1 1.3 %collective-permute-start.10 = (bf16[1,144,128]{2,1,0:T(8,128)(2,1)}, bf16[1,144,128]{2,1,0:T(8,128)(2,1)S(1)}, u32[]{:S(2)}, u32[]{:S(2)}) collective-permute-start(bf16[1,144,128]{2,1,0:T(8,128)(2,1)} %get-tuple-element.45), channel_id=1, source_target_pairs={{0,12},{1,13},{2,14},{3,15},{4,8},{5,9},{6,10},{7,11},{8,4},{9,5},... | collective-permute-start | bytes 110600 | tf_op jit(solution)/shard_map/ppermute | solution.py:359
  96.5 3.1 %collective-permute-done.9.refs_2_ = bf16[1,144,128]{2,1,0:T(8,128)(2,1)S(1)} collective-permute-done((bf16[1,144,128]{2,1,0:T(8,128)(2,1)}, bf16[1,144,128]{2,1,0:T(8,128)(2,1)S(1)}, u32[]{:S(2)}, u32[]{:S(2)}) %collective-permute-start.9) | collective-permute-done | bytes 36896 | tf_op jit(solution)/shard_map/ppermute | solution.py:359
  99.5 1.6 %collective-permute-done.10.refs_3_ = bf16[1,144,128]{2,1,0:T(8,128)(2,1)S(1)} collective-permute-done((bf16[1,144,128]{2,1,0:T(8,128)(2,1)}, bf16[1,144,128]{2,1,0:T(8,128)(2,1)S(1)}, u32[]{:S(2)}, u32[]{:S(2)}) %collective-permute-start.10) | collective-permute-done | bytes 36896 | tf_op jit(solution)/shard_map/ppermute | solution.py:359
  101.7 1.5 %sum_parts.5 = bf16[1,144,128]{2,1,0:T(8,128)(2,1)} custom-call(bf16[1,144,128]{2,1,0:T(8,128)(2,1)} %get-tuple-element.42.refs_0_, bf16[1,144,128]{2,1,0:T(8,128)(2,1)} %copy-done.11, bf16[1,144,128]{2,1,0:T(8,128)(2,1)} %copy-done.12, bf16[1,144,128]{2,1,0:T(8,128)(2,1)} %copy-done.13), custom_call_target="tpu_custom_call" | custom-call | tf_op jit(solution)/shard_map/sum_parts/pallas_call | solution.py:372
  103.2 1.3 %collective-permute-start.13 = (bf16[1,144,128]{2,1,0:T(8,128)(2,1)}, bf16[1,144,128]{2,1,0:T(8,128)(2,1)S(1)}, u32[]{:S(2)}, u32[]{:S(2)}) collective-permute-start(bf16[1,144,128]{2,1,0:T(8,128)(2,1)} %sum_parts.5), channel_id=1, source_target_pairs={{0,12},{1,13},{2,14},{3,15},{4,8},{5,9},{6,10},{7,11},{8,4},{9,5},... | collective-permute-start | bytes 110600 | tf_op jit(solution)/shard_map/ppermute | solution.py:359
  104.5 3.0 %collective-permute-start.11 = (bf16[1,144,128]{2,1,0:T(8,128)(2,1)}, bf16[1,144,128]{2,1,0:T(8,128)(2,1)S(1)}, u32[]{:S(2)}, u32[]{:S(2)}) collective-permute-start(bf16[1,144,128]{2,1,0:T(8,128)(2,1)} %sum_parts.5), channel_id=1, source_target_pairs={{0,4},{1,5},{2,6},{3,7},{4,0},{5,1},{6,2},{7,3},{8,12},{9,13},{10,... | collective-permute-start | bytes 110600 | tf_op jit(solution)/shard_map/ppermute | solution.py:359
  107.6 1.6 %collective-permute-done.13 = bf16[1,144,128]{2,1,0:T(8,128)(2,1)S(1)} collective-permute-done((bf16[1,144,128]{2,1,0:T(8,128)(2,1)}, bf16[1,144,128]{2,1,0:T(8,128)(2,1)S(1)}, u32[]{:S(2)}, u32[]{:S(2)}) %collective-permute-start.13) | collective-permute-done | bytes 36896 | tf_op jit(solution)/shard_map/ppermute | solution.py:359
  110.9 1.1 collective-permute-start.14
  112.0 4.1 %collective-permute-done.14.refs_1_ = bf16[4,144,128]{2,1,0:T(8,128)(2,1)S(1)} collective-permute-done((bf16[4,144,128]{2,1,0:T(8,128)(2,1)S(1)}, bf16[4,144,128]{2,1,0:T(8,128)(2,1)S(1)}, u32[]{:S(2)}, u32[]{:S(2)}) %collective-permute-start.14) | collective-permute-done | bytes 147488 | tf_op jit(solution)/shard_map/ppermute | solution.py:359
  116.2 1.4 %collective-permute-done.16.refs_3_ = bf16[4,144,128]{2,1,0:T(8,128)(2,1)S(1)} collective-permute-done((bf16[4,144,128]{2,1,0:T(8,128)(2,1)S(1)}, bf16[4,144,128]{2,1,0:T(8,128)(2,1)S(1)}, u32[]{:S(2)}, u32[]{:S(2)}) %collective-permute-start.16) | collective-permute-done | bytes 147488 | tf_op jit(solution)/shard_map/ppermute | solution.py:359
  118.2 2.4 %finish.1 = (f32[2,256,512]{2,1,0:T(8,128)}, f32[2,256,32]{2,1,0:T(8,128)}, f32[2,16,128]{2,1,0:T(8,128)}, f32[2,64]{1,0:T(2,128)}) custom-call(s32[2]{0:T(128)} %pad_add_fusion.pos_ref, bf16[4,144,128]{2,1,0:T(8,128)(2,1)} %copy-done.3, bf16[4,144,128]{2,1,0:T(8,128)(2,1)} %copy-done.7, bf16[4,144,128]{2,1,0:T(8,128)(2,1)} %copy-done.9, ...), custom_call_target="tpu_custom_call" | custom-call | tf_op jit(solution)/shard_map/finish/pallas_call | solution.py:408
  120.6 1.7 %copy.23 = f32[2,256,32]{1,2,0:T(8,128)} copy(f32[2,256,32]{2,1,0:T(8,128)} %get-tuple-element.58) | data formatting | bytes 131072
  123.3 4.3 %expand.1 = bf16[4608,128]{1,0:T(8,128)(2,1)} custom-call(s32[1,4608]{1,0:T(1,128)} %bitcast.13, bf16[4096,128]{1,0:T(8,128)(2,1)} %bitcast.8), custom_call_target="tpu_custom_call" | custom-call | tf_op jit(solution)/shard_map/expand/pallas_call | solution.py:76
  (63 shorter events, 12.6 us)
Async XLA Ops:
  4.7 7.5 %copy-start.17 = (bf16[2,64]{1,0:T(2,128)(2,1)S(1)}, bf16[2,64]{1,0:T(2,128)(2,1)}, u32[]{:S(2)}) copy-start(bf16[2,64]{1,0:T(2,128)(2,1)} %param.16) | copy-start | bytes 772
  4.7 9.1 %copy-start.16 = (bf16[2,16,128]{2,1,0:T(8,128)(2,1)S(1)}, bf16[2,16,128]{2,1,0:T(8,128)(2,1)}, u32[]{:S(2)}) copy-start(bf16[2,16,128]{2,1,0:T(8,128)(2,1)} %param.14) | copy-start | bytes 24580
  4.7 9.6 %copy-start.14 = (bf16[2,256,32]{1,2,0:T(8,128)(2,1)S(1)}, bf16[2,256,32]{1,2,0:T(8,128)(2,1)}, u32[]{:S(2)}) copy-start(bf16[2,256,32]{1,2,0:T(8,128)(2,1)} %param.13) | copy-start | bytes 98308
  4.7 11.2 %copy-start.4 = (bf16[2,256,512]{2,1,0:T(8,128)(2,1)S(1)}, bf16[2,256,512]{2,1,0:T(8,128)(2,1)}, u32[]{:S(2)}) copy-start(bf16[2,256,512]{2,1,0:T(8,128)(2,1)} %param.15) | copy-start | bytes 1572868
  4.7 12.3 %copy-start.15 = (s32[512,4]{0,1:T(4,128)S(1)}, s32[512,4]{0,1:T(4,128)}, u32[]{:S(2)}) copy-start(s32[512,4]{0,1:T(4,128)} %param.12) | copy-start | bytes 24580
  4.7 30.5 %all-to-all-start = ((bf16[16,256,128]{2,1,0:T(8,128)(2,1)}), bf16[16,256,128]{2,1,0:T(8,128)(2,1)S(1)}, u32[]{:S(2)}, u32[]{:S(2)}) async-start(bf16[16,256,128]{2,1,0:T(8,128)(2,1)} %bitcast.9), calls=%async_computation | async-start | bytes 2097152 | tf_op jit(solution)/shard_map/all_to_all | solution.py:456
  12.2 5.6 %collective-permute-start.3 = (bf16[2,64]{1,0:T(2,128)(2,1)S(1)}, bf16[2,64]{1,0:T(2,128)(2,1)S(1)}, u32[]{:S(2)}, u32[]{:S(2)}) collective-permute-start(bf16[2,64]{1,0:T(2,128)(2,1)S(1)} %copy-done.17), channel_id=1, source_target_pairs={{0,16},{16,0},{1,17},{17,1},{2,18},{18,2},{3,19},{19,3},{4,20},{20... | collective-permute-start | bytes 776 | tf_op jit(solution)/shard_map/ppermute | solution.py:349
  13.8 4.6 %collective-permute-start.1 = (bf16[2,16,128]{2,1,0:T(8,128)(2,1)S(1)}, bf16[2,16,128]{2,1,0:T(8,128)(2,1)S(1)}, u32[]{:S(2)}, u32[]{:S(2)}) collective-permute-start(bf16[2,16,128]{2,1,0:T(8,128)(2,1)S(1)} %copy-done.16), channel_id=1, source_target_pairs={{0,16},{16,0},{1,17},{17,1},{2,18},{18,2},{3,19},{19,3},{4,20},{20... | collective-permute-start | bytes 24584 | tf_op jit(solution)/shard_map/ppermute | solution.py:349
  14.3 4.7 %collective-permute-start = (bf16[2,256,32]{1,2,0:T(8,128)(2,1)S(1)}, bf16[2,256,32]{1,2,0:T(8,128)(2,1)S(1)}, u32[]{:S(2)}, u32[]{:S(2)}) collective-permute-start(bf16[2,256,32]{1,2,0:T(8,128)(2,1)S(1)} %copy-done.14), channel_id=1, source_target_pairs={{0,16},{16,0},{1,17},{17,1},{2,18},{18,2},{3,19},{19,3},{4,20},{20... | collective-permute-start | bytes 98312 | tf_op jit(solution)/shard_map/ppermute | solution.py:349
  15.9 13.6 %collective-permute-start.2 = (bf16[2,256,512]{2,1,0:T(8,128)(2,1)S(1)}, bf16[2,256,512]{2,1,0:T(8,128)(2,1)S(1)}, u32[]{:S(2)}, u32[]{:S(2)}) collective-permute-start(bf16[2,256,512]{2,1,0:T(8,128)(2,1)S(1)} %copy-done.4), channel_id=1, source_target_pairs={{0,16},{16,0},{1,17},{17,1},{2,18},{18,2},{3,19},{19,3},{4,20},{20... | collective-permute-start | bytes 1572872 | tf_op jit(solution)/shard_map/ppermute | solution.py:349
  61.6 7.0 %copy-start.18 = (bf16[16,144,128]{2,1,0:T(8,128)(2,1)S(1)}, bf16[16,144,128]{2,1,0:T(8,128)(2,1)}, u32[]{:S(2)}) copy-start(bf16[16,144,128]{2,1,0:T(8,128)(2,1)} %get-tuple-element.37) | copy-start | bytes 1769476
  61.6 60.7 %all-to-all-start.1 = ((bf16[16,256,128]{2,1,0:T(8,128)(2,1)}), bf16[16,256,128]{2,1,0:T(8,128)(2,1)S(1)}, u32[]{:S(2)}, u32[]{:S(2)}) async-start(bf16[16,256,128]{2,1,0:T(8,128)(2,1)} %get-tuple-element.35), calls=%async_computation.1 | async-start | bytes 2097152 | tf_op jit(solution)/shard_map/all_to_all | solution.py:465
  68.6 2.1 %collective-permute-start.4 = (bf16[16,144,128]{2,1,0:T(8,128)(2,1)S(1)}, bf16[16,144,128]{2,1,0:T(8,128)(2,1)S(1)}, u32[]{:S(2)}, u32[]{:S(2)}) collective-permute-start(bf16[16,144,128]{2,1,0:T(8,128)(2,1)S(1)} %copy-done.18), channel_id=1, source_target_pairs={{0,1},{1,0},{2,3},{3,2},{4,5},{5,4},{6,7},{7,6},{8,9},{9,8},{10,11... | collective-permute-start | bytes 1769480 | tf_op jit(solution)/shard_map/ppermute | solution.py:359
  73.6 6.3 %collective-permute-start.5 = (bf16[4,144,128]{2,1,0:T(8,128)(2,1)}, bf16[4,144,128]{2,1,0:T(8,128)(2,1)S(1)}, u32[]{:S(2)}, u32[]{:S(2)}) collective-permute-start(bf16[4,144,128]{2,1,0:T(8,128)(2,1)} %get-tuple-element.39), channel_id=1, source_target_pairs={{0,16},{1,17},{2,18},{3,19},{4,20},{5,21},{6,22},{7,23},{8,24},{9,... | collective-permute-start | bytes 442376 | tf_op jit(solution)/shard_map/ppermute | solution.py:359
  75.1 10.4 %collective-permute-start.6 = (bf16[4,144,128]{2,1,0:T(8,128)(2,1)}, bf16[4,144,128]{2,1,0:T(8,128)(2,1)S(1)}, u32[]{:S(2)}, u32[]{:S(2)}) collective-permute-start(bf16[4,144,128]{2,1,0:T(8,128)(2,1)} %get-tuple-element.40), channel_id=1, source_target_pairs={{0,2},{1,3},{2,0},{3,1},{4,6},{5,7},{6,4},{7,5},{8,10},{9,11},{10,... | collective-permute-start | bytes 442376 | tf_op jit(solution)/shard_map/ppermute | solution.py:359
  77.0 11.1 %collective-permute-start.7 = (bf16[4,144,128]{2,1,0:T(8,128)(2,1)}, bf16[4,144,128]{2,1,0:T(8,128)(2,1)S(1)}, u32[]{:S(2)}, u32[]{:S(2)}) collective-permute-start(bf16[4,144,128]{2,1,0:T(8,128)(2,1)} %get-tuple-element.41), channel_id=1, source_target_pairs={{0,18},{1,19},{2,16},{3,17},{4,22},{5,23},{6,20},{7,21},{8,26},{9,... | collective-permute-start | bytes 442376 | tf_op jit(solution)/shard_map/ppermute | solution.py:359
  79.9 8.2 %copy-start.5 = (bf16[4,144,128]{2,1,0:T(8,128)(2,1)}, bf16[4,144,128]{2,1,0:T(8,128)(2,1)S(1)}, u32[]{:S(2)}) copy-start(bf16[4,144,128]{2,1,0:T(8,128)(2,1)S(1)} %collective-permute-done.5.refs_1_) | copy-start | bytes 442372
  85.5 2.6 %copy-start.6 = (bf16[4,144,128]{2,1,0:T(8,128)(2,1)}, bf16[4,144,128]{2,1,0:T(8,128)(2,1)S(1)}, u32[]{:S(2)}) copy-start(bf16[4,144,128]{2,1,0:T(8,128)(2,1)S(1)} %collective-permute-done.6.refs_2_) | copy-start | bytes 442372
  90.6 5.9 %collective-permute-start.8 = (bf16[1,144,128]{2,1,0:T(8,128)(2,1)}, bf16[1,144,128]{2,1,0:T(8,128)(2,1)S(1)}, u32[]{:S(2)}, u32[]{:S(2)}) collective-permute-start(bf16[1,144,128]{2,1,0:T(8,128)(2,1)} %get-tuple-element.43), channel_id=1, source_target_pairs={{0,4},{1,5},{2,6},{3,7},{4,0},{5,1},{6,2},{7,3},{8,12},{9,13},{10,... | collective-permute-start | bytes 110600 | tf_op jit(solution)/shard_map/ppermute | solution.py:359
  94.1 5.5 %collective-permute-start.9 = (bf16[1,144,128]{2,1,0:T(8,128)(2,1)}, bf16[1,144,128]{2,1,0:T(8,128)(2,1)S(1)}, u32[]{:S(2)}, u32[]{:S(2)}) collective-permute-start(bf16[1,144,128]{2,1,0:T(8,128)(2,1)} %get-tuple-element.44), channel_id=1, source_target_pairs={{0,8},{1,9},{2,10},{3,11},{4,12},{5,13},{6,14},{7,15},{8,0},{9,1},... | collective-permute-start | bytes 110600 | tf_op jit(solution)/shard_map/ppermute | solution.py:359
  95.1 6.0 %collective-permute-start.10 = (bf16[1,144,128]{2,1,0:T(8,128)(2,1)}, bf16[1,144,128]{2,1,0:T(8,128)(2,1)S(1)}, u32[]{:S(2)}, u32[]{:S(2)}) collective-permute-start(bf16[1,144,128]{2,1,0:T(8,128)(2,1)} %get-tuple-element.45), channel_id=1, source_target_pairs={{0,12},{1,13},{2,14},{3,15},{4,8},{5,9},{6,10},{7,11},{8,4},{9,5},... | collective-permute-start | bytes 110600 | tf_op jit(solution)/shard_map/ppermute | solution.py:359
  96.5 4.6 %copy-start.11 = (bf16[1,144,128]{2,1,0:T(8,128)(2,1)}, bf16[1,144,128]{2,1,0:T(8,128)(2,1)S(1)}, u32[]{:S(2)}) copy-start(bf16[1,144,128]{2,1,0:T(8,128)(2,1)S(1)} %collective-permute-done.8.refs_1_) | copy-start | bytes 110596
  99.5 1.6 %copy-start.12 = (bf16[1,144,128]{2,1,0:T(8,128)(2,1)}, bf16[1,144,128]{2,1,0:T(8,128)(2,1)S(1)}, u32[]{:S(2)}) copy-start(bf16[1,144,128]{2,1,0:T(8,128)(2,1)S(1)} %collective-permute-done.9.refs_2_) | copy-start | bytes 110596
  103.2 6.0 %collective-permute-start.13 = (bf16[1,144,128]{2,1,0:T(8,128)(2,1)}, bf16[1,144,128]{2,1,0:T(8,128)(2,1)S(1)}, u32[]{:S(2)}, u32[]{:S(2)}) collective-permute-start(bf16[1,144,128]{2,1,0:T(8,128)(2,1)} %sum_parts.5), channel_id=1, source_target_pairs={{0,12},{1,13},{2,14},{3,15},{4,8},{5,9},{6,10},{7,11},{8,4},{9,5},... | collective-permute-start | bytes 110600 | tf_op jit(solution)/shard_map/ppermute | solution.py:359
  104.5 5.5 %collective-permute-start.12 = (bf16[1,144,128]{2,1,0:T(8,128)(2,1)}, bf16[1,144,128]{2,1,0:T(8,128)(2,1)S(1)}, u32[]{:S(2)}, u32[]{:S(2)}) collective-permute-start(bf16[1,144,128]{2,1,0:T(8,128)(2,1)} %sum_parts.5), channel_id=1, source_target_pairs={{0,8},{1,9},{2,10},{3,11},{4,12},{5,13},{6,14},{7,15},{8,0},{9,1},... | collective-permute-start | bytes 110600 | tf_op jit(solution)/shard_map/ppermute | solution.py:359
  104.5 5.6 %collective-permute-start.11 = (bf16[1,144,128]{2,1,0:T(8,128)(2,1)}, bf16[1,144,128]{2,1,0:T(8,128)(2,1)S(1)}, u32[]{:S(2)}, u32[]{:S(2)}) collective-permute-start(bf16[1,144,128]{2,1,0:T(8,128)(2,1)} %sum_parts.5), channel_id=1, source_target_pairs={{0,4},{1,5},{2,6},{3,7},{4,0},{5,1},{6,2},{7,3},{8,12},{9,13},{10,... | collective-permute-start | bytes 110600 | tf_op jit(solution)/shard_map/ppermute | solution.py:359
  110.9 6.6 %copy-start.3 = (bf16[4,144,128]{2,1,0:T(8,128)(2,1)}, bf16[4,144,128]{2,1,0:T(8,128)(2,1)S(1)}, u32[]{:S(2)}) copy-start(bf16[4,144,128]{2,1,0:T(8,128)(2,1)S(1)} %pad_maximum_fusion.refs_0_) | copy-start | bytes 442372
  110.9 5.2 %collective-permute-start.14 = (bf16[4,144,128]{2,1,0:T(8,128)(2,1)S(1)}, bf16[4,144,128]{2,1,0:T(8,128)(2,1)S(1)}, u32[]{:S(2)}, u32[]{:S(2)}) collective-permute-start(bf16[4,144,128]{2,1,0:T(8,128)(2,1)S(1)} %pad_maximum_fusion.refs_0_), channel_id=1, source_target_pairs={{0,2},{1,3},{2,0},{3,1},{4,6},{5,7},{6,4},{7,5},{8,10},{9,11},{10,... | collective-permute-start | bytes 442376 | tf_op jit(solution)/shard_map/ppermute | solution.py:359
  112.0 4.1 %collective-permute-start.15 = (bf16[4,144,128]{2,1,0:T(8,128)(2,1)S(1)}, bf16[4,144,128]{2,1,0:T(8,128)(2,1)S(1)}, u32[]{:S(2)}, u32[]{:S(2)}) collective-permute-start(bf16[4,144,128]{2,1,0:T(8,128)(2,1)S(1)} %pad_maximum_fusion.refs_0_), channel_id=1, source_target_pairs={{0,1},{1,0},{2,3},{3,2},{4,5},{5,4},{6,7},{7,6},{8,9},{9,8},{10,11... | collective-permute-start | bytes 442376 | tf_op jit(solution)/shard_map/ppermute | solution.py:359
  116.1 1.4 %copy-start.7 = (bf16[4,144,128]{2,1,0:T(8,128)(2,1)}, bf16[4,144,128]{2,1,0:T(8,128)(2,1)S(1)}, u32[]{:S(2)}) copy-start(bf16[4,144,128]{2,1,0:T(8,128)(2,1)S(1)} %collective-permute-done.14.refs_1_) | copy-start | bytes 442372
  116.1 1.4 %collective-permute-start.16 = (bf16[4,144,128]{2,1,0:T(8,128)(2,1)S(1)}, bf16[4,144,128]{2,1,0:T(8,128)(2,1)S(1)}, u32[]{:S(2)}, u32[]{:S(2)}) collective-permute-start(bf16[4,144,128]{2,1,0:T(8,128)(2,1)S(1)} %collective-permute-done.14.refs_1_), channel_id=1, source_target_pairs={{0,1},{1,0},{2,3},{3,2},{4,5},{5,4},{6,7},{7,6},{8,9},{9,8},{10,11... | collective-permute-start | bytes 442376 | tf_op jit(solution)/shard_map/ppermute | solution.py:359
  116.1 1.4 %copy-start.9 = (bf16[4,144,128]{2,1,0:T(8,128)(2,1)}, bf16[4,144,128]{2,1,0:T(8,128)(2,1)S(1)}, u32[]{:S(2)}) copy-start(bf16[4,144,128]{2,1,0:T(8,128)(2,1)S(1)} %collective-permute-done.15.refs_2_) | copy-start | bytes 442372
  (6 other events, 4.7 us)

commit v2 on v0

v2 whole, which is shorter than its diff:
```python
import functools

import jax
import jax.numpy as jnp
from jax import lax
from jax.experimental import pallas as pl
from jax.experimental.pallas import tpu as pltpu
from jax.sharding import PartitionSpec as P

F = 512
E = 128
K = 32
LAYERS = 2
SAMP_DEV = 8
PAIR = 2
PW = PAIR * E
PAIRS = SAMP_DEV // PAIR
CHUNK = 128
EPS = 1e-05
VMEM_LIMIT = 62 * 1024 * 1024
PIECE = 144
BF = jnp.bfloat16
F32 = jnp.float32


def params():
    return pltpu.CompilerParams(vmem_limit_bytes=VMEM_LIMIT)


def dot(left, right):
    return jnp.dot(left, right, preferred_element_type=F32)


def dot_nt(left, right):
    return lax.dot_general(left, right, (((1,), (1,)), ((), ())), preferred_element_type=F32)


def dot_tn(left, right):
    return lax.dot_general(left, right, (((0,), (0,)), ((), ())), preferred_element_type=F32)


class Copies:
    def __init__(self, sems):
        self.sems, self.used, self.open = sems, 0, {}

    def start(self, key, source, target):
        copy = pltpu.make_async_copy(source, target, self.sems.at[self.used])
        self.used += 1
        copy.start()
        self.open[key] = copy

    def wait(self, *keys):
        for key in keys:
            if key in self.open:
                self.open.pop(key).wait()

    def drain(self):
        self.wait(*list(self.open))


BLOCK = 128
ANY = pl.BlockSpec(memory_space=pltpu.HBM)
VMEM = pl.BlockSpec(memory_space=pltpu.VMEM)


def pool_kernel(ids_ref, rows_ref, out_ref):
    bags, rows = out_ref.shape[0], rows_ref.shape[0]
    for low in range(0, bags, BLOCK):
        high = min(low + BLOCK + rows - bags, rows)
        bag = lax.broadcasted_iota(jnp.int32, (BLOCK, high - low), 0) + low
        hot = jnp.where(ids_ref[:, low:high] == bag, 1.0, 0.0).astype(BF)
        out_ref[low : low + BLOCK, :] = dot(hot, rows_ref[low:high, :]).astype(BF)


def pool(ids, rows, bags):
    return pl.pallas_call(
        pool_kernel,
        out_shape=jax.ShapeDtypeStruct((bags, E), BF),
        compiler_params=params(),
        name="pool",
    )(ids, rows)


def expand_kernel(ids_ref, bags_ref, out_ref, table):
    rows, bags = out_ref.shape[0], bags_ref.shape[0]
    table[...] = jnp.zeros_like(table)
    for part in range(rows // BLOCK):
        table[part : part + 1, :] = ids_ref[:, part * BLOCK : (part + 1) * BLOCK]
    columns = table[...].T
    for part in range(rows // BLOCK):
        low = part * BLOCK
        first = max(low - (rows - bags), 0)
        last = min(low + BLOCK, bags)
        bag = lax.broadcasted_iota(jnp.int32, (BLOCK, last - first), 1) + first
        hot = jnp.where(columns[:, part : part + 1] == bag, 1.0, 0.0).astype(BF)
        out_ref[low : low + BLOCK, :] = dot(hot, bags_ref[first:last, :]).astype(BF)


def expand(ids, owner, rows):
    return pl.pallas_call(
        expand_kernel,
        out_shape=jax.ShapeDtypeStruct((rows, E), BF),
        scratch_shapes=[pltpu.VMEM((BLOCK, BLOCK), jnp.int32)],
        compiler_params=params(),
        name="expand",
    )(ids, owner)


def prepare_kernel(pos_ref, slot_ref, expo_ref, *refs, halves):
    weights, outs = refs[: 4 * halves], refs[4 * halves :]
    projects, outputs, mixes, gains = (weights[n * halves : (n + 1) * halves] for n in range(4))
    left_ref, back_ref, diag_ref, project_ref, gain_ref, scale_ref, perm_ref, unperm_ref = outs
    first = pos_ref[0] == 0

    def joined(parts, axis):
        if halves == 1:
            return parts[0]
        return jnp.where(
            first, jnp.concatenate(parts, axis=axis), jnp.concatenate(parts[::-1], axis=axis)
        )

    for layer in range(LAYERS):
        for half in range(halves):
            size = F // halves
            start = 0 if halves == 1 else pl.multiple_of((pos_ref[0] ^ half) * size, size)
            left_ref[layer, pl.ds(start, size), :] = mixes[half][layer]
        back_ref[layer] = left_ref[layer, :F, :].T
        project_t = joined([ref[layer] for ref in projects], 1)
        left_ref[layer, F:, :] = project_t
        none = jnp.zeros((PAIR * K, F), BF)
        project_ref[layer] = jnp.concatenate([none, project_t, none[:K]], axis=0).T
        row = joined([ref[layer].astype(F32) for ref in outputs], 0).astype(BF)
        none = jnp.zeros_like(row)
        diag_ref[layer] = jnp.concatenate(
            [
                jnp.concatenate([row, none], axis=1),
                jnp.concatenate([none, row], axis=1),
                jnp.zeros((E - PAIR * K, PW), BF),
            ],
            axis=0,
        )
    gain_ref[...] = joined([ref[...].astype(F32) for ref in gains], 1)
    expo = expo_ref[...]
    small = jnp.where(
        expo == 0, 0.25, jnp.where(expo == 1, 0.5, jnp.where(expo == 2, 1.0, 2.0))
    ).astype(BF)
    blocks = expo.shape[0]
    spread = jnp.where(
        lax.broadcasted_iota(jnp.int32, (blocks, E), 1) // (E // blocks)
        == lax.broadcasted_iota(jnp.int32, (blocks, E), 0),
        1.0,
        0.0,
    ).astype(BF)
    scale_ref[...] = dot_tn(small, spread)
    hot = jnp.where(slot_ref[...] == lax.broadcasted_iota(jnp.int32, (F, F), 0), 1.0, 0.0)
    perm_ref[...] = hot.astype(BF)
    unperm_ref[...] = hot.T.astype(BF)


def prepare(pos, slot_feature, block_exponent, weights):
    halves = len(weights[0])
    flat = [part for parts in weights for part in parts]
    return pl.pallas_call(
        functools.partial(prepare_kernel, halves=halves),
        out_shape=(
            jax.ShapeDtypeStruct((LAYERS, F + K, F), BF),
            jax.ShapeDtypeStruct((LAYERS, F, F), BF),
            jax.ShapeDtypeStruct((LAYERS, E, PW), BF),
            jax.ShapeDtypeStruct((LAYERS, F, E), BF),
            jax.ShapeDtypeStruct((LAYERS, E), F32),
            jax.ShapeDtypeStruct((F, E), F32),
            jax.ShapeDtypeStruct((F, F), BF),
            jax.ShapeDtypeStruct((F, F), BF),
        ),
        in_specs=[pl.BlockSpec(memory_space=pltpu.SMEM)] + [VMEM] * (2 + len(flat)),
        out_specs=(VMEM,) * 8,
        compiler_params=params(),
        name="prepare",
    )(pos, slot_feature.reshape(1, F), block_exponent.T, *flat)


def unslot(block, f_dev):
    if f_dev % 16:
        block = block.astype(F32)
    parts = [block[:, t * f_dev : (t + 1) * f_dev, :].reshape(F, E) for t in range(PAIR)]
    return jnp.concatenate(parts, axis=1).astype(BF)


CONSTANTS = ("perm", "scale", "left", "diag", "back", "project", "unperm")


def layers_kernel(pos_ref, gain_ref, recv_hbm, cot_hbm, *refs, f_dev, packed):
    sources, refs = dict(zip(CONSTANTS, refs)), refs[len(CONSTANTS) :]
    feats_hbm, slots_hbm = refs[:2]
    grads = 2 if packed else 4
    grad_outs, refs = refs[2 : 2 + grads], refs[2 + grads :]
    held, refs = dict(zip(CONSTANTS, refs)), refs[len(CONSTANTS) :]
    recv_ref, cot_ref, feats_ref, slots_ref = refs[:4]
    grad_refs, refs = refs[4 : 4 + grads], refs[4 + grads :]
    xs, ts, normed_s, inv_s, grad_s, next_s, wacc, gacc, dm, pj, ex, sems = refs
    left_ref, back_ref, diag_ref = held["left"], held["back"], held["diag"]
    project_ref, scale_ref = held["project"], held["scale"]
    copies = Copies(sems)

    def slot_rows(p):
        return slice(p * PAIR * f_dev, (p + 1) * PAIR * f_dev)

    def fetch(name):
        copies.start(name, sources[name], held[name])

    copies.start("recv", recv_hbm, recv_ref)
    for name in ("perm", "scale", "left", "diag"):
        fetch(name)
    copies.start("cot", cot_hbm, cot_ref)
    for name in ("back", "project", "unperm"):
        fetch(name)

    wacc[...] = jnp.zeros_like(wacc)
    gacc[...] = jnp.zeros_like(gacc)

    def pair_steps(p):
        columns = slice(p * PW, (p + 1) * PW)
        x = dot(held["perm"][...], unslot(recv_ref[:, slot_rows(p)], f_dev))
        scale = scale_ref[...]
        x = (x * jnp.concatenate([scale] * PAIR, axis=1)).astype(BF)
        same = (
            lax.broadcasted_iota(jnp.int32, (PAIR * K, PW), 0) // K
            == lax.broadcasted_iota(jnp.int32, (PAIR * K, PW), 1) // E
        )
        saved = []
        for layer in range(LAYERS):
            xs[layer, :, columns] = x
            mixed = dot(left_ref[layer], x)
            projected = jnp.concatenate([mixed[F:]] * PAIR, axis=0)
            projected = jnp.where(same, projected, 0.0).astype(BF)
            paired = dot_nt(x, projected).astype(BF)
            low = dot(paired, diag_ref[layer, : PAIR * K])
            gain = gain_ref[layer : layer + 1, :]
            saved.append((x, projected, paired))
            yield
            for t in range(PAIR):
                lanes = slice(t * E, (t + 1) * E)
                for r in range(0, F, CHUNK):
                    rows = slice(r, r + CHUNK)
                    total = x[rows, lanes].astype(F32) + mixed[rows, lanes] + low[rows, lanes]
                    centred = total - jnp.sum(total, axis=-1, keepdims=True) * (1.0 / E)
                    variance = jnp.sum(centred * centred, axis=-1, keepdims=True) * (1.0 / E)
                    inverse = lax.rsqrt(variance + EPS)
                    normed = centred * inverse
                    normed_s[p, layer, rows, lanes] = normed
                    inv_s[p, layer, rows, lanes] = jnp.broadcast_to(inverse, (CHUNK, E))
                    out = (normed * gain).astype(BF)
                    if layer == LAYERS - 1:
                        feats_ref[p * PAIR + t, rows, :] = out
                    else:
                        next_s[p, rows, lanes] = out
            yield
            x = next_s[p]

        for layer in reversed(range(LAYERS)):
            x, projected, paired = saved[layer]
            gain = gain_ref[layer : layer + 1, :]
            dgain = jnp.zeros((8, E), F32)
            for t in range(PAIR):
                lanes = slice(t * E, (t + 1) * E)
                for r in range(0, F, CHUNK):
                    rows = slice(r, r + CHUNK)
                    if layer == LAYERS - 1:
                        upper = cot_ref[p * PAIR + t, rows, :].astype(F32)
                    else:
                        upper = next_s[p, rows, lanes].astype(F32)
                    normed = normed_s[p, layer, rows, lanes]
                    dgain = dgain + jnp.sum((upper * normed).reshape(CHUNK // 8, 8, E), axis=0)
                    scaled = upper * gain
                    first = jnp.sum(scaled, axis=-1, keepdims=True) * (1.0 / E)
                    second = jnp.sum(scaled * normed, axis=-1, keepdims=True) * (1.0 / E)
                    total = inv_s[p, layer, rows, lanes] * (scaled - first - normed * second)
                    grad_s[p, rows, lanes] = total
                    next_s[p, rows, lanes] = total.astype(BF)
            gacc[layer] += dgain
            yield
            total_low = next_s[p]
            ts[layer, :F, columns] = total_low
            grad_paired = dot_nt(total_low, diag_ref[layer]).astype(BF)
            wide = dot_tn(grad_paired[:, : PAIR * K], x)
            grad_projected = jnp.concatenate(
                [wide[t * K : (t + 1) * K, t * E : (t + 1) * E] for t in range(PAIR)], axis=1
            ).astype(BF)
            ts[layer, F:, columns] = grad_projected
            wide = dot_tn(paired, total_low)
            for t in range(PAIR):
                wacc[layer] += wide[t * K : (t + 1) * K, t * E : (t + 1) * E]
            rest = jnp.zeros((E - (PAIR + 1) * K, PW), BF)
            upstream = dot(back_ref[layer], total_low) + dot(
                grad_paired + project_ref[layer],
                jnp.concatenate([projected, grad_projected, rest], axis=0),
            )
            yield
            for t in range(PAIR):
                lanes = slice(t * E, (t + 1) * E)
                for r in range(0, F, CHUNK):
                    rows = slice(r, r + CHUNK)
                    out = (grad_s[p, rows, lanes] + upstream[rows, lanes]).astype(BF)
                    if layer == 0:
                        out = (out.astype(F32) * scale_ref[rows]).astype(BF)
                    next_s[p, rows, lanes] = out

        slots = dot(held["unperm"][...], next_s[p])
        if f_dev % 16 == 0:
            slots = slots.astype(BF)
        for t in range(PAIR):
            low = (p * PAIR + t) * f_dev
            slots_ref[:, low : low + f_dev, :] = (
                slots[:, t * E : (t + 1) * E].reshape(F // f_dev, f_dev, E).astype(BF)
            )
        yield

    def weight_grads(layer):
        dm[layer] = dot_nt(ts[layer], xs[layer])
        gain_row = jnp.sum(gacc[layer], axis=0, keepdims=True)
        if not packed:
            mix_ref, project_t_ref, output_ref, gain_out_ref = grad_refs
            mix_ref[layer] = dm[layer, :F, :]
            project_t_ref[layer] = dm[layer, F:, :]
            output_ref[layer] = wacc[layer]
            gain_out_ref[layer : layer + 1, :] = gain_row
            return
        half = F // 2
        for d in range(2):
            for q in range(8):
                low = d * half + (q // 4) * E
                pj[d, layer * 8 + q] = dm[
                    layer, F + 8 * (q % 4) : F + 8 * (q % 4) + 8, low : low + E
                ]
                if q < 2:
                    low = d * (K // 2) + 8 * q
                    ex[d, layer * 8 + q] = wacc[layer, low : low + 8, :]
                else:
                    row = gain_row[:, d * 64 : (d + 1) * 64]
                    ex[d, layer * 8 + q] = jnp.broadcast_to(
                        jnp.concatenate([row, row], axis=1), (8, E)
                    )
        my_d, my_m = pos_ref[0], pos_ref[1]
        flip = (my_m >> 3) ^ layer
        for core in range(2):
            for rx in range(2):
                for ry in range(2):
                    for low_z in range(2):
                        q = (my_m & 7) ^ (low_z * 4 + rx * 2 + core)
                        d = my_d ^ ry
                        start = pl.multiple_of(d * half + q * 32, 32)
                        block = dm[layer, pl.ds(start, 32), :]
                        pieces = [block[:, c * E : (c + 1) * E] for c in range(4)]
                        pieces += [pj[d, layer * 8 + q], ex[d, layer * 8 + q]]
                        place = (rx * 2 + ry) * 4 + low_z + 2 * flip
                        grad_refs[core][place] = jnp.concatenate(pieces, axis=0).astype(BF)

    programs = [pair_steps(p) for p in range(PAIRS)]
    phases = 4 * LAYERS + 1
    for tick in range(phases + PAIRS - 1):
        if tick == 0:
            copies.wait("recv", "perm", "scale", "left", "diag")
        if tick == 2 * LAYERS:
            copies.wait("cot", "back", "project", "unperm")
        if tick == 2 * LAYERS + PAIRS - 1:
            copies.start("feats", feats_ref, feats_hbm)
        for p in range(PAIRS):
            if 0 <= tick - p < phases:
                next(programs[p])
        for layer in reversed(range(LAYERS)):
            if tick - (PAIRS - 1) == phases - 2 - 2 * layer:
                weight_grads(layer)
    copies.start("slots", slots_ref, slots_hbm)
    for n in range(grads):
        copies.start(("grad", n), grad_refs[n], grad_outs[n])
    copies.drain()


def run_layers(pos, recv, cotangent, operands, f_dev, packed):
    left, back, diag, project, gain, scale, perm, unperm = operands
    tables = F // f_dev

    def shape(dims, dtype=F32):
        return jax.ShapeDtypeStruct(dims, dtype)

    if packed:
        grads = [shape((16, PIECE, E), BF)] * 2
    else:
        grads = [
            shape((LAYERS, F, F)),
            shape((LAYERS, K, F)),
            shape((LAYERS, K, E)),
            shape((LAYERS, E)),
        ]
    given = dict(
        perm=perm, scale=scale, left=left, diag=diag, back=back, project=project, unperm=unperm
    )
    constants = [given[name] for name in CONSTANTS]
    width = SAMP_DEV * E
    big = [shape((SAMP_DEV, F, E), BF), shape((tables, SAMP_DEV * f_dev, E), BF)]
    outs = big + grads

    def scratch(x):
        return pltpu.VMEM(x.shape, x.dtype)

    copies = len(constants) + 4 + len(grads)
    return pl.pallas_call(
        functools.partial(layers_kernel, f_dev=f_dev, packed=packed),
        out_shape=outs,
        in_specs=[pl.BlockSpec(memory_space=pltpu.SMEM), VMEM] + [ANY] * (2 + len(constants)),
        out_specs=[ANY] * len(outs),
        scratch_shapes=[scratch(x) for x in constants]
        + [scratch(recv), scratch(cotangent)]
        + [scratch(x) for x in outs]
        + [
            pltpu.VMEM((LAYERS, F, width), BF),
            pltpu.VMEM((LAYERS, F + K, width), BF),
            pltpu.VMEM((PAIRS, LAYERS, F, PW), F32),
            pltpu.VMEM((PAIRS, LAYERS, F, PW), F32),
            pltpu.VMEM((PAIRS, F, PW), F32),
            pltpu.VMEM((PAIRS, F, PW), BF),
            pltpu.VMEM((LAYERS, K, E), F32),
            pltpu.VMEM((LAYERS, 8, E), F32),
            pltpu.VMEM((LAYERS, F + K, F), F32),
            pltpu.VMEM((2, 16, 8, E), F32),
            pltpu.VMEM((2, 16, 8, E), F32),
            pltpu.SemaphoreType.DMA((copies,)),
        ],
        compiler_params=params(),
        name="layers",
    )(pos, gain, recv, cotangent, *constants)


def across(x, d, m):
    pairs = [(i, i ^ (d * 16 + m)) for i in range(32)]
    return lax.ppermute(x, ("dp", "mp"), pairs)


def added(parts):
    return sum(part.astype(F32) for part in parts).astype(BF)


def finish_kernel(pos_ref, *refs, factor):
    parts = refs[:4]
    mix_ref, project_ref, output_ref, gain_ref, pj, ex = refs[4:]
    my_m = pos_ref[1]
    for c in range(2):
        for rx in range(2):
            for rz in range(4):
                m = my_m ^ (rz * 4 + rx * 2 + c)
                piece = parts[c * 2 + rx][rz].astype(F32) * factor
                start = pl.multiple_of((m & 7) * 32, 32)
                for n in range(4):
                    mix_ref[m >> 3, pl.ds(start, 32), n * E : (n + 1) * E] = piece[
                        n * 32 : (n + 1) * 32
                    ]
                pj[m] = piece[128:136]
                ex[m] = piece[136:144]
    for l in range(LAYERS):
        for h in range(2):
            for b in range(4):
                project_ref[l, b * 8 : (b + 1) * 8, h * E : (h + 1) * E] = pj[l * 8 + h * 4 + b]
        for b in range(2):
            output_ref[l, b * 8 : (b + 1) * 8, :] = ex[l * 8 + b]
        gain_ref[l : l + 1, :] = ex[l * 8 + 2][0:1, :64]


def finish(pos, parts, factor):
    return pl.pallas_call(
        functools.partial(finish_kernel, factor=factor),
        out_shape=[
            jax.ShapeDtypeStruct((LAYERS, F // 2, F), F32),
            jax.ShapeDtypeStruct((LAYERS, K, F // 2), F32),
            jax.ShapeDtypeStruct((LAYERS, K // 2, E), F32),
            jax.ShapeDtypeStruct((LAYERS, E // 2), F32),
        ],
        in_specs=[pl.BlockSpec(memory_space=pltpu.SMEM)] + [VMEM] * 4,
        out_specs=[VMEM] * 4,
        scratch_shapes=[pltpu.VMEM((16, 8, E), F32)] * 2,
        compiler_params=params(),
        name="finish",
    )(pos, *parts)


def exchange(x):
    return lax.all_to_all(x, "mp", split_axis=0, concat_axis=0, tiled=True)


def return_packed(pos, slots, keep, send, ids, factor):
    rows, bags = ids.shape[1], slots.shape[0] * slots.shape[1]
    other = across(send, 0, 1)
    own, to_y, to_x, to_xy = [
        added([part[4 * r : 4 * r + 4] for part in (keep, other)]) for r in range(4)
    ]
    parts = [own, across(to_y, 1, 0), across(to_x, 0, 2), across(to_xy, 1, 2)]
    owner = exchange(slots)
    quarters = [added([part[r : r + 1] for part in parts]) for r in range(4)]
    parts = [quarters[0]] + [across(quarters[r], 0, 4 * r) for r in range(1, 4)]
    piece = added(parts)
    column = jnp.concatenate([piece] + [across(piece, 0, 4 * r) for r in range(1, 4)], axis=0)
    column, owner = lax.optimization_barrier((column, owner))
    beside = across(column, 0, 2)
    row_grads = expand(ids, owner.reshape(bags, E), rows)
    parts = [column, beside, across(column, 0, 1), across(beside, 0, 1)]
    parts, row_grads = lax.optimization_barrier((parts, row_grads))
    return row_grads, finish(pos, parts, factor)


def per_device(
    table_rows,
    bag_ids,
    slot_feature,
    block_exponent,
    fm_project,
    fm_output,
    mix_weight,
    norm_gain,
    out_cotangent,
):
    tables, groups = lax.axis_size("mp"), lax.axis_size("dp")
    f_dev = F // tables
    bags = SAMP_DEV * tables * f_dev
    rows = table_rows.shape[2]
    ids = bag_ids.reshape(1, rows)
    factor = 1.0 / float(SAMP_DEV * tables * groups) ** 0.5
    pos = jnp.stack([lax.axis_index("dp"), lax.axis_index("mp")]).astype(jnp.int32)

    pooled = pool(ids, table_rows.reshape(rows, E), bags).reshape(tables, SAMP_DEV * f_dev, E)
    recv = exchange(pooled)
    weights = (fm_project.transpose(0, 2, 1), fm_output, mix_weight, norm_gain)
    if groups == 2:
        weights = [(part, lax.ppermute(part, "dp", [(0, 1), (1, 0)])) for part in weights]
    else:
        weights = [
            (lax.all_gather(part, "dp", axis=axis, tiled=True),)
            for part, axis in zip(weights, (2, 1, 1, 1))
        ]
    operands = prepare(pos, slot_feature, block_exponent, weights)
    packed = (groups, tables) == (2, 16)
    feats, slots, *grads = run_layers(pos, recv, out_cotangent, operands, f_dev, packed)
    if packed:
        row_grads, shares = return_packed(pos, slots, *grads, ids, factor)
        project_t, output_g, mix_g, gain_g = shares[1], shares[2], shares[0], shares[3]
    else:
        row_grads = expand(ids, exchange(slots).reshape(bags, E), rows)
        mix_g, project_t, output_g, gain_g = (
            lax.psum_scatter(part.astype(BF), "dp", scatter_dimension=axis, tiled=True).astype(F32)
            * factor
            for part, axis in zip(lax.psum(tuple(grads), "mp"), (1, 2, 1, 1))
        )
    return (
        feats,
        row_grads.reshape(1, 1, rows, E),
        project_t.transpose(0, 2, 1),
        output_g,
        mix_g,
        gain_g,
    )


def solution(mesh):
    placed = (
        P("dp", "mp", None, None),
        P("dp", "mp", None),
        P(),
        P(),
        P(None, "dp", None),
        P(None, "dp", None),
        P(None, "dp", None),
        P(None, "dp"),
        P(("dp", "mp"), None, None),
    )
    return jax.shard_map(
        per_device,
        mesh=mesh,
        in_specs=placed,
        out_specs=(
            P(("dp", "mp"), None, None),
            P("dp", "mp", None, None),
            P(None, "dp", None),
            P(None, "dp", None),
            P(None, "dp", None),
            P(None, "dp"),
        ),
        check_vma=False,
    )
```

time: 240 us -> 109 us (0.45)
  blocking collectives: 91.4 us -> 0 us
  other arithmetic: 45.5 us -> 0.94 us
  Pallas kernels: 0 us -> 30.2 us
  local copies, waits for them, and re-layouts: 29.1 us -> 3.1 us
  matrix products: 25.4 us -> 0 us
  starting transfers between devices: 11.4 us -> 33.3 us
  waiting for transfers between devices: 20.2 us -> 40.5 us
  between operations: 14.5 us -> 0.78 us
    psum x1 -> x0, blocking collectives: 78.1 us -> none  [per_device(): summed = lax.psum(partial_grads, 'mp')]
    ppermute x0 -> x17, waiting for transfers between devices: none -> 37.3 us  [the longest x13 26.8 us: across(): return lax.ppermute(x, ('dp', 'mp'), pairs)]
    pallas_call x0 -> x5, Pallas kernels: none -> 30.2 us  [the longest x1 16.6 us: run_layers(): pl.pallas_call(functools.partial(layers_kernel, f_dev=f_dev, packed=packe...]
    scatter-add x1 -> x0, other arithmetic: 26 us -> none  [per_device(): jax.ops.segment_sum(table_rows[0, 0].astype(jnp.float32), own_ids, num_se...]
    dot_general x24 -> x0, matrix products: 25.4 us -> none  [product(): return jnp.einsum(form, left, right, preferred_element_type=jnp.float32)]
    ppermute x0 -> x17, starting transfers between devices: none -> 18.8 us  [the longest x13 14.7 us: across(): return lax.ppermute(x, ('dp', 'mp'), pairs)]
    gather x5 -> x0, local copies, waits for them, and re-layouts: 15.7 us -> none  [the longest x1 10.2 us: per_device(): row_grads = owner_grads.reshape(BAGS, E)[own_ids].reshape(1, 1, -1, E)]
    all_gather x3 -> x0, blocking collectives: 13.3 us -> none  [the longest x1 4.59 us: per_device(): lax.all_gather(fm_project, 'dp', axis=1, tiled=True)]
  transfers between devices with their start and end apart: 7 -> 19, of which waited for: 3 -> 12; matrix products, arithmetic and copies ran while one was open for 19% -> 1% of each run, Pallas kernels for 0% -> 7%
where the time goes in v2:
time: 109 us
  waiting for transfers between devices  40.5 us (37%)
  starting transfers between devices  33.3 us (31%)
  Pallas kernels  30.2 us (28%)
  local copies, waits for them, and re-layouts  3.1 us (3%)
    ppermute x13, waiting for transfers between devices, across(): return lax.ppermute(x, ('dp', 'mp'), pairs)  26.8 us
    pallas_call x1, Pallas kernels, run_layers(): pl.pallas_call(functools.partial(layers_kernel, f_dev=f_dev, packed=packe...  16.6 us
    ppermute x13, starting transfers between devices, across(): return lax.ppermute(x, ('dp', 'mp'), pairs)  14.7 us
    all_to_all x2, starting transfers between devices, exchange(): return lax.all_to_all(x, 'mp', split_axis=0, concat_axis=0, tiled=True)  14.5 us
    ppermute x4, waiting for transfers between devices, per_device(): lax.ppermute(part, 'dp', [(0, 1), (1, 0)])  10.4 us
    ppermute x4, starting transfers between devices, per_device(): lax.ppermute(part, 'dp', [(0, 1), (1, 0)])  4.12 us
    pallas_call x1, Pallas kernels, expand(): pl.pallas_call(expand_kernel, out_shape=jax.ShapeDtypeStruct((rows, E), B...  3.99 us
    pallas_call x1, Pallas kernels, pool(): pl.pallas_call(pool_kernel, out_shape=jax.ShapeDtypeStruct((bags, E), BF)...  3.78 us
  transfers between devices with their start and end apart: 19, of which 12 were waited for; matrix products, arithmetic and copies ran while one was open for 1% of the time, Pallas kernels for 7%

profile of v2, /device:TPU:0, one launch (start us, length us, event | category | flops | bytes accessed | tf_op | source)
XLA Modules:
  0.0 108.9 jit_solution(17061581272478676692)
XLA Ops:
  0.6 3.8 %pool.1 = bf16[4096,128]{1,0:T(8,128)(2,1)} custom-call(s32[1,4608]{1,0:T(1,128)} %bitcast.15, bf16[4608,128]{1,0:T(8,128)(2,1)} %bitcast.13), custom_call_target="tpu_custom_call" | custom-call | tf_op jit(solution)/shard_map/pool/pallas_call | solution.py:76
  4.4 7.5 %all-to-all-start = ((bf16[16,256,128]{2,1,0:T(8,128)(2,1)}), bf16[16,256,128]{2,1,0:T(8,128)(2,1)S(1)}, u32[]{:S(2)}, u32[]{:S(2)}) async-start(bf16[16,256,128]{2,1,0:T(8,128)(2,1)} %bitcast.12), calls=%async_computation | async-start | bytes 2097152 | tf_op jit(solution)/shard_map/all_to_all | solution.py:486
  11.9 1.6 %collective-permute-start.2 = (bf16[2,256,512]{2,1,0:T(8,128)(2,1)S(1)}, bf16[2,256,512]{2,1,0:T(8,128)(2,1)S(1)}, u32[]{:S(2)}, u32[]{:S(2)}) collective-permute-start(bf16[2,256,512]{2,1,0:T(8,128)(2,1)S(1)} %copy-done.4), channel_id=1, source_target_pairs={{0,16},{16,0},{1,17},{17,1},{2,18},{18,2},{3,19},{19,3},{4,20},{20... | collective-permute-start | bytes 1572872 | tf_op jit(solution)/shard_map/ppermute | solution.py:532
  14.0 1.5 %collective-permute-start.1 = (bf16[2,16,128]{2,1,0:T(8,128)(2,1)S(1)}, bf16[2,16,128]{2,1,0:T(8,128)(2,1)S(1)}, u32[]{:S(2)}, u32[]{:S(2)}) collective-permute-start(bf16[2,16,128]{2,1,0:T(8,128)(2,1)S(1)} %copy-done.11), channel_id=1, source_target_pairs={{0,16},{16,0},{1,17},{17,1},{2,18},{18,2},{3,19},{19,3},{4,20},{20... | collective-permute-start | bytes 24584 | tf_op jit(solution)/shard_map/ppermute | solution.py:532
  16.1 0.7 pad_add_fusion.pos_ref
  16.7 10.0 %collective-permute-done.3.refs_7_ = bf16[2,64]{1,0:T(2,128)(2,1)S(1)} collective-permute-done((bf16[2,64]{1,0:T(2,128)(2,1)S(1)}, bf16[2,64]{1,0:T(2,128)(2,1)S(1)}, u32[]{:S(2)}, u32[]{:S(2)}) %collective-permute-start.3) | collective-permute-done | bytes 288 | tf_op jit(solution)/shard_map/ppermute | solution.py:532
  27.2 0.8 copy-done.5
  28.0 3.6 %prepare.1 = (bf16[2,544,512]{2,1,0:T(8,128)(2,1)}, bf16[2,512,512]{2,1,0:T(8,128)(2,1)}, bf16[2,128,256]{2,1,0:T(8,128)(2,1)}, bf16[2,512,128]{2,1,0:T(8,128)(2...) custom-call(s32[2]{0:T(128)} %pad_add_fusion.pos_ref, ...), custom_call_target="tpu_custom_call" | custom-call | tf_op jit(solution)/shard_map/prepare/pallas_call | solution.py:163
  31.6 3.3 %all-to-all-done.recv_hbm = bf16[16,256,128]{2,1,0:T(8,128)(2,1)S(1)} async-done(((bf16[16,256,128]{2,1,0:T(8,128)(2,1)}), bf16[16,256,128]{2,1,0:T(8,128)(2,1)S(1)}, u32[]{:S(2)}, u32[]{:S(2)}) %all-to-all-start) | async-done | bytes 1048608 | tf_op jit(solution)/shard_map/all_to_all | solution.py:486
  34.9 1.0 copy-done.1
  35.8 16.6 %layers.1 = (bf16[8,512,128]{2,1,0:T(8,128)(2,1)}, bf16[16,256,128]{2,1,0:T(8,128)(2,1)}, bf16[16,144,128]{2,1,0:T(8,128)(2,1)}, bf16[16,144,128]{2,1,0:T(8,128)(2,1)}) custom-call(s32[2]{0:T(128)} %pad_add_fusion.pos_ref, f32[2,128]{1,0:T(2,128)} %get-tuple-element.29.gain_ref, bf16[16,256,128]{2,1,0:T(8,128)(2,1)} %copy-done.1, ...), custom_call_target="tpu_custom_call" | custom-call | tf_op jit(solution)/shard_map/layers/pallas_call | solution.py:407
  52.4 7.0 %all-to-all-start.1 = ((bf16[16,256,128]{2,1,0:T(8,128)(2,1)}), bf16[16,256,128]{2,1,0:T(8,128)(2,1)S(1)}, u32[]{:S(2)}, u32[]{:S(2)}) async-start(bf16[16,256,128]{2,1,0:T(8,128)(2,1)} %get-tuple-element.40), calls=%async_computation.1 | async-start | bytes 2097152 | tf_op jit(solution)/shard_map/all_to_all | solution.py:486
  59.9 1.6 %collective-permute-done.4 = bf16[16,144,128]{2,1,0:T(8,128)(2,1)S(1)} collective-permute-done((bf16[16,144,128]{2,1,0:T(8,128)(2,1)S(1)}, bf16[16,144,128]{2,1,0:T(8,128)(2,1)S(1)}, u32[]{:S(2)}, u32[]{:S(2)}) %collective-permute-start.4) | collective-permute-done | bytes 589856 | tf_op jit(solution)/shard_map/ppermute | solution.py:436
  61.7 2.9 %collective-permute-start.7 = (bf16[4,144,128]{2,1,0:T(8,128)(2,1)S(1)}, bf16[4,144,128]{2,1,0:T(8,128)(2,1)S(1)}, u32[]{:S(2)}, u32[]{:S(2)}) collective-permute-start(bf16[4,144,128]{2,1,0:T(8,128)(2,1)S(1)} %get-tuple-element.53), channel_id=1, source_target_pairs={{0,18},{1,19},{2,16},{3,17},{4,22},{5,23},{6,20},{7,21},{8,26},{9,... | collective-permute-start | bytes 442376 | tf_op jit(solution)/shard_map/ppermute | solution.py:436
  64.8 0.5 collective-permute-start.5
  65.3 10.3 %collective-permute-done.7 = bf16[4,144,128]{2,1,0:T(8,128)(2,1)S(1)} collective-permute-done((bf16[4,144,128]{2,1,0:T(8,128)(2,1)S(1)}, bf16[4,144,128]{2,1,0:T(8,128)(2,1)S(1)}, u32[]{:S(2)}, u32[]{:S(2)}) %collective-permute-start.7) | collective-permute-done | bytes 147488 | tf_op jit(solution)/shard_map/ppermute | solution.py:436
  75.6 2.4 %collective-permute-done.6 = bf16[4,144,128]{2,1,0:T(8,128)(2,1)S(1)} collective-permute-done((bf16[4,144,128]{2,1,0:T(8,128)(2,1)S(1)}, bf16[4,144,128]{2,1,0:T(8,128)(2,1)S(1)}, u32[]{:S(2)}, u32[]{:S(2)}) %collective-permute-start.6) | collective-permute-done | bytes 147488 | tf_op jit(solution)/shard_map/ppermute | solution.py:436
  78.0 1.0 collective-permute-start.8
  79.0 3.2 %collective-permute-start.10 = (bf16[1,144,128]{2,1,0:T(8,128)(2,1)S(1)}, bf16[1,144,128]{2,1,0:T(8,128)(2,1)S(1)}, u32[]{:S(2)}, u32[]{:S(2)}) collective-permute-start(bf16[1,144,128]{2,1,0:T(8,128)(2,1)S(1)} %get-tuple-element.57), channel_id=1, source_target_pairs={{0,12},{1,13},{2,14},{3,15},{4,8},{5,9},{6,10},{7,11},{8,4},{9,5},... | collective-permute-start | bytes 110600 | tf_op jit(solution)/shard_map/ppermute | solution.py:436
  82.7 1.5 %collective-permute-done.8 = bf16[1,144,128]{2,1,0:T(8,128)(2,1)S(1)} collective-permute-done((bf16[1,144,128]{2,1,0:T(8,128)(2,1)S(1)}, bf16[1,144,128]{2,1,0:T(8,128)(2,1)S(1)}, u32[]{:S(2)}, u32[]{:S(2)}) %collective-permute-start.8) | collective-permute-done | bytes 36896 | tf_op jit(solution)/shard_map/ppermute | solution.py:436
  84.2 0.7 collective-permute-done.10
  84.9 4.3 %collective-permute-done.9 = bf16[1,144,128]{2,1,0:T(8,128)(2,1)S(1)} collective-permute-done((bf16[1,144,128]{2,1,0:T(8,128)(2,1)S(1)}, bf16[1,144,128]{2,1,0:T(8,128)(2,1)S(1)}, u32[]{:S(2)}, u32[]{:S(2)}) %collective-permute-start.9) | collective-permute-done | bytes 36896 | tf_op jit(solution)/shard_map/ppermute | solution.py:436
  89.2 1.5 %collective-permute-start.13 = (bf16[1,144,128]{2,1,0:T(8,128)(2,1)S(1)}, bf16[1,144,128]{2,1,0:T(8,128)(2,1)S(1)}, u32[]{:S(2)}, u32[]{:S(2)}) collective-permute-start(bf16[1,144,128]{2,1,0:T(8,128)(2,1)S(1)} %add_convert_fusion.4), channel_id=1, source_target_pairs={{0,12},{1,13},{2,14},{3,15},{4,8},{5,9},{6,10},{7,11},{8,4},{9,5},... | collective-permute-start | bytes 110600 | tf_op jit(solution)/shard_map/ppermute | solution.py:436
  90.9 2.8 %collective-permute-start.11 = (bf16[1,144,128]{2,1,0:T(8,128)(2,1)S(1)}, bf16[1,144,128]{2,1,0:T(8,128)(2,1)S(1)}, u32[]{:S(2)}, u32[]{:S(2)}) collective-permute-start(bf16[1,144,128]{2,1,0:T(8,128)(2,1)S(1)} %add_convert_fusion.4), channel_id=1, source_target_pairs={{0,4},{1,5},{2,6},{3,7},{4,0},{5,1},{6,2},{7,3},{8,12},{9,13},{10,... | collective-permute-start | bytes 110600 | tf_op jit(solution)/shard_map/ppermute | solution.py:436
  93.7 1.6 %collective-permute-done.13 = bf16[1,144,128]{2,1,0:T(8,128)(2,1)S(1)} collective-permute-done((bf16[1,144,128]{2,1,0:T(8,128)(2,1)S(1)}, bf16[1,144,128]{2,1,0:T(8,128)(2,1)S(1)}, u32[]{:S(2)}, u32[]{:S(2)}) %collective-permute-start.13) | collective-permute-done | bytes 36896 | tf_op jit(solution)/shard_map/ppermute | solution.py:436
  95.3 0.8 collective-permute-done.12
  96.1 1.5 %collective-permute-start.14 = (bf16[4,144,128]{2,1,0:T(8,128)(2,1)S(1)}, bf16[4,144,128]{2,1,0:T(8,128)(2,1)S(1)}, u32[]{:S(2)}, u32[]{:S(2)}) collective-permute-start(bf16[4,144,128]{2,1,0:T(8,128)(2,1)S(1)} %pad_maximum_fusion.refs_0_), channel_id=1, source_target_pairs={{0,2},{1,3},{2,0},{3,1},{4,6},{5,7},{6,4},{7,5},{8,10},{9,11},{10,... | collective-permute-start | bytes 442376 | tf_op jit(solution)/shard_map/ppermute | solution.py:436
  97.7 3.7 %collective-permute-done.14.refs_1_ = bf16[4,144,128]{2,1,0:T(8,128)(2,1)S(1)} collective-permute-done((bf16[4,144,128]{2,1,0:T(8,128)(2,1)S(1)}, bf16[4,144,128]{2,1,0:T(8,128)(2,1)S(1)}, u32[]{:S(2)}, u32[]{:S(2)}) %collective-permute-start.14) | collective-permute-done | bytes 147488 | tf_op jit(solution)/shard_map/ppermute | solution.py:436
  101.3 4.0 %expand.1 = bf16[4608,128]{1,0:T(8,128)(2,1)} custom-call(s32[1,4608]{1,0:T(1,128)} %bitcast.16, bf16[4096,128]{1,0:T(8,128)(2,1)} %bitcast.11), custom_call_target="tpu_custom_call" | custom-call | tf_op jit(solution)/shard_map/expand/pallas_call | solution.py:100
  105.4 0.6 copy-done.7
  106.0 0.7 copy-done.8
  106.7 2.2 %finish.1 = (f32[2,256,512]{2,1,0:T(8,128)}, f32[2,32,256]{2,1,0:T(8,128)}, f32[2,16,128]{2,1,0:T(8,128)}, f32[2,64]{1,0:T(2,128)}) custom-call(s32[2]{0:T(128)} %pad_add_fusion.pos_ref, bf16[4,144,128]{2,1,0:T(8,128)(2,1)} %copy-done.3, bf16[4,144,128]{2,1,0:T(8,128)(2,1)} %copy-done.6, bf16[4,144,128]{2,1,0:T(8,128)(2,1)} %copy-done.7, ...), custom_call_target="tpu_custom_call" | custom-call | tf_op jit(solution)/shard_map/finish/pallas_call | solution.py:469
  (48 shorter events, 3.0 us)
Async XLA Ops:
  4.4 7.5 %copy-start.4 = (bf16[2,256,512]{2,1,0:T(8,128)(2,1)S(1)}, bf16[2,256,512]{2,1,0:T(8,128)(2,1)}, u32[]{:S(2)}) copy-start(bf16[2,256,512]{2,1,0:T(8,128)(2,1)} %refs_4_.1) | copy-start | bytes 1572868
  4.4 9.1 %copy-start.13 = (bf16[2,64]{1,0:T(2,128)(2,1)S(1)}, bf16[2,64]{1,0:T(2,128)(2,1)}, u32[]{:S(2)}) copy-start(bf16[2,64]{1,0:T(2,128)(2,1)} %refs_6_.1) | copy-start | bytes 772
  4.4 9.6 %copy-start.11 = (bf16[2,16,128]{2,1,0:T(8,128)(2,1)S(1)}, bf16[2,16,128]{2,1,0:T(8,128)(2,1)}, u32[]{:S(2)}) copy-start(bf16[2,16,128]{2,1,0:T(8,128)(2,1)} %refs_2_.1) | copy-start | bytes 24580
  4.4 11.2 %copy-start.9 = (bf16[2,256,32]{1,2,0:T(8,128)(2,1)S(1)}, bf16[2,256,32]{1,2,0:T(8,128)(2,1)}, u32[]{:S(2)}) copy-start(bf16[2,256,32]{1,2,0:T(8,128)(2,1)} %param.13) | copy-start | bytes 98308
  4.4 30.5 %all-to-all-start = ((bf16[16,256,128]{2,1,0:T(8,128)(2,1)}), bf16[16,256,128]{2,1,0:T(8,128)(2,1)S(1)}, u32[]{:S(2)}, u32[]{:S(2)}) async-start(bf16[16,256,128]{2,1,0:T(8,128)(2,1)} %bitcast.12), calls=%async_computation | async-start | bytes 2097152 | tf_op jit(solution)/shard_map/all_to_all | solution.py:486
  11.9 15.2 %collective-permute-start.2 = (bf16[2,256,512]{2,1,0:T(8,128)(2,1)S(1)}, bf16[2,256,512]{2,1,0:T(8,128)(2,1)S(1)}, u32[]{:S(2)}, u32[]{:S(2)}) collective-permute-start(bf16[2,256,512]{2,1,0:T(8,128)(2,1)S(1)} %copy-done.4), channel_id=1, source_target_pairs={{0,16},{16,0},{1,17},{17,1},{2,18},{18,2},{3,19},{19,3},{4,20},{20... | collective-permute-start | bytes 1572872 | tf_op jit(solution)/shard_map/ppermute | solution.py:532
  13.5 13.2 %collective-permute-start.3 = (bf16[2,64]{1,0:T(2,128)(2,1)S(1)}, bf16[2,64]{1,0:T(2,128)(2,1)S(1)}, u32[]{:S(2)}, u32[]{:S(2)}) collective-permute-start(bf16[2,64]{1,0:T(2,128)(2,1)S(1)} %copy-done.13), channel_id=1, source_target_pairs={{0,16},{16,0},{1,17},{17,1},{2,18},{18,2},{3,19},{19,3},{4,20},{20... | collective-permute-start | bytes 776 | tf_op jit(solution)/shard_map/ppermute | solution.py:532
  14.0 12.8 %collective-permute-start.1 = (bf16[2,16,128]{2,1,0:T(8,128)(2,1)S(1)}, bf16[2,16,128]{2,1,0:T(8,128)(2,1)S(1)}, u32[]{:S(2)}, u32[]{:S(2)}) collective-permute-start(bf16[2,16,128]{2,1,0:T(8,128)(2,1)S(1)} %copy-done.11), channel_id=1, source_target_pairs={{0,16},{16,0},{1,17},{17,1},{2,18},{18,2},{3,19},{19,3},{4,20},{20... | collective-permute-start | bytes 24584 | tf_op jit(solution)/shard_map/ppermute | solution.py:532
  15.6 11.6 %collective-permute-start = (bf16[2,32,256]{2,1,0:T(8,128)(2,1)S(1)}, bf16[2,32,256]{2,1,0:T(8,128)(2,1)S(1)}, u32[]{:S(2)}, u32[]{:S(2)}) collective-permute-start(bf16[2,32,256]{2,1,0:T(8,128)(2,1)S(1)} %bitcast.18), channel_id=1, source_target_pairs={{0,16},{16,0},{1,17},{17,1},{2,18},{18,2},{3,19},{19,3},{4,20},{20... | collective-permute-start | bytes 98312 | tf_op jit(solution)/shard_map/ppermute | solution.py:532
  26.8 1.2 %copy-start.14 = (bf16[2,64]{1,0:T(2,128)(2,1)}, bf16[2,64]{1,0:T(2,128)(2,1)S(1)}, u32[]{:S(2)}) copy-start(bf16[2,64]{1,0:T(2,128)(2,1)S(1)} %collective-permute-done.3.refs_7_) | copy-start | bytes 772
  26.8 1.1 %copy-start.12 = (bf16[2,16,128]{2,1,0:T(8,128)(2,1)}, bf16[2,16,128]{2,1,0:T(8,128)(2,1)S(1)}, u32[]{:S(2)}) copy-start(bf16[2,16,128]{2,1,0:T(8,128)(2,1)S(1)} %collective-permute-done.1.refs_3_) | copy-start | bytes 24580
  27.2 0.8 copy-start.10
  34.9 1.0 copy-start.1
  52.4 7.0 %copy-start.15 = (bf16[16,144,128]{2,1,0:T(8,128)(2,1)S(1)}, bf16[16,144,128]{2,1,0:T(8,128)(2,1)}, u32[]{:S(2)}) copy-start(bf16[16,144,128]{2,1,0:T(8,128)(2,1)} %get-tuple-element.39) | copy-start | bytes 1769476
  52.4 9.1 %copy-start.2 = (bf16[16,144,128]{2,1,0:T(8,128)(2,1)S(1)}, bf16[16,144,128]{2,1,0:T(8,128)(2,1)}, u32[]{:S(2)}) copy-start(bf16[16,144,128]{2,1,0:T(8,128)(2,1)} %get-tuple-element.38) | copy-start | bytes 1769476
  52.4 43.7 %all-to-all-start.1 = ((bf16[16,256,128]{2,1,0:T(8,128)(2,1)}), bf16[16,256,128]{2,1,0:T(8,128)(2,1)S(1)}, u32[]{:S(2)}, u32[]{:S(2)}) async-start(bf16[16,256,128]{2,1,0:T(8,128)(2,1)} %get-tuple-element.40), calls=%async_computation.1 | async-start | bytes 2097152 | tf_op jit(solution)/shard_map/all_to_all | solution.py:486
  59.5 2.1 %collective-permute-start.4 = (bf16[16,144,128]{2,1,0:T(8,128)(2,1)S(1)}, bf16[16,144,128]{2,1,0:T(8,128)(2,1)S(1)}, u32[]{:S(2)}, u32[]{:S(2)}) collective-permute-start(bf16[16,144,128]{2,1,0:T(8,128)(2,1)S(1)} %copy-done.15), channel_id=1, source_target_pairs={{0,1},{1,0},{2,3},{3,2},{4,5},{5,4},{6,7},{7,6},{8,9},{9,8},{10,11... | collective-permute-start | bytes 1769480 | tf_op jit(solution)/shard_map/ppermute | solution.py:436
  61.7 13.9 %collective-permute-start.7 = (bf16[4,144,128]{2,1,0:T(8,128)(2,1)S(1)}, bf16[4,144,128]{2,1,0:T(8,128)(2,1)S(1)}, u32[]{:S(2)}, u32[]{:S(2)}) collective-permute-start(bf16[4,144,128]{2,1,0:T(8,128)(2,1)S(1)} %get-tuple-element.53), channel_id=1, source_target_pairs={{0,18},{1,19},{2,16},{3,17},{4,22},{5,23},{6,20},{7,21},{8,26},{9,... | collective-permute-start | bytes 442376 | tf_op jit(solution)/shard_map/ppermute | solution.py:436
  64.6 13.3 %collective-permute-start.6 = (bf16[4,144,128]{2,1,0:T(8,128)(2,1)S(1)}, bf16[4,144,128]{2,1,0:T(8,128)(2,1)S(1)}, u32[]{:S(2)}, u32[]{:S(2)}) collective-permute-start(bf16[4,144,128]{2,1,0:T(8,128)(2,1)S(1)} %get-tuple-element.54), channel_id=1, source_target_pairs={{0,2},{1,3},{2,0},{3,1},{4,6},{5,7},{6,4},{7,5},{8,10},{9,11},{10,... | collective-permute-start | bytes 442376 | tf_op jit(solution)/shard_map/ppermute | solution.py:436
  64.8 13.2 %collective-permute-start.5 = (bf16[4,144,128]{2,1,0:T(8,128)(2,1)S(1)}, bf16[4,144,128]{2,1,0:T(8,128)(2,1)S(1)}, u32[]{:S(2)}, u32[]{:S(2)}) collective-permute-start(bf16[4,144,128]{2,1,0:T(8,128)(2,1)S(1)} %get-tuple-element.55), channel_id=1, source_target_pairs={{0,16},{1,17},{2,18},{3,19},{4,20},{5,21},{6,22},{7,23},{8,24},{9,... | collective-permute-start | bytes 442376 | tf_op jit(solution)/shard_map/ppermute | solution.py:436
  78.0 6.1 %collective-permute-start.8 = (bf16[1,144,128]{2,1,0:T(8,128)(2,1)S(1)}, bf16[1,144,128]{2,1,0:T(8,128)(2,1)S(1)}, u32[]{:S(2)}, u32[]{:S(2)}) collective-permute-start(bf16[1,144,128]{2,1,0:T(8,128)(2,1)S(1)} %get-tuple-element.56), channel_id=1, source_target_pairs={{0,4},{1,5},{2,6},{3,7},{4,0},{5,1},{6,2},{7,3},{8,12},{9,13},{10,... | collective-permute-start | bytes 110600 | tf_op jit(solution)/shard_map/ppermute | solution.py:436
  79.0 5.9 %collective-permute-start.10 = (bf16[1,144,128]{2,1,0:T(8,128)(2,1)S(1)}, bf16[1,144,128]{2,1,0:T(8,128)(2,1)S(1)}, u32[]{:S(2)}, u32[]{:S(2)}) collective-permute-start(bf16[1,144,128]{2,1,0:T(8,128)(2,1)S(1)} %get-tuple-element.57), channel_id=1, source_target_pairs={{0,12},{1,13},{2,14},{3,15},{4,8},{5,9},{6,10},{7,11},{8,4},{9,5},... | collective-permute-start | bytes 110600 | tf_op jit(solution)/shard_map/ppermute | solution.py:436
  82.2 7.0 %collective-permute-start.9 = (bf16[1,144,128]{2,1,0:T(8,128)(2,1)S(1)}, bf16[1,144,128]{2,1,0:T(8,128)(2,1)S(1)}, u32[]{:S(2)}, u32[]{:S(2)}) collective-permute-start(bf16[1,144,128]{2,1,0:T(8,128)(2,1)S(1)} %get-tuple-element.58), channel_id=1, source_target_pairs={{0,8},{1,9},{2,10},{3,11},{4,12},{5,13},{6,14},{7,15},{8,0},{9,1},... | collective-permute-start | bytes 110600 | tf_op jit(solution)/shard_map/ppermute | solution.py:436
  89.2 6.0 %collective-permute-start.13 = (bf16[1,144,128]{2,1,0:T(8,128)(2,1)S(1)}, bf16[1,144,128]{2,1,0:T(8,128)(2,1)S(1)}, u32[]{:S(2)}, u32[]{:S(2)}) collective-permute-start(bf16[1,144,128]{2,1,0:T(8,128)(2,1)S(1)} %add_convert_fusion.4), channel_id=1, source_target_pairs={{0,12},{1,13},{2,14},{3,15},{4,8},{5,9},{6,10},{7,11},{8,4},{9,5},... | collective-permute-start | bytes 110600 | tf_op jit(solution)/shard_map/ppermute | solution.py:436
  90.7 5.3 %collective-permute-start.12 = (bf16[1,144,128]{2,1,0:T(8,128)(2,1)S(1)}, bf16[1,144,128]{2,1,0:T(8,128)(2,1)S(1)}, u32[]{:S(2)}, u32[]{:S(2)}) collective-permute-start(bf16[1,144,128]{2,1,0:T(8,128)(2,1)S(1)} %add_convert_fusion.4), channel_id=1, source_target_pairs={{0,8},{1,9},{2,10},{3,11},{4,12},{5,13},{6,14},{7,15},{8,0},{9,1},... | collective-permute-start | bytes 110600 | tf_op jit(solution)/shard_map/ppermute | solution.py:436
  90.9 5.1 %collective-permute-start.11 = (bf16[1,144,128]{2,1,0:T(8,128)(2,1)S(1)}, bf16[1,144,128]{2,1,0:T(8,128)(2,1)S(1)}, u32[]{:S(2)}, u32[]{:S(2)}) collective-permute-start(bf16[1,144,128]{2,1,0:T(8,128)(2,1)S(1)} %add_convert_fusion.4), channel_id=1, source_target_pairs={{0,4},{1,5},{2,6},{3,7},{4,0},{5,1},{6,2},{7,3},{8,12},{9,13},{10,... | collective-permute-start | bytes 110600 | tf_op jit(solution)/shard_map/ppermute | solution.py:436
  96.1 9.3 %copy-start.3 = (bf16[4,144,128]{2,1,0:T(8,128)(2,1)}, bf16[4,144,128]{2,1,0:T(8,128)(2,1)S(1)}, u32[]{:S(2)}) copy-start(bf16[4,144,128]{2,1,0:T(8,128)(2,1)S(1)} %pad_maximum_fusion.refs_0_) | copy-start | bytes 442372
  96.1 5.2 %copy-start = (bf16[16,256,128]{2,1,0:T(8,128)(2,1)}, bf16[16,256,128]{2,1,0:T(8,128)(2,1)S(1)}, u32[]{:S(2)}) copy-start(bf16[16,256,128]{2,1,0:T(8,128)(2,1)S(1)} %all-to-all-done.1) | copy-start | bytes 3145732
  96.1 5.2 %collective-permute-start.14 = (bf16[4,144,128]{2,1,0:T(8,128)(2,1)S(1)}, bf16[4,144,128]{2,1,0:T(8,128)(2,1)S(1)}, u32[]{:S(2)}, u32[]{:S(2)}) collective-permute-start(bf16[4,144,128]{2,1,0:T(8,128)(2,1)S(1)} %pad_maximum_fusion.refs_0_), channel_id=1, source_target_pairs={{0,2},{1,3},{2,0},{3,1},{4,6},{5,7},{6,4},{7,5},{8,10},{9,11},{10,... | collective-permute-start | bytes 442376 | tf_op jit(solution)/shard_map/ppermute | solution.py:436
  97.7 7.7 %collective-permute-start.15 = (bf16[4,144,128]{2,1,0:T(8,128)(2,1)S(1)}, bf16[4,144,128]{2,1,0:T(8,128)(2,1)S(1)}, u32[]{:S(2)}, u32[]{:S(2)}) collective-permute-start(bf16[4,144,128]{2,1,0:T(8,128)(2,1)S(1)} %pad_maximum_fusion.refs_0_), channel_id=1, source_target_pairs={{0,1},{1,0},{2,3},{3,2},{4,5},{5,4},{6,7},{7,6},{8,9},{9,8},{10,11... | collective-permute-start | bytes 442376 | tf_op jit(solution)/shard_map/ppermute | solution.py:436
  101.3 4.0 %copy-start.6 = (bf16[4,144,128]{2,1,0:T(8,128)(2,1)}, bf16[4,144,128]{2,1,0:T(8,128)(2,1)S(1)}, u32[]{:S(2)}) copy-start(bf16[4,144,128]{2,1,0:T(8,128)(2,1)S(1)} %collective-permute-done.14.refs_1_) | copy-start | bytes 442372
  101.3 4.0 %collective-permute-start.16 = (bf16[4,144,128]{2,1,0:T(8,128)(2,1)S(1)}, bf16[4,144,128]{2,1,0:T(8,128)(2,1)S(1)}, u32[]{:S(2)}, u32[]{:S(2)}) collective-permute-start(bf16[4,144,128]{2,1,0:T(8,128)(2,1)S(1)} %collective-permute-done.14.refs_1_), channel_id=1, source_target_pairs={{0,1},{1,0},{2,3},{3,2},{4,5},{5,4},{6,7},{7,6},{8,9},{9,8},{10,11... | collective-permute-start | bytes 442376 | tf_op jit(solution)/shard_map/ppermute | solution.py:436
  (3 other events, 2.1 us)

commit v3 on v2

--- a/solution.py
+++ b/solution.py
@@ -12,19 +12,20 @@
 K = 32
 LAYERS = 2
 SAMP_DEV = 8
-PAIR = 2
+PAIR = 4
 PW = PAIR * E
 PAIRS = SAMP_DEV // PAIR
 CHUNK = 128
 EPS = 1e-05
-VMEM_LIMIT = 62 * 1024 * 1024
+MIB = 1024 * 1024
+WHOLE, PART = 62, 46
 PIECE = 144
 BF = jnp.bfloat16
 F32 = jnp.float32
 
 
-def params():
-    return pltpu.CompilerParams(vmem_limit_bytes=VMEM_LIMIT)
+def params(mib):
+    return pltpu.CompilerParams(vmem_limit_bytes=mib * MIB)
 
 
 def dot(left, right):
@@ -59,7 +60,7 @@
 
 
 BLOCK = 128
-ANY = pl.BlockSpec(memory_space=pltpu.HBM)
+HBM = pl.BlockSpec(memory_space=pltpu.HBM)
 VMEM = pl.BlockSpec(memory_space=pltpu.VMEM)
 
 
@@ -76,7 +77,7 @@
     return pl.pallas_call(
         pool_kernel,
         out_shape=jax.ShapeDtypeStruct((bags, E), BF),
-        compiler_params=params(),
+        compiler_params=params(WHOLE),
         name="pool",
     )(ids, rows)
 
@@ -101,7 +102,7 @@
         expand_kernel,
         out_shape=jax.ShapeDtypeStruct((rows, E), BF),
         scratch_shapes=[pltpu.VMEM((BLOCK, BLOCK), jnp.int32)],
-        compiler_params=params(),
+        compiler_params=params(PART),
         name="expand",
     )(ids, owner)
 
@@ -127,18 +128,12 @@
         back_ref[layer] = left_ref[layer, :F, :].T
         project_t = joined([ref[layer] for ref in projects], 1)
         left_ref[layer, F:, :] = project_t
-        none = jnp.zeros((PAIR * K, F), BF)
-        project_ref[layer] = jnp.concatenate([none, project_t, none[:K]], axis=0).T
+        none = jnp.zeros((E - K, F), BF)
+        project_ref[layer] = jnp.concatenate([project_t, none], axis=0).T
         row = joined([ref[layer].astype(F32) for ref in outputs], 0).astype(BF)
-        none = jnp.zeros_like(row)
-        diag_ref[layer] = jnp.concatenate(
-            [
-                jnp.concatenate([row, none], axis=1),
-                jnp.concatenate([none, row], axis=1),
-                jnp.zeros((E - PAIR * K, PW), BF),
-            ],
-            axis=0,
-        )
+        diag_ref[layer] = jnp.zeros((PAIR * K, PW), BF)
+        for t in range(PAIR):
+            diag_ref[layer, t * K : (t + 1) * K, t * E : (t + 1) * E] = row
     gain_ref[...] = joined([ref[...].astype(F32) for ref in gains], 1)
     expo = expo_ref[...]
     small = jnp.where(
@@ -165,7 +160,7 @@
         out_shape=(
             jax.ShapeDtypeStruct((LAYERS, F + K, F), BF),
             jax.ShapeDtypeStruct((LAYERS, F, F), BF),
-            jax.ShapeDtypeStruct((LAYERS, E, PW), BF),
+            jax.ShapeDtypeStruct((LAYERS, PAIR * K, PW), BF),
             jax.ShapeDtypeStruct((LAYERS, F, E), BF),
             jax.ShapeDtypeStruct((LAYERS, E), F32),
             jax.ShapeDtypeStruct((F, E), F32),
@@ -174,7 +169,7 @@
         ),
         in_specs=[pl.BlockSpec(memory_space=pltpu.SMEM)] + [VMEM] * (2 + len(flat)),
         out_specs=(VMEM,) * 8,
-        compiler_params=params(),
+        compiler_params=params(WHOLE),
         name="prepare",
     )(pos, slot_feature.reshape(1, F), block_exponent.T, *flat)
 
@@ -189,14 +184,14 @@
 CONSTANTS = ("perm", "scale", "left", "diag", "back", "project", "unperm")
 
 
-def layers_kernel(pos_ref, gain_ref, recv_hbm, cot_hbm, *refs, f_dev, packed):
+def layers_kernel(pos_ref, gain_ref, recv_ref, cot_hbm, *refs, f_dev, packed):
     sources, refs = dict(zip(CONSTANTS, refs)), refs[len(CONSTANTS) :]
     feats_hbm, slots_hbm = refs[:2]
     grads = 2 if packed else 4
     grad_outs, refs = refs[2 : 2 + grads], refs[2 + grads :]
     held, refs = dict(zip(CONSTANTS, refs)), refs[len(CONSTANTS) :]
-    recv_ref, cot_ref, feats_ref, slots_ref = refs[:4]
-    grad_refs, refs = refs[4 : 4 + grads], refs[4 + grads :]
+    cot_ref, feats_ref, slots_ref = refs[:3]
+    grad_refs, refs = refs[3 : 3 + grads], refs[3 + grads :]
     xs, ts, normed_s, inv_s, grad_s, next_s, wacc, gacc, dm, pj, ex, sems = refs
     left_ref, back_ref, diag_ref = held["left"], held["back"], held["diag"]
     project_ref, scale_ref = held["project"], held["scale"]
@@ -208,7 +203,6 @@
     def fetch(name):
         copies.start(name, sources[name], held[name])
 
-    copies.start("recv", recv_hbm, recv_ref)
     for name in ("perm", "scale", "left", "diag"):
         fetch(name)
     copies.start("cot", cot_hbm, cot_ref)
@@ -223,6 +217,7 @@
         x = dot(held["perm"][...], unslot(recv_ref[:, slot_rows(p)], f_dev))
         scale = scale_ref[...]
         x = (x * jnp.concatenate([scale] * PAIR, axis=1)).astype(BF)
+        yield
         same = (
             lax.broadcasted_iota(jnp.int32, (PAIR * K, PW), 0) // K
             == lax.broadcasted_iota(jnp.int32, (PAIR * K, PW), 1) // E
@@ -234,7 +229,7 @@
             projected = jnp.concatenate([mixed[F:]] * PAIR, axis=0)
             projected = jnp.where(same, projected, 0.0).astype(BF)
             paired = dot_nt(x, projected).astype(BF)
-            low = dot(paired, diag_ref[layer, : PAIR * K])
+            low = dot(paired, diag_ref[layer])
             gain = gain_ref[layer : layer + 1, :]
             saved.append((x, projected, paired))
             yield
@@ -282,7 +277,7 @@
             total_low = next_s[p]
             ts[layer, :F, columns] = total_low
             grad_paired = dot_nt(total_low, diag_ref[layer]).astype(BF)
-            wide = dot_tn(grad_paired[:, : PAIR * K], x)
+            wide = dot_tn(grad_paired, x)
             grad_projected = jnp.concatenate(
                 [wide[t * K : (t + 1) * K, t * E : (t + 1) * E] for t in range(PAIR)], axis=1
             ).astype(BF)
@@ -290,9 +285,9 @@
             wide = dot_tn(paired, total_low)
             for t in range(PAIR):
                 wacc[layer] += wide[t * K : (t + 1) * K, t * E : (t + 1) * E]
-            rest = jnp.zeros((E - (PAIR + 1) * K, PW), BF)
+            rest = jnp.zeros((E - K, PW), BF)
             upstream = dot(back_ref[layer], total_low) + dot(
-                grad_paired + project_ref[layer],
+                jnp.concatenate([grad_paired, project_ref[layer]], axis=1),
                 jnp.concatenate([projected, grad_projected, rest], axis=0),
             )
             yield
@@ -356,19 +351,20 @@
                         grad_refs[core][place] = jnp.concatenate(pieces, axis=0).astype(BF)
 
     programs = [pair_steps(p) for p in range(PAIRS)]
-    phases = 4 * LAYERS + 1
-    for tick in range(phases + PAIRS - 1):
+    phases = 4 * LAYERS + 2
+    for tick in range(phases):
         if tick == 0:
-            copies.wait("recv", "perm", "scale", "left", "diag")
-        if tick == 2 * LAYERS:
+            copies.wait("perm", "scale")
+        if tick == 1:
+            copies.wait("left", "diag")
+        if tick == 2 * LAYERS + 1:
             copies.wait("cot", "back", "project", "unperm")
-        if tick == 2 * LAYERS + PAIRS - 1:
+        if tick == 2 * LAYERS + 1:
             copies.start("feats", feats_ref, feats_hbm)
-        for p in range(PAIRS):
-            if 0 <= tick - p < phases:
-                next(programs[p])
+        for program in programs:
+            next(program)
         for layer in reversed(range(LAYERS)):
-            if tick - (PAIRS - 1) == phases - 2 - 2 * layer:
+            if tick == phases - 1 - 2 * layer:
                 weight_grads(layer)
     copies.start("slots", slots_ref, slots_hbm)
     for n in range(grads):
@@ -403,14 +399,15 @@
     def scratch(x):
         return pltpu.VMEM(x.shape, x.dtype)
 
-    copies = len(constants) + 4 + len(grads)
+    copies = len(constants) + 3 + len(grads)
     return pl.pallas_call(
         functools.partial(layers_kernel, f_dev=f_dev, packed=packed),
         out_shape=outs,
-        in_specs=[pl.BlockSpec(memory_space=pltpu.SMEM), VMEM] + [ANY] * (2 + len(constants)),
-        out_specs=[ANY] * len(outs),
+        in_specs=[pl.BlockSpec(memory_space=pltpu.SMEM), VMEM, VMEM]
+        + [HBM] * (1 + len(constants)),
+        out_specs=[HBM] * len(outs),
         scratch_shapes=[scratch(x) for x in constants]
-        + [scratch(recv), scratch(cotangent)]
+        + [scratch(cotangent)]
         + [scratch(x) for x in outs]
         + [
             pltpu.VMEM((LAYERS, F, width), BF),
@@ -426,7 +423,7 @@
             pltpu.VMEM((2, 16, 8, E), F32),
             pltpu.SemaphoreType.DMA((copies,)),
         ],
-        compiler_params=params(),
+        compiler_params=params(58),
         name="layers",
     )(pos, gain, recv, cotangent, *constants)
 
@@ -477,7 +474,7 @@
         in_specs=[pl.BlockSpec(memory_space=pltpu.SMEM)] + [VMEM] * 4,
         out_specs=[VMEM] * 4,
         scratch_shapes=[pltpu.VMEM((16, 8, E), F32)] * 2,
-        compiler_params=params(),
+        compiler_params=params(PART),
         name="finish",
     )(pos, *parts)
 
@@ -501,6 +498,7 @@
     column, owner = lax.optimization_barrier((column, owner))
     beside = across(column, 0, 2)
     row_grads = expand(ids, owner.reshape(bags, E), rows)
+    beside, row_grads = lax.optimization_barrier((beside, row_grads))
     parts = [column, beside, across(column, 0, 1), across(beside, 0, 1)]
     parts, row_grads = lax.optimization_barrier((parts, row_grads))
     return row_grads, finish(pos, parts, factor)

time: 109 us -> 103 us (0.945)
  Pallas kernels: 30.2 us -> 26.4 us
  waiting for transfers between devices: 40.5 us -> 39.2 us
  local copies, waits for them, and re-layouts: 3.1 us -> 1.81 us
    pallas_call x1, Pallas kernels: 16.6 us -> 14.6 us  [run_layers(): pl.pallas_call(functools.partial(layers_kernel, f_dev=f_dev, packed=packe...]
    ppermute x13, waiting for transfers between devices: 26.8 us -> 25.5 us  [across(): return lax.ppermute(x, ('dp', 'mp'), pairs)]
    pallas_call x1, Pallas kernels: 3.99 us -> 2.69 us  [expand(): pl.pallas_call(expand_kernel, out_shape=jax.ShapeDtypeStruct((rows, E), B...]
    unnamed x32 -> x26, local copies, waits for them, and re-layouts: 3.1 us -> 1.81 us
  transfers between devices with their start and end apart: 19 -> 19, of which waited for: 12 -> 13; matrix products, arithmetic and copies ran while one was open for 1% -> 1% of each run, Pallas kernels for 7% -> 6%
where the time goes in v3:
time: 103 us; the launch traced here: 102 us
  waiting for transfers between devices  39.2 us (38%)
  starting transfers between devices  33.3 us (32%)
  Pallas kernels  26.4 us (26%)
  local copies, waits for them, and re-layouts  1.81 us (2%)
    ppermute x13, waiting for transfers between devices, across(): return lax.ppermute(x, ('dp', 'mp'), pairs)  25.5 us
    ppermute x13, starting transfers between devices, across(): return lax.ppermute(x, ('dp', 'mp'), pairs)  14.7 us
    pallas_call x1, Pallas kernels, run_layers(): pl.pallas_call(functools.partial(layers_kernel, f_dev=f_dev, packed=packe...  14.6 us
    all_to_all x2, starting transfers between devices, exchange(): return lax.all_to_all(x, 'mp', split_axis=0, concat_axis=0, tiled=True)  14.5 us
    ppermute x4, waiting for transfers between devices, per_device(): lax.ppermute(part, 'dp', [(0, 1), (1, 0)])  10.5 us
    ppermute x4, starting transfers between devices, per_device(): lax.ppermute(part, 'dp', [(0, 1), (1, 0)])  4.12 us
    pallas_call x1, Pallas kernels, pool(): pl.pallas_call(pool_kernel, out_shape=jax.ShapeDtypeStruct((bags, E), BF)...  3.78 us
    pallas_call x1, Pallas kernels, prepare(): pl.pallas_call(functools.partial(prepare_kernel, halves=halves), out_shap...  3.69 us
  transfers between devices with their start and end apart: 19, of which 13 were waited for; matrix products, arithmetic and copies ran while one was open for 1% of the time, Pallas kernels for 6%

profile of v3, /device:TPU:0, one launch (start us, length us, event | category | flops | bytes accessed | tf_op | source)
XLA Modules:
  0.0 102.3 jit_solution(17200856079146335860)
XLA Ops:
  0.6 3.8 %pool.1 = bf16[4096,128]{1,0:T(8,128)(2,1)} custom-call(s32[1,4608]{1,0:T(1,128)} %bitcast.12, bf16[4608,128]{1,0:T(8,128)(2,1)} %bitcast.15), custom_call_target="tpu_custom_call" | custom-call | tf_op jit(solution)/shard_map/pool/pallas_call | solution.py:77
  4.4 7.5 %all-to-all-start = ((bf16[16,256,128]{2,1,0:T(8,128)(2,1)}), bf16[16,256,128]{2,1,0:T(8,128)(2,1)S(1)}, u32[]{:S(2)}, u32[]{:S(2)}) async-start(bf16[16,256,128]{2,1,0:T(8,128)(2,1)} %bitcast.14), calls=%async_computation | async-start | bytes 2097152 | tf_op jit(solution)/shard_map/all_to_all | solution.py:483
  11.9 1.6 %collective-permute-start.2 = (bf16[2,256,512]{2,1,0:T(8,128)(2,1)S(1)}, bf16[2,256,512]{2,1,0:T(8,128)(2,1)S(1)}, u32[]{:S(2)}, u32[]{:S(2)}) collective-permute-start(bf16[2,256,512]{2,1,0:T(8,128)(2,1)S(1)} %copy-done.4), channel_id=1, source_target_pairs={{0,16},{16,0},{1,17},{17,1},{2,18},{18,2},{3,19},{19,3},{4,20},{20... | collective-permute-start | bytes 1572872 | tf_op jit(solution)/shard_map/ppermute | solution.py:530
  13.5 0.5 collective-permute-start.3
  14.0 1.5 %collective-permute-start.1 = (bf16[2,16,128]{2,1,0:T(8,128)(2,1)S(1)}, bf16[2,16,128]{2,1,0:T(8,128)(2,1)S(1)}, u32[]{:S(2)}, u32[]{:S(2)}) collective-permute-start(bf16[2,16,128]{2,1,0:T(8,128)(2,1)S(1)} %copy-done.8), channel_id=1, source_target_pairs={{0,16},{16,0},{1,17},{17,1},{2,18},{18,2},{3,19},{19,3},{4,20},{20... | collective-permute-start | bytes 24584 | tf_op jit(solution)/shard_map/ppermute | solution.py:530
  16.1 0.6 pad_add_fusion.pos_ref
  16.7 10.1 %collective-permute-done.3.refs_7_ = bf16[2,64]{1,0:T(2,128)(2,1)S(1)} collective-permute-done((bf16[2,64]{1,0:T(2,128)(2,1)S(1)}, bf16[2,64]{1,0:T(2,128)(2,1)S(1)}, u32[]{:S(2)}, u32[]{:S(2)}) %collective-permute-start.3) | collective-permute-done | bytes 288 | tf_op jit(solution)/shard_map/ppermute | solution.py:530
  27.2 0.8 copy-done.5
  28.0 3.7 %prepare.1 = (bf16[2,544,512]{2,1,0:T(8,128)(2,1)}, bf16[2,512,512]{2,1,0:T(8,128)(2,1)}, bf16[2,128,512]{2,1,0:T(8,128)(2,1)}, bf16[2,512,128]{2,1,0:T(8,128)(2...) custom-call(s32[2]{0:T(128)} %pad_add_fusion.pos_ref, ...), custom_call_target="tpu_custom_call" | custom-call | tf_op jit(solution)/shard_map/prepare/pallas_call | solution.py:158
  31.7 3.2 %all-to-all-done.recv_ref = bf16[16,256,128]{2,1,0:T(8,128)(2,1)S(1)} async-done(((bf16[16,256,128]{2,1,0:T(8,128)(2,1)}), bf16[16,256,128]{2,1,0:T(8,128)(2,1)S(1)}, u32[]{:S(2)}, u32[]{:S(2)}) %all-to-all-start) | async-done | bytes 1048608 | tf_op jit(solution)/shard_map/all_to_all | solution.py:483
  34.9 1.0 copy-done.2
  35.8 14.6 %layers.1 = (bf16[8,512,128]{2,1,0:T(8,128)(2,1)}, bf16[16,256,128]{2,1,0:T(8,128)(2,1)}, bf16[16,144,128]{2,1,0:T(8,128)(2,1)}, bf16[16,144,128]{2,1,0:T(8,128)(2,1)}) custom-call(s32[2]{0:T(128)} %pad_add_fusion.pos_ref, f32[2,128]{1,0:T(2,128)} %get-tuple-element.31.gain_ref, bf16[16,256,128]{2,1,0:T(8,128)(2,1)} %copy-done.2, ...), custom_call_target="tpu_custom_call" | custom-call | tf_op jit(solution)/shard_map/layers/pallas_call | solution.py:403
  50.5 7.0 %all-to-all-start.1 = ((bf16[16,256,128]{2,1,0:T(8,128)(2,1)}), bf16[16,256,128]{2,1,0:T(8,128)(2,1)S(1)}, u32[]{:S(2)}, u32[]{:S(2)}) async-start(bf16[16,256,128]{2,1,0:T(8,128)(2,1)} %get-tuple-element.42), calls=%async_computation.1 | async-start | bytes 2097152 | tf_op jit(solution)/shard_map/all_to_all | solution.py:483
  58.0 1.6 %collective-permute-done.4 = bf16[16,144,128]{2,1,0:T(8,128)(2,1)S(1)} collective-permute-done((bf16[16,144,128]{2,1,0:T(8,128)(2,1)S(1)}, bf16[16,144,128]{2,1,0:T(8,128)(2,1)S(1)}, u32[]{:S(2)}, u32[]{:S(2)}) %collective-permute-start.4) | collective-permute-done | bytes 589856 | tf_op jit(solution)/shard_map/ppermute | solution.py:433
  59.8 2.9 %collective-permute-start.7 = (bf16[4,144,128]{2,1,0:T(8,128)(2,1)S(1)}, bf16[4,144,128]{2,1,0:T(8,128)(2,1)S(1)}, u32[]{:S(2)}, u32[]{:S(2)}) collective-permute-start(bf16[4,144,128]{2,1,0:T(8,128)(2,1)S(1)} %get-tuple-element.57), channel_id=1, source_target_pairs={{0,18},{1,19},{2,16},{3,17},{4,22},{5,23},{6,20},{7,21},{8,26},{9,... | collective-permute-start | bytes 442376 | tf_op jit(solution)/shard_map/ppermute | solution.py:433
  62.8 0.5 collective-permute-start.5
  63.3 10.3 %collective-permute-done.7 = bf16[4,144,128]{2,1,0:T(8,128)(2,1)S(1)} collective-permute-done((bf16[4,144,128]{2,1,0:T(8,128)(2,1)S(1)}, bf16[4,144,128]{2,1,0:T(8,128)(2,1)S(1)}, u32[]{:S(2)}, u32[]{:S(2)}) %collective-permute-start.7) | collective-permute-done | bytes 147488 | tf_op jit(solution)/shard_map/ppermute | solution.py:433
  73.6 2.4 %collective-permute-done.6 = bf16[4,144,128]{2,1,0:T(8,128)(2,1)S(1)} collective-permute-done((bf16[4,144,128]{2,1,0:T(8,128)(2,1)S(1)}, bf16[4,144,128]{2,1,0:T(8,128)(2,1)S(1)}, u32[]{:S(2)}, u32[]{:S(2)}) %collective-permute-start.6) | collective-permute-done | bytes 147488 | tf_op jit(solution)/shard_map/ppermute | solution.py:433
  76.1 0.9 collective-permute-start.8
  77.0 3.3 %collective-permute-start.10 = (bf16[1,144,128]{2,1,0:T(8,128)(2,1)S(1)}, bf16[1,144,128]{2,1,0:T(8,128)(2,1)S(1)}, u32[]{:S(2)}, u32[]{:S(2)}) collective-permute-start(bf16[1,144,128]{2,1,0:T(8,128)(2,1)S(1)} %get-tuple-element.61), channel_id=1, source_target_pairs={{0,12},{1,13},{2,14},{3,15},{4,8},{5,9},{6,10},{7,11},{8,4},{9,5},... | collective-permute-start | bytes 110600 | tf_op jit(solution)/shard_map/ppermute | solution.py:433
  80.7 1.5 %collective-permute-done.8 = bf16[1,144,128]{2,1,0:T(8,128)(2,1)S(1)} collective-permute-done((bf16[1,144,128]{2,1,0:T(8,128)(2,1)S(1)}, bf16[1,144,128]{2,1,0:T(8,128)(2,1)S(1)}, u32[]{:S(2)}, u32[]{:S(2)}) %collective-permute-start.8) | collective-permute-done | bytes 36896 | tf_op jit(solution)/shard_map/ppermute | solution.py:433
  82.2 0.6 collective-permute-done.10
  82.9 4.4 %collective-permute-done.9 = bf16[1,144,128]{2,1,0:T(8,128)(2,1)S(1)} collective-permute-done((bf16[1,144,128]{2,1,0:T(8,128)(2,1)S(1)}, bf16[1,144,128]{2,1,0:T(8,128)(2,1)S(1)}, u32[]{:S(2)}, u32[]{:S(2)}) %collective-permute-start.9) | collective-permute-done | bytes 36896 | tf_op jit(solution)/shard_map/ppermute | solution.py:433
  87.3 1.5 %collective-permute-start.13 = (bf16[1,144,128]{2,1,0:T(8,128)(2,1)S(1)}, bf16[1,144,128]{2,1,0:T(8,128)(2,1)S(1)}, u32[]{:S(2)}, u32[]{:S(2)}) collective-permute-start(bf16[1,144,128]{2,1,0:T(8,128)(2,1)S(1)} %add_convert_fusion.4), channel_id=1, source_target_pairs={{0,12},{1,13},{2,14},{3,15},{4,8},{5,9},{6,10},{7,11},{8,4},{9,5},... | collective-permute-start | bytes 110600 | tf_op jit(solution)/shard_map/ppermute | solution.py:433
  89.0 2.8 %collective-permute-start.11 = (bf16[1,144,128]{2,1,0:T(8,128)(2,1)S(1)}, bf16[1,144,128]{2,1,0:T(8,128)(2,1)S(1)}, u32[]{:S(2)}, u32[]{:S(2)}) collective-permute-start(bf16[1,144,128]{2,1,0:T(8,128)(2,1)S(1)} %add_convert_fusion.4), channel_id=1, source_target_pairs={{0,4},{1,5},{2,6},{3,7},{4,0},{5,1},{6,2},{7,3},{8,12},{9,13},{10,... | collective-permute-start | bytes 110600 | tf_op jit(solution)/shard_map/ppermute | solution.py:433
  91.7 1.6 %collective-permute-done.13 = bf16[1,144,128]{2,1,0:T(8,128)(2,1)S(1)} collective-permute-done((bf16[1,144,128]{2,1,0:T(8,128)(2,1)S(1)}, bf16[1,144,128]{2,1,0:T(8,128)(2,1)S(1)}, u32[]{:S(2)}, u32[]{:S(2)}) %collective-permute-start.13) | collective-permute-done | bytes 36896 | tf_op jit(solution)/shard_map/ppermute | solution.py:433
  93.3 0.8 collective-permute-done.12
  94.1 1.5 %collective-permute-start.14 = (bf16[4,144,128]{2,1,0:T(8,128)(2,1)S(1)}, bf16[4,144,128]{2,1,0:T(8,128)(2,1)S(1)}, u32[]{:S(2)}, u32[]{:S(2)}) collective-permute-start(bf16[4,144,128]{2,1,0:T(8,128)(2,1)S(1)} %pad_maximum_fusion.refs_0_), channel_id=1, source_target_pairs={{0,2},{1,3},{2,0},{3,1},{4,6},{5,7},{6,4},{7,5},{8,10},{9,11},{10,... | collective-permute-start | bytes 442376 | tf_op jit(solution)/shard_map/ppermute | solution.py:433
  95.7 2.7 %expand.1 = bf16[4608,128]{1,0:T(8,128)(2,1)} custom-call(s32[1,4608]{1,0:T(1,128)S(1)} %bitcast.13, bf16[4096,128]{1,0:T(8,128)(2,1)S(1)} %bitcast.11), custom_call_target="tpu_custom_call" | custom-call | tf_op jit(solution)/shard_map/expand/pallas_call | solution.py:101
  98.4 1.0 collective-permute-done.14.refs_1_
  99.4 1.4 %collective-permute-done.16.refs_3_ = bf16[4,144,128]{2,1,0:T(8,128)(2,1)S(1)} collective-permute-done((bf16[4,144,128]{2,1,0:T(8,128)(2,1)S(1)}, bf16[4,144,128]{2,1,0:T(8,128)(2,1)S(1)}, u32[]{:S(2)}, u32[]{:S(2)}) %collective-permute-start.16) | collective-permute-done | bytes 147488 | tf_op jit(solution)/shard_map/ppermute | solution.py:433
  100.7 1.6 %finish.1 = (f32[2,256,512]{2,1,0:T(8,128)}, f32[2,32,256]{2,1,0:T(8,128)}, f32[2,16,128]{2,1,0:T(8,128)}, f32[2,64]{1,0:T(2,128)}) custom-call(s32[2]{0:T(128)S(1)} %copy-done.1, bf16[4,144,128]{2,1,0:T(8,128)(2,1)S(1)} %pad_maximum_fusion.refs_0_, bf16[4,144,128]{2,1,0:T(8,128)(2,1)S(1)} %collective-permute-done.14.refs_1_, ...), custom_call_target="tpu_custom_call" | custom-call | tf_op jit(solution)/shard_map/finish/pallas_call | solution.py:466
  (42 shorter events, 2.5 us)
Async XLA Ops:
  4.4 7.5 %copy-start.4 = (bf16[2,256,512]{2,1,0:T(8,128)(2,1)S(1)}, bf16[2,256,512]{2,1,0:T(8,128)(2,1)}, u32[]{:S(2)}) copy-start(bf16[2,256,512]{2,1,0:T(8,128)(2,1)} %refs_4_.1) | copy-start | bytes 1572868
  4.4 9.1 %copy-start.10 = (bf16[2,64]{1,0:T(2,128)(2,1)S(1)}, bf16[2,64]{1,0:T(2,128)(2,1)}, u32[]{:S(2)}) copy-start(bf16[2,64]{1,0:T(2,128)(2,1)} %refs_6_.1) | copy-start | bytes 772
  4.4 9.6 %copy-start.8 = (bf16[2,16,128]{2,1,0:T(8,128)(2,1)S(1)}, bf16[2,16,128]{2,1,0:T(8,128)(2,1)}, u32[]{:S(2)}) copy-start(bf16[2,16,128]{2,1,0:T(8,128)(2,1)} %refs_2_.1) | copy-start | bytes 24580
  4.4 11.2 %copy-start.6 = (bf16[2,256,32]{1,2,0:T(8,128)(2,1)S(1)}, bf16[2,256,32]{1,2,0:T(8,128)(2,1)}, u32[]{:S(2)}) copy-start(bf16[2,256,32]{1,2,0:T(8,128)(2,1)} %param.13) | copy-start | bytes 98308
  4.4 30.5 %all-to-all-start = ((bf16[16,256,128]{2,1,0:T(8,128)(2,1)}), bf16[16,256,128]{2,1,0:T(8,128)(2,1)S(1)}, u32[]{:S(2)}, u32[]{:S(2)}) async-start(bf16[16,256,128]{2,1,0:T(8,128)(2,1)} %bitcast.14), calls=%async_computation | async-start | bytes 2097152 | tf_op jit(solution)/shard_map/all_to_all | solution.py:483
  11.9 15.2 %collective-permute-start.2 = (bf16[2,256,512]{2,1,0:T(8,128)(2,1)S(1)}, bf16[2,256,512]{2,1,0:T(8,128)(2,1)S(1)}, u32[]{:S(2)}, u32[]{:S(2)}) collective-permute-start(bf16[2,256,512]{2,1,0:T(8,128)(2,1)S(1)} %copy-done.4), channel_id=1, source_target_pairs={{0,16},{16,0},{1,17},{17,1},{2,18},{18,2},{3,19},{19,3},{4,20},{20... | collective-permute-start | bytes 1572872 | tf_op jit(solution)/shard_map/ppermute | solution.py:530
  13.5 13.2 %collective-permute-start.3 = (bf16[2,64]{1,0:T(2,128)(2,1)S(1)}, bf16[2,64]{1,0:T(2,128)(2,1)S(1)}, u32[]{:S(2)}, u32[]{:S(2)}) collective-permute-start(bf16[2,64]{1,0:T(2,128)(2,1)S(1)} %copy-done.10), channel_id=1, source_target_pairs={{0,16},{16,0},{1,17},{17,1},{2,18},{18,2},{3,19},{19,3},{4,20},{20... | collective-permute-start | bytes 776 | tf_op jit(solution)/shard_map/ppermute | solution.py:530
  14.0 12.8 %collective-permute-start.1 = (bf16[2,16,128]{2,1,0:T(8,128)(2,1)S(1)}, bf16[2,16,128]{2,1,0:T(8,128)(2,1)S(1)}, u32[]{:S(2)}, u32[]{:S(2)}) collective-permute-start(bf16[2,16,128]{2,1,0:T(8,128)(2,1)S(1)} %copy-done.8), channel_id=1, source_target_pairs={{0,16},{16,0},{1,17},{17,1},{2,18},{18,2},{3,19},{19,3},{4,20},{20... | collective-permute-start | bytes 24584 | tf_op jit(solution)/shard_map/ppermute | solution.py:530
  15.6 11.6 %collective-permute-start = (bf16[2,32,256]{2,1,0:T(8,128)(2,1)S(1)}, bf16[2,32,256]{2,1,0:T(8,128)(2,1)S(1)}, u32[]{:S(2)}, u32[]{:S(2)}) collective-permute-start(bf16[2,32,256]{2,1,0:T(8,128)(2,1)S(1)} %bitcast.18), channel_id=1, source_target_pairs={{0,16},{16,0},{1,17},{17,1},{2,18},{18,2},{3,19},{19,3},{4,20},{20... | collective-permute-start | bytes 98312 | tf_op jit(solution)/shard_map/ppermute | solution.py:530
  26.8 1.2 %copy-start.11 = (bf16[2,64]{1,0:T(2,128)(2,1)}, bf16[2,64]{1,0:T(2,128)(2,1)S(1)}, u32[]{:S(2)}) copy-start(bf16[2,64]{1,0:T(2,128)(2,1)S(1)} %collective-permute-done.3.refs_7_) | copy-start | bytes 772
  26.8 1.2 %copy-start.9 = (bf16[2,16,128]{2,1,0:T(8,128)(2,1)}, bf16[2,16,128]{2,1,0:T(8,128)(2,1)S(1)}, u32[]{:S(2)}) copy-start(bf16[2,16,128]{2,1,0:T(8,128)(2,1)S(1)} %collective-permute-done.1.refs_3_) | copy-start | bytes 24580
  27.2 0.8 copy-start.7
  27.2 0.8 copy-start.5
  34.9 1.0 copy-start.2
  50.4 7.0 %copy-start.12 = (bf16[16,144,128]{2,1,0:T(8,128)(2,1)S(1)}, bf16[16,144,128]{2,1,0:T(8,128)(2,1)}, u32[]{:S(2)}) copy-start(bf16[16,144,128]{2,1,0:T(8,128)(2,1)} %get-tuple-element.41) | copy-start | bytes 1769476
  50.5 9.1 %copy-start.3 = (bf16[16,144,128]{2,1,0:T(8,128)(2,1)S(1)}, bf16[16,144,128]{2,1,0:T(8,128)(2,1)}, u32[]{:S(2)}) copy-start(bf16[16,144,128]{2,1,0:T(8,128)(2,1)} %get-tuple-element.40) | copy-start | bytes 1769476
  50.5 43.7 %all-to-all-start.1 = ((bf16[16,256,128]{2,1,0:T(8,128)(2,1)}), bf16[16,256,128]{2,1,0:T(8,128)(2,1)S(1)}, u32[]{:S(2)}, u32[]{:S(2)}) async-start(bf16[16,256,128]{2,1,0:T(8,128)(2,1)} %get-tuple-element.42), calls=%async_computation.1 | async-start | bytes 2097152 | tf_op jit(solution)/shard_map/all_to_all | solution.py:483
  57.5 2.1 %collective-permute-start.4 = (bf16[16,144,128]{2,1,0:T(8,128)(2,1)S(1)}, bf16[16,144,128]{2,1,0:T(8,128)(2,1)S(1)}, u32[]{:S(2)}, u32[]{:S(2)}) collective-permute-start(bf16[16,144,128]{2,1,0:T(8,128)(2,1)S(1)} %copy-done.12), channel_id=1, source_target_pairs={{0,1},{1,0},{2,3},{3,2},{4,5},{5,4},{6,7},{7,6},{8,9},{9,8},{10,11... | collective-permute-start | bytes 1769480 | tf_op jit(solution)/shard_map/ppermute | solution.py:433
  59.6 36.1 %copy-start = (s32[1,1,4608]{2,1,0:T(1,128)S(1)}, s32[1,1,4608]{2,1,0:T(1,128)}, u32[]{:S(2)}) copy-start(s32[1,1,4608]{2,1,0:T(1,128)} %param.10) | copy-start | bytes 55300
  59.8 13.9 %collective-permute-start.7 = (bf16[4,144,128]{2,1,0:T(8,128)(2,1)S(1)}, bf16[4,144,128]{2,1,0:T(8,128)(2,1)S(1)}, u32[]{:S(2)}, u32[]{:S(2)}) collective-permute-start(bf16[4,144,128]{2,1,0:T(8,128)(2,1)S(1)} %get-tuple-element.57), channel_id=1, source_target_pairs={{0,18},{1,19},{2,16},{3,17},{4,22},{5,23},{6,20},{7,21},{8,26},{9,... | collective-permute-start | bytes 442376 | tf_op jit(solution)/shard_map/ppermute | solution.py:433
  62.7 13.3 %collective-permute-start.6 = (bf16[4,144,128]{2,1,0:T(8,128)(2,1)S(1)}, bf16[4,144,128]{2,1,0:T(8,128)(2,1)S(1)}, u32[]{:S(2)}, u32[]{:S(2)}) collective-permute-start(bf16[4,144,128]{2,1,0:T(8,128)(2,1)S(1)} %get-tuple-element.58), channel_id=1, source_target_pairs={{0,2},{1,3},{2,0},{3,1},{4,6},{5,7},{6,4},{7,5},{8,10},{9,11},{10,... | collective-permute-start | bytes 442376 | tf_op jit(solution)/shard_map/ppermute | solution.py:433
  62.8 13.2 %collective-permute-start.5 = (bf16[4,144,128]{2,1,0:T(8,128)(2,1)S(1)}, bf16[4,144,128]{2,1,0:T(8,128)(2,1)S(1)}, u32[]{:S(2)}, u32[]{:S(2)}) collective-permute-start(bf16[4,144,128]{2,1,0:T(8,128)(2,1)S(1)} %get-tuple-element.59), channel_id=1, source_target_pairs={{0,16},{1,17},{2,18},{3,19},{4,20},{5,21},{6,22},{7,23},{8,24},{9,... | collective-permute-start | bytes 442376 | tf_op jit(solution)/shard_map/ppermute | solution.py:433
  76.1 6.1 %collective-permute-start.8 = (bf16[1,144,128]{2,1,0:T(8,128)(2,1)S(1)}, bf16[1,144,128]{2,1,0:T(8,128)(2,1)S(1)}, u32[]{:S(2)}, u32[]{:S(2)}) collective-permute-start(bf16[1,144,128]{2,1,0:T(8,128)(2,1)S(1)} %get-tuple-element.60), channel_id=1, source_target_pairs={{0,4},{1,5},{2,6},{3,7},{4,0},{5,1},{6,2},{7,3},{8,12},{9,13},{10,... | collective-permute-start | bytes 110600 | tf_op jit(solution)/shard_map/ppermute | solution.py:433
  77.0 5.9 %collective-permute-start.10 = (bf16[1,144,128]{2,1,0:T(8,128)(2,1)S(1)}, bf16[1,144,128]{2,1,0:T(8,128)(2,1)S(1)}, u32[]{:S(2)}, u32[]{:S(2)}) collective-permute-start(bf16[1,144,128]{2,1,0:T(8,128)(2,1)S(1)} %get-tuple-element.61), channel_id=1, source_target_pairs={{0,12},{1,13},{2,14},{3,15},{4,8},{5,9},{6,10},{7,11},{8,4},{9,5},... | collective-permute-start | bytes 110600 | tf_op jit(solution)/shard_map/ppermute | solution.py:433
  80.2 7.0 %collective-permute-start.9 = (bf16[1,144,128]{2,1,0:T(8,128)(2,1)S(1)}, bf16[1,144,128]{2,1,0:T(8,128)(2,1)S(1)}, u32[]{:S(2)}, u32[]{:S(2)}) collective-permute-start(bf16[1,144,128]{2,1,0:T(8,128)(2,1)S(1)} %get-tuple-element.62), channel_id=1, source_target_pairs={{0,8},{1,9},{2,10},{3,11},{4,12},{5,13},{6,14},{7,15},{8,0},{9,1},... | collective-permute-start | bytes 110600 | tf_op jit(solution)/shard_map/ppermute | solution.py:433
  87.3 6.0 %collective-permute-start.13 = (bf16[1,144,128]{2,1,0:T(8,128)(2,1)S(1)}, bf16[1,144,128]{2,1,0:T(8,128)(2,1)S(1)}, u32[]{:S(2)}, u32[]{:S(2)}) collective-permute-start(bf16[1,144,128]{2,1,0:T(8,128)(2,1)S(1)} %add_convert_fusion.4), channel_id=1, source_target_pairs={{0,12},{1,13},{2,14},{3,15},{4,8},{5,9},{6,10},{7,11},{8,4},{9,5},... | collective-permute-start | bytes 110600 | tf_op jit(solution)/shard_map/ppermute | solution.py:433
  88.8 5.3 %collective-permute-start.12 = (bf16[1,144,128]{2,1,0:T(8,128)(2,1)S(1)}, bf16[1,144,128]{2,1,0:T(8,128)(2,1)S(1)}, u32[]{:S(2)}, u32[]{:S(2)}) collective-permute-start(bf16[1,144,128]{2,1,0:T(8,128)(2,1)S(1)} %add_convert_fusion.4), channel_id=1, source_target_pairs={{0,8},{1,9},{2,10},{3,11},{4,12},{5,13},{6,14},{7,15},{8,0},{9,1},... | collective-permute-start | bytes 110600 | tf_op jit(solution)/shard_map/ppermute | solution.py:433
  89.0 5.1 %collective-permute-start.11 = (bf16[1,144,128]{2,1,0:T(8,128)(2,1)S(1)}, bf16[1,144,128]{2,1,0:T(8,128)(2,1)S(1)}, u32[]{:S(2)}, u32[]{:S(2)}) collective-permute-start(bf16[1,144,128]{2,1,0:T(8,128)(2,1)S(1)} %add_convert_fusion.4), channel_id=1, source_target_pairs={{0,4},{1,5},{2,6},{3,7},{4,0},{5,1},{6,2},{7,3},{8,12},{9,13},{10,... | collective-permute-start | bytes 110600 | tf_op jit(solution)/shard_map/ppermute | solution.py:433
  94.1 6.6 %copy-start.1 = (s32[2]{0:T(128)S(1)}, s32[2]{0:T(128)}, u32[]{:S(2)}) copy-start(s32[2]{0:T(128)} %pad_add_fusion.pos_ref) | copy-start | bytes 28
  94.1 5.2 %collective-permute-start.14 = (bf16[4,144,128]{2,1,0:T(8,128)(2,1)S(1)}, bf16[4,144,128]{2,1,0:T(8,128)(2,1)S(1)}, u32[]{:S(2)}, u32[]{:S(2)}) collective-permute-start(bf16[4,144,128]{2,1,0:T(8,128)(2,1)S(1)} %pad_maximum_fusion.refs_0_), channel_id=1, source_target_pairs={{0,2},{1,3},{2,0},{3,1},{4,6},{5,7},{6,4},{7,5},{8,10},{9,11},{10,... | collective-permute-start | bytes 442376 | tf_op jit(solution)/shard_map/ppermute | solution.py:433
  95.7 3.7 %collective-permute-start.15 = (bf16[4,144,128]{2,1,0:T(8,128)(2,1)S(1)}, bf16[4,144,128]{2,1,0:T(8,128)(2,1)S(1)}, u32[]{:S(2)}, u32[]{:S(2)}) collective-permute-start(bf16[4,144,128]{2,1,0:T(8,128)(2,1)S(1)} %pad_maximum_fusion.refs_0_), channel_id=1, source_target_pairs={{0,1},{1,0},{2,3},{3,2},{4,5},{5,4},{6,7},{7,6},{8,9},{9,8},{10,11... | collective-permute-start | bytes 442376 | tf_op jit(solution)/shard_map/ppermute | solution.py:433
  99.4 1.4 %collective-permute-start.16 = (bf16[4,144,128]{2,1,0:T(8,128)(2,1)S(1)}, bf16[4,144,128]{2,1,0:T(8,128)(2,1)S(1)}, u32[]{:S(2)}, u32[]{:S(2)}) collective-permute-start(bf16[4,144,128]{2,1,0:T(8,128)(2,1)S(1)} %collective-permute-done.14.refs_1_), channel_id=1, source_target_pairs={{0,1},{1,0},{2,3},{3,2},{4,5},{5,4},{6,7},{7,6},{8,9},{9,8},{10,11... | collective-permute-start | bytes 442376 | tf_op jit(solution)/shard_map/ppermute | solution.py:433

commit v4 on v3

--- a/solution.py
+++ b/solution.py
@@ -18,14 +18,14 @@
 CHUNK = 128
 EPS = 1e-05
 MIB = 1024 * 1024
-WHOLE, PART = 62, 46
+FULL, WHOLE, PART = 63.5, 58, 46
 PIECE = 144
 BF = jnp.bfloat16
 F32 = jnp.float32
 
 
 def params(mib):
-    return pltpu.CompilerParams(vmem_limit_bytes=mib * MIB)
+    return pltpu.CompilerParams(vmem_limit_bytes=int(mib * MIB))
 
 
 def dot(left, right):
@@ -169,7 +169,7 @@
         ),
         in_specs=[pl.BlockSpec(memory_space=pltpu.SMEM)] + [VMEM] * (2 + len(flat)),
         out_specs=(VMEM,) * 8,
-        compiler_params=params(WHOLE),
+        compiler_params=params(FULL),
         name="prepare",
     )(pos, slot_feature.reshape(1, F), block_exponent.T, *flat)
 
@@ -184,14 +184,14 @@
 CONSTANTS = ("perm", "scale", "left", "diag", "back", "project", "unperm")
 
 
-def layers_kernel(pos_ref, gain_ref, recv_ref, cot_hbm, *refs, f_dev, packed):
+def layers_kernel(pos_ref, gain_ref, recv_hbm, cot_hbm, *refs, f_dev, packed):
     sources, refs = dict(zip(CONSTANTS, refs)), refs[len(CONSTANTS) :]
     feats_hbm, slots_hbm = refs[:2]
     grads = 2 if packed else 4
     grad_outs, refs = refs[2 : 2 + grads], refs[2 + grads :]
     held, refs = dict(zip(CONSTANTS, refs)), refs[len(CONSTANTS) :]
-    cot_ref, feats_ref, slots_ref = refs[:3]
-    grad_refs, refs = refs[3 : 3 + grads], refs[3 + grads :]
+    recv_ref, cot_ref, feats_ref, slots_ref = refs[:4]
+    grad_refs, refs = refs[4 : 4 + grads], refs[4 + grads :]
     xs, ts, normed_s, inv_s, grad_s, next_s, wacc, gacc, dm, pj, ex, sems = refs
     left_ref, back_ref, diag_ref = held["left"], held["back"], held["diag"]
     project_ref, scale_ref = held["project"], held["scale"]
@@ -203,6 +203,7 @@
     def fetch(name):
         copies.start(name, sources[name], held[name])
 
+    copies.start("recv", recv_hbm, recv_ref)
     for name in ("perm", "scale", "left", "diag"):
         fetch(name)
     copies.start("cot", cot_hbm, cot_ref)
@@ -354,7 +355,7 @@
     phases = 4 * LAYERS + 2
     for tick in range(phases):
         if tick == 0:
-            copies.wait("perm", "scale")
+            copies.wait("recv", "perm", "scale")
         if tick == 1:
             copies.wait("left", "diag")
         if tick == 2 * LAYERS + 1:
@@ -399,15 +400,15 @@
     def scratch(x):
         return pltpu.VMEM(x.shape, x.dtype)
 
-    copies = len(constants) + 3 + len(grads)
+    copies = len(constants) + 4 + len(grads)
     return pl.pallas_call(
         functools.partial(layers_kernel, f_dev=f_dev, packed=packed),
         out_shape=outs,
-        in_specs=[pl.BlockSpec(memory_space=pltpu.SMEM), VMEM, VMEM]
-        + [HBM] * (1 + len(constants)),
+        in_specs=[pl.BlockSpec(memory_space=pltpu.SMEM), VMEM]
+        + [HBM] * (2 + len(constants)),
         out_specs=[HBM] * len(outs),
         scratch_shapes=[scratch(x) for x in constants]
-        + [scratch(cotangent)]
+        + [scratch(recv), scratch(cotangent)]
         + [scratch(x) for x in outs]
         + [
             pltpu.VMEM((LAYERS, F, width), BF),
@@ -423,7 +424,7 @@
             pltpu.VMEM((2, 16, 8, E), F32),
             pltpu.SemaphoreType.DMA((copies,)),
         ],
-        compiler_params=params(58),
+        compiler_params=params(WHOLE),
         name="layers",
     )(pos, gain, recv, cotangent, *constants)
 

time: 103 us -> 102 us (level)
  no operation moved by 1% of the time
where the time goes in v4:
time: 102 us; the launch traced here: 101 us
  waiting for transfers between devices  39.3 us (39%)
  starting transfers between devices  33.4 us (33%)
  Pallas kernels  26.1 us (26%)
    ppermute x13, waiting for transfers between devices, across(): return lax.ppermute(x, ('dp', 'mp'), pairs)  25.5 us
    ppermute x13, starting transfers between devices, across(): return lax.ppermute(x, ('dp', 'mp'), pairs)  14.7 us
    all_to_all x2, starting transfers between devices, exchange(): return lax.all_to_all(x, 'mp', split_axis=0, concat_axis=0, tiled=True)  14.6 us
    pallas_call x1, Pallas kernels, run_layers(): pl.pallas_call(functools.partial(layers_kernel, f_dev=f_dev, packed=packe...  14.4 us
    ppermute x4, waiting for transfers between devices, per_device(): lax.ppermute(part, 'dp', [(0, 1), (1, 0)])  10.4 us
    ppermute x4, starting transfers between devices, per_device(): lax.ppermute(part, 'dp', [(0, 1), (1, 0)])  4.12 us
    pallas_call x1, Pallas kernels, pool(): pl.pallas_call(pool_kernel, out_shape=jax.ShapeDtypeStruct((bags, E), BF)...  3.78 us
    pallas_call x1, Pallas kernels, prepare(): pl.pallas_call(functools.partial(prepare_kernel, halves=halves), out_shap...  3.68 us
  transfers between devices with their start and end apart: 19, of which 13 were waited for; matrix products, arithmetic and copies ran while one was open for 1% of the time, Pallas kernels for 6%

profile of v4, /device:TPU:0, one launch (start us, length us, event | category | flops | bytes accessed | tf_op | source)
XLA Modules:
  0.0 101.3 jit_solution(3059857885894428292)
XLA Ops:
  0.6 3.8 %pool.1 = bf16[4096,128]{1,0:T(8,128)(2,1)} custom-call(s32[1,4608]{1,0:T(1,128)} %bitcast.12, bf16[4608,128]{1,0:T(8,128)(2,1)} %bitcast.15), custom_call_target="tpu_custom_call" | custom-call | tf_op jit(solution)/shard_map/pool/pallas_call | solution.py:77
  4.4 7.6 %all-to-all-start = ((bf16[16,256,128]{2,1,0:T(8,128)(2,1)}), bf16[16,256,128]{2,1,0:T(8,128)(2,1)}, u32[]{:S(2)}, u32[]{:S(2)}) async-start(bf16[16,256,128]{2,1,0:T(8,128)(2,1)} %bitcast.14), calls=%async_computation | async-start | bytes 2097152 | tf_op jit(solution)/shard_map/all_to_all | solution.py:484
  12.0 1.6 %collective-permute-start.2 = (bf16[2,256,512]{2,1,0:T(8,128)(2,1)S(1)}, bf16[2,256,512]{2,1,0:T(8,128)(2,1)S(1)}, u32[]{:S(2)}, u32[]{:S(2)}) collective-permute-start(bf16[2,256,512]{2,1,0:T(8,128)(2,1)S(1)} %copy-done.3), channel_id=1, source_target_pairs={{0,16},{16,0},{1,17},{17,1},{2,18},{18,2},{3,19},{19,3},{4,20},{20... | collective-permute-start | bytes 1572872 | tf_op jit(solution)/shard_map/ppermute | solution.py:531
  13.6 0.5 collective-permute-start.3
  14.1 1.5 %collective-permute-start.1 = (bf16[2,16,128]{2,1,0:T(8,128)(2,1)S(1)}, bf16[2,16,128]{2,1,0:T(8,128)(2,1)S(1)}, u32[]{:S(2)}, u32[]{:S(2)}) collective-permute-start(bf16[2,16,128]{2,1,0:T(8,128)(2,1)S(1)} %copy-done.7), channel_id=1, source_target_pairs={{0,16},{16,0},{1,17},{17,1},{2,18},{18,2},{3,19},{19,3},{4,20},{20... | collective-permute-start | bytes 24584 | tf_op jit(solution)/shard_map/ppermute | solution.py:531
  15.6 0.5 collective-permute-start
  16.1 0.6 pad_add_fusion.pos_ref
  16.7 10.0 %collective-permute-done.3.refs_7_ = bf16[2,64]{1,0:T(2,128)(2,1)S(1)} collective-permute-done((bf16[2,64]{1,0:T(2,128)(2,1)S(1)}, bf16[2,64]{1,0:T(2,128)(2,1)S(1)}, u32[]{:S(2)}, u32[]{:S(2)}) %collective-permute-start.3) | collective-permute-done | bytes 288 | tf_op jit(solution)/shard_map/ppermute | solution.py:531
  27.1 0.8 copy-done.4
  27.9 3.7 %prepare.1 = (bf16[2,544,512]{2,1,0:T(8,128)(2,1)}, bf16[2,512,512]{2,1,0:T(8,128)(2,1)}, bf16[2,128,512]{2,1,0:T(8,128)(2,1)}, bf16[2,512,128]{2,1,0:T(8,128)(2...) custom-call(s32[2]{0:T(128)} %pad_add_fusion.pos_ref, ...), custom_call_target="tpu_custom_call" | custom-call | tf_op jit(solution)/shard_map/prepare/pallas_call | solution.py:158
  31.6 3.4 %all-to-all-done.recv_hbm = bf16[16,256,128]{2,1,0:T(8,128)(2,1)} async-done(((bf16[16,256,128]{2,1,0:T(8,128)(2,1)}), bf16[16,256,128]{2,1,0:T(8,128)(2,1)}, u32[]{:S(2)}, u32[]{:S(2)}) %all-to-all-start) | async-done | bytes 1048608 | tf_op jit(solution)/shard_map/all_to_all | solution.py:484
  35.0 14.4 %layers.1 = (bf16[8,512,128]{2,1,0:T(8,128)(2,1)}, bf16[16,256,128]{2,1,0:T(8,128)(2,1)}, bf16[16,144,128]{2,1,0:T(8,128)(2,1)}, bf16[16,144,128]{2,1,0:T(8,128)(2,1)}) custom-call(s32[2]{0:T(128)} %pad_add_fusion.pos_ref, f32[2,128]{1,0:T(2,128)} %get-tuple-element.31.gain_ref, bf16[16,256,128]{2,1,0:T(8,128)(2,1)} %all-to-all-done.recv_hbm, ...), custom_call_target="tpu_custom_call" | custom-call | tf_op jit(solution)/shard_map/layers/pallas_call | solution.py:404
  49.4 7.0 %all-to-all-start.1 = ((bf16[16,256,128]{2,1,0:T(8,128)(2,1)}), bf16[16,256,128]{2,1,0:T(8,128)(2,1)S(1)}, u32[]{:S(2)}, u32[]{:S(2)}) async-start(bf16[16,256,128]{2,1,0:T(8,128)(2,1)} %get-tuple-element.42), calls=%async_computation.1 | async-start | bytes 2097152 | tf_op jit(solution)/shard_map/all_to_all | solution.py:484
  56.9 1.6 %collective-permute-done.4 = bf16[16,144,128]{2,1,0:T(8,128)(2,1)S(1)} collective-permute-done((bf16[16,144,128]{2,1,0:T(8,128)(2,1)S(1)}, bf16[16,144,128]{2,1,0:T(8,128)(2,1)S(1)}, u32[]{:S(2)}, u32[]{:S(2)}) %collective-permute-start.4) | collective-permute-done | bytes 589856 | tf_op jit(solution)/shard_map/ppermute | solution.py:434
  58.7 2.9 %collective-permute-start.7 = (bf16[4,144,128]{2,1,0:T(8,128)(2,1)S(1)}, bf16[4,144,128]{2,1,0:T(8,128)(2,1)S(1)}, u32[]{:S(2)}, u32[]{:S(2)}) collective-permute-start(bf16[4,144,128]{2,1,0:T(8,128)(2,1)S(1)} %get-tuple-element.57), channel_id=1, source_target_pairs={{0,18},{1,19},{2,16},{3,17},{4,22},{5,23},{6,20},{7,21},{8,26},{9,... | collective-permute-start | bytes 442376 | tf_op jit(solution)/shard_map/ppermute | solution.py:434
  61.7 0.5 collective-permute-start.5
  62.2 10.3 %collective-permute-done.7 = bf16[4,144,128]{2,1,0:T(8,128)(2,1)S(1)} collective-permute-done((bf16[4,144,128]{2,1,0:T(8,128)(2,1)S(1)}, bf16[4,144,128]{2,1,0:T(8,128)(2,1)S(1)}, u32[]{:S(2)}, u32[]{:S(2)}) %collective-permute-start.7) | collective-permute-done | bytes 147488 | tf_op jit(solution)/shard_map/ppermute | solution.py:434
  72.5 2.4 %collective-permute-done.6 = bf16[4,144,128]{2,1,0:T(8,128)(2,1)S(1)} collective-permute-done((bf16[4,144,128]{2,1,0:T(8,128)(2,1)S(1)}, bf16[4,144,128]{2,1,0:T(8,128)(2,1)S(1)}, u32[]{:S(2)}, u32[]{:S(2)}) %collective-permute-start.6) | collective-permute-done | bytes 147488 | tf_op jit(solution)/shard_map/ppermute | solution.py:434
  75.0 0.9 collective-permute-start.8
  75.9 3.3 %collective-permute-start.10 = (bf16[1,144,128]{2,1,0:T(8,128)(2,1)S(1)}, bf16[1,144,128]{2,1,0:T(8,128)(2,1)S(1)}, u32[]{:S(2)}, u32[]{:S(2)}) collective-permute-start(bf16[1,144,128]{2,1,0:T(8,128)(2,1)S(1)} %get-tuple-element.61), channel_id=1, source_target_pairs={{0,12},{1,13},{2,14},{3,15},{4,8},{5,9},{6,10},{7,11},{8,4},{9,5},... | collective-permute-start | bytes 110600 | tf_op jit(solution)/shard_map/ppermute | solution.py:434
  79.6 1.5 %collective-permute-done.8 = bf16[1,144,128]{2,1,0:T(8,128)(2,1)S(1)} collective-permute-done((bf16[1,144,128]{2,1,0:T(8,128)(2,1)S(1)}, bf16[1,144,128]{2,1,0:T(8,128)(2,1)S(1)}, u32[]{:S(2)}, u32[]{:S(2)}) %collective-permute-start.8) | collective-permute-done | bytes 36896 | tf_op jit(solution)/shard_map/ppermute | solution.py:434
  81.1 0.6 collective-permute-done.10
  81.8 4.4 %collective-permute-done.9 = bf16[1,144,128]{2,1,0:T(8,128)(2,1)S(1)} collective-permute-done((bf16[1,144,128]{2,1,0:T(8,128)(2,1)S(1)}, bf16[1,144,128]{2,1,0:T(8,128)(2,1)S(1)}, u32[]{:S(2)}, u32[]{:S(2)}) %collective-permute-start.9) | collective-permute-done | bytes 36896 | tf_op jit(solution)/shard_map/ppermute | solution.py:434
  86.2 1.5 %collective-permute-start.13 = (bf16[1,144,128]{2,1,0:T(8,128)(2,1)S(1)}, bf16[1,144,128]{2,1,0:T(8,128)(2,1)S(1)}, u32[]{:S(2)}, u32[]{:S(2)}) collective-permute-start(bf16[1,144,128]{2,1,0:T(8,128)(2,1)S(1)} %add_convert_fusion.4), channel_id=1, source_target_pairs={{0,12},{1,13},{2,14},{3,15},{4,8},{5,9},{6,10},{7,11},{8,4},{9,5},... | collective-permute-start | bytes 110600 | tf_op jit(solution)/shard_map/ppermute | solution.py:434
  87.9 2.8 %collective-permute-start.11 = (bf16[1,144,128]{2,1,0:T(8,128)(2,1)S(1)}, bf16[1,144,128]{2,1,0:T(8,128)(2,1)S(1)}, u32[]{:S(2)}, u32[]{:S(2)}) collective-permute-start(bf16[1,144,128]{2,1,0:T(8,128)(2,1)S(1)} %add_convert_fusion.4), channel_id=1, source_target_pairs={{0,4},{1,5},{2,6},{3,7},{4,0},{5,1},{6,2},{7,3},{8,12},{9,13},{10,... | collective-permute-start | bytes 110600 | tf_op jit(solution)/shard_map/ppermute | solution.py:434
  90.6 1.6 %collective-permute-done.13 = bf16[1,144,128]{2,1,0:T(8,128)(2,1)S(1)} collective-permute-done((bf16[1,144,128]{2,1,0:T(8,128)(2,1)S(1)}, bf16[1,144,128]{2,1,0:T(8,128)(2,1)S(1)}, u32[]{:S(2)}, u32[]{:S(2)}) %collective-permute-start.13) | collective-permute-done | bytes 36896 | tf_op jit(solution)/shard_map/ppermute | solution.py:434
  92.2 0.8 collective-permute-done.12
  93.1 1.5 %collective-permute-start.14 = (bf16[4,144,128]{2,1,0:T(8,128)(2,1)S(1)}, bf16[4,144,128]{2,1,0:T(8,128)(2,1)S(1)}, u32[]{:S(2)}, u32[]{:S(2)}) collective-permute-start(bf16[4,144,128]{2,1,0:T(8,128)(2,1)S(1)} %pad_maximum_fusion.refs_0_), channel_id=1, source_target_pairs={{0,2},{1,3},{2,0},{3,1},{4,6},{5,7},{6,4},{7,5},{8,10},{9,11},{10,... | collective-permute-start | bytes 442376 | tf_op jit(solution)/shard_map/ppermute | solution.py:434
  94.6 2.7 %expand.1 = bf16[4608,128]{1,0:T(8,128)(2,1)} custom-call(s32[1,4608]{1,0:T(1,128)S(1)} %bitcast.13, bf16[4096,128]{1,0:T(8,128)(2,1)S(1)} %bitcast.11), custom_call_target="tpu_custom_call" | custom-call | tf_op jit(solution)/shard_map/expand/pallas_call | solution.py:101
  97.3 1.0 collective-permute-done.14.refs_1_
  98.3 1.4 %collective-permute-done.16.refs_3_ = bf16[4,144,128]{2,1,0:T(8,128)(2,1)S(1)} collective-permute-done((bf16[4,144,128]{2,1,0:T(8,128)(2,1)S(1)}, bf16[4,144,128]{2,1,0:T(8,128)(2,1)S(1)}, u32[]{:S(2)}, u32[]{:S(2)}) %collective-permute-start.16) | collective-permute-done | bytes 147488 | tf_op jit(solution)/shard_map/ppermute | solution.py:434
  99.7 1.6 %finish.1 = (f32[2,256,512]{2,1,0:T(8,128)}, f32[2,32,256]{2,1,0:T(8,128)}, f32[2,16,128]{2,1,0:T(8,128)}, f32[2,64]{1,0:T(2,128)}) custom-call(s32[2]{0:T(128)S(1)} %copy-done.1, bf16[4,144,128]{2,1,0:T(8,128)(2,1)S(1)} %pad_maximum_fusion.refs_0_, bf16[4,144,128]{2,1,0:T(8,128)(2,1)S(1)} %collective-permute-done.14.refs_1_, ...), custom_call_target="tpu_custom_call" | custom-call | tf_op jit(solution)/shard_map/finish/pallas_call | solution.py:467
  (40 shorter events, 2.0 us)
Async XLA Ops:
  4.4 7.6 %copy-start.3 = (bf16[2,256,512]{2,1,0:T(8,128)(2,1)S(1)}, bf16[2,256,512]{2,1,0:T(8,128)(2,1)}, u32[]{:S(2)}) copy-start(bf16[2,256,512]{2,1,0:T(8,128)(2,1)} %refs_4_.1) | copy-start | bytes 1572868
  4.4 9.2 %copy-start.9 = (bf16[2,64]{1,0:T(2,128)(2,1)S(1)}, bf16[2,64]{1,0:T(2,128)(2,1)}, u32[]{:S(2)}) copy-start(bf16[2,64]{1,0:T(2,128)(2,1)} %refs_6_.1) | copy-start | bytes 772
  4.4 9.7 %copy-start.7 = (bf16[2,16,128]{2,1,0:T(8,128)(2,1)S(1)}, bf16[2,16,128]{2,1,0:T(8,128)(2,1)}, u32[]{:S(2)}) copy-start(bf16[2,16,128]{2,1,0:T(8,128)(2,1)} %refs_2_.1) | copy-start | bytes 24580
  4.4 11.2 %copy-start.5 = (bf16[2,256,32]{1,2,0:T(8,128)(2,1)S(1)}, bf16[2,256,32]{1,2,0:T(8,128)(2,1)}, u32[]{:S(2)}) copy-start(bf16[2,256,32]{1,2,0:T(8,128)(2,1)} %param.13) | copy-start | bytes 98308
  4.4 30.6 %all-to-all-start = ((bf16[16,256,128]{2,1,0:T(8,128)(2,1)}), bf16[16,256,128]{2,1,0:T(8,128)(2,1)}, u32[]{:S(2)}, u32[]{:S(2)}) async-start(bf16[16,256,128]{2,1,0:T(8,128)(2,1)} %bitcast.14), calls=%async_computation | async-start | bytes 2097152 | tf_op jit(solution)/shard_map/all_to_all | solution.py:484
  12.0 15.1 %collective-permute-start.2 = (bf16[2,256,512]{2,1,0:T(8,128)(2,1)S(1)}, bf16[2,256,512]{2,1,0:T(8,128)(2,1)S(1)}, u32[]{:S(2)}, u32[]{:S(2)}) collective-permute-start(bf16[2,256,512]{2,1,0:T(8,128)(2,1)S(1)} %copy-done.3), channel_id=1, source_target_pairs={{0,16},{16,0},{1,17},{17,1},{2,18},{18,2},{3,19},{19,3},{4,20},{20... | collective-permute-start | bytes 1572872 | tf_op jit(solution)/shard_map/ppermute | solution.py:531
  13.6 13.2 %collective-permute-start.3 = (bf16[2,64]{1,0:T(2,128)(2,1)S(1)}, bf16[2,64]{1,0:T(2,128)(2,1)S(1)}, u32[]{:S(2)}, u32[]{:S(2)}) collective-permute-start(bf16[2,64]{1,0:T(2,128)(2,1)S(1)} %copy-done.9), channel_id=1, source_target_pairs={{0,16},{16,0},{1,17},{17,1},{2,18},{18,2},{3,19},{19,3},{4,20},{20... | collective-permute-start | bytes 776 | tf_op jit(solution)/shard_map/ppermute | solution.py:531
  14.1 12.7 %collective-permute-start.1 = (bf16[2,16,128]{2,1,0:T(8,128)(2,1)S(1)}, bf16[2,16,128]{2,1,0:T(8,128)(2,1)S(1)}, u32[]{:S(2)}, u32[]{:S(2)}) collective-permute-start(bf16[2,16,128]{2,1,0:T(8,128)(2,1)S(1)} %copy-done.7), channel_id=1, source_target_pairs={{0,16},{16,0},{1,17},{17,1},{2,18},{18,2},{3,19},{19,3},{4,20},{20... | collective-permute-start | bytes 24584 | tf_op jit(solution)/shard_map/ppermute | solution.py:531
  15.6 11.5 %collective-permute-start = (bf16[2,32,256]{2,1,0:T(8,128)(2,1)S(1)}, bf16[2,32,256]{2,1,0:T(8,128)(2,1)S(1)}, u32[]{:S(2)}, u32[]{:S(2)}) collective-permute-start(bf16[2,32,256]{2,1,0:T(8,128)(2,1)S(1)} %bitcast.18), channel_id=1, source_target_pairs={{0,16},{16,0},{1,17},{17,1},{2,18},{18,2},{3,19},{19,3},{4,20},{20... | collective-permute-start | bytes 98312 | tf_op jit(solution)/shard_map/ppermute | solution.py:531
  26.7 1.2 %copy-start.10 = (bf16[2,64]{1,0:T(2,128)(2,1)}, bf16[2,64]{1,0:T(2,128)(2,1)S(1)}, u32[]{:S(2)}) copy-start(bf16[2,64]{1,0:T(2,128)(2,1)S(1)} %collective-permute-done.3.refs_7_) | copy-start | bytes 772
  26.8 1.2 %copy-start.8 = (bf16[2,16,128]{2,1,0:T(8,128)(2,1)}, bf16[2,16,128]{2,1,0:T(8,128)(2,1)S(1)}, u32[]{:S(2)}) copy-start(bf16[2,16,128]{2,1,0:T(8,128)(2,1)S(1)} %collective-permute-done.1.refs_3_) | copy-start | bytes 24580
  27.1 0.8 copy-start.6
  27.1 0.8 copy-start.4
  49.4 7.0 %copy-start.11 = (bf16[16,144,128]{2,1,0:T(8,128)(2,1)S(1)}, bf16[16,144,128]{2,1,0:T(8,128)(2,1)}, u32[]{:S(2)}) copy-start(bf16[16,144,128]{2,1,0:T(8,128)(2,1)} %get-tuple-element.41) | copy-start | bytes 1769476
  49.4 9.1 %copy-start.2 = (bf16[16,144,128]{2,1,0:T(8,128)(2,1)S(1)}, bf16[16,144,128]{2,1,0:T(8,128)(2,1)}, u32[]{:S(2)}) copy-start(bf16[16,144,128]{2,1,0:T(8,128)(2,1)} %get-tuple-element.40) | copy-start | bytes 1769476
  49.4 43.7 %all-to-all-start.1 = ((bf16[16,256,128]{2,1,0:T(8,128)(2,1)}), bf16[16,256,128]{2,1,0:T(8,128)(2,1)S(1)}, u32[]{:S(2)}, u32[]{:S(2)}) async-start(bf16[16,256,128]{2,1,0:T(8,128)(2,1)} %get-tuple-element.42), calls=%async_computation.1 | async-start | bytes 2097152 | tf_op jit(solution)/shard_map/all_to_all | solution.py:484
  56.4 2.1 %collective-permute-start.4 = (bf16[16,144,128]{2,1,0:T(8,128)(2,1)S(1)}, bf16[16,144,128]{2,1,0:T(8,128)(2,1)S(1)}, u32[]{:S(2)}, u32[]{:S(2)}) collective-permute-start(bf16[16,144,128]{2,1,0:T(8,128)(2,1)S(1)} %copy-done.11), channel_id=1, source_target_pairs={{0,1},{1,0},{2,3},{3,2},{4,5},{5,4},{6,7},{7,6},{8,9},{9,8},{10,11... | collective-permute-start | bytes 1769480 | tf_op jit(solution)/shard_map/ppermute | solution.py:434
  58.5 36.1 %copy-start = (s32[1,1,4608]{2,1,0:T(1,128)S(1)}, s32[1,1,4608]{2,1,0:T(1,128)}, u32[]{:S(2)}) copy-start(s32[1,1,4608]{2,1,0:T(1,128)} %param.10) | copy-start | bytes 55300
  58.7 13.9 %collective-permute-start.7 = (bf16[4,144,128]{2,1,0:T(8,128)(2,1)S(1)}, bf16[4,144,128]{2,1,0:T(8,128)(2,1)S(1)}, u32[]{:S(2)}, u32[]{:S(2)}) collective-permute-start(bf16[4,144,128]{2,1,0:T(8,128)(2,1)S(1)} %get-tuple-element.57), channel_id=1, source_target_pairs={{0,18},{1,19},{2,16},{3,17},{4,22},{5,23},{6,20},{7,21},{8,26},{9,... | collective-permute-start | bytes 442376 | tf_op jit(solution)/shard_map/ppermute | solution.py:434
  61.6 13.3 %collective-permute-start.6 = (bf16[4,144,128]{2,1,0:T(8,128)(2,1)S(1)}, bf16[4,144,128]{2,1,0:T(8,128)(2,1)S(1)}, u32[]{:S(2)}, u32[]{:S(2)}) collective-permute-start(bf16[4,144,128]{2,1,0:T(8,128)(2,1)S(1)} %get-tuple-element.58), channel_id=1, source_target_pairs={{0,2},{1,3},{2,0},{3,1},{4,6},{5,7},{6,4},{7,5},{8,10},{9,11},{10,... | collective-permute-start | bytes 442376 | tf_op jit(solution)/shard_map/ppermute | solution.py:434
  61.7 13.2 %collective-permute-start.5 = (bf16[4,144,128]{2,1,0:T(8,128)(2,1)S(1)}, bf16[4,144,128]{2,1,0:T(8,128)(2,1)S(1)}, u32[]{:S(2)}, u32[]{:S(2)}) collective-permute-start(bf16[4,144,128]{2,1,0:T(8,128)(2,1)S(1)} %get-tuple-element.59), channel_id=1, source_target_pairs={{0,16},{1,17},{2,18},{3,19},{4,20},{5,21},{6,22},{7,23},{8,24},{9,... | collective-permute-start | bytes 442376 | tf_op jit(solution)/shard_map/ppermute | solution.py:434
  75.0 6.1 %collective-permute-start.8 = (bf16[1,144,128]{2,1,0:T(8,128)(2,1)S(1)}, bf16[1,144,128]{2,1,0:T(8,128)(2,1)S(1)}, u32[]{:S(2)}, u32[]{:S(2)}) collective-permute-start(bf16[1,144,128]{2,1,0:T(8,128)(2,1)S(1)} %get-tuple-element.60), channel_id=1, source_target_pairs={{0,4},{1,5},{2,6},{3,7},{4,0},{5,1},{6,2},{7,3},{8,12},{9,13},{10,... | collective-permute-start | bytes 110600 | tf_op jit(solution)/shard_map/ppermute | solution.py:434
  75.9 5.9 %collective-permute-start.10 = (bf16[1,144,128]{2,1,0:T(8,128)(2,1)S(1)}, bf16[1,144,128]{2,1,0:T(8,128)(2,1)S(1)}, u32[]{:S(2)}, u32[]{:S(2)}) collective-permute-start(bf16[1,144,128]{2,1,0:T(8,128)(2,1)S(1)} %get-tuple-element.61), channel_id=1, source_target_pairs={{0,12},{1,13},{2,14},{3,15},{4,8},{5,9},{6,10},{7,11},{8,4},{9,5},... | collective-permute-start | bytes 110600 | tf_op jit(solution)/shard_map/ppermute | solution.py:434
  79.2 7.0 %collective-permute-start.9 = (bf16[1,144,128]{2,1,0:T(8,128)(2,1)S(1)}, bf16[1,144,128]{2,1,0:T(8,128)(2,1)S(1)}, u32[]{:S(2)}, u32[]{:S(2)}) collective-permute-start(bf16[1,144,128]{2,1,0:T(8,128)(2,1)S(1)} %get-tuple-element.62), channel_id=1, source_target_pairs={{0,8},{1,9},{2,10},{3,11},{4,12},{5,13},{6,14},{7,15},{8,0},{9,1},... | collective-permute-start | bytes 110600 | tf_op jit(solution)/shard_map/ppermute | solution.py:434
  86.2 6.1 %collective-permute-start.13 = (bf16[1,144,128]{2,1,0:T(8,128)(2,1)S(1)}, bf16[1,144,128]{2,1,0:T(8,128)(2,1)S(1)}, u32[]{:S(2)}, u32[]{:S(2)}) collective-permute-start(bf16[1,144,128]{2,1,0:T(8,128)(2,1)S(1)} %add_convert_fusion.4), channel_id=1, source_target_pairs={{0,12},{1,13},{2,14},{3,15},{4,8},{5,9},{6,10},{7,11},{8,4},{9,5},... | collective-permute-start | bytes 110600 | tf_op jit(solution)/shard_map/ppermute | solution.py:434
  87.7 5.3 %collective-permute-start.12 = (bf16[1,144,128]{2,1,0:T(8,128)(2,1)S(1)}, bf16[1,144,128]{2,1,0:T(8,128)(2,1)S(1)}, u32[]{:S(2)}, u32[]{:S(2)}) collective-permute-start(bf16[1,144,128]{2,1,0:T(8,128)(2,1)S(1)} %add_convert_fusion.4), channel_id=1, source_target_pairs={{0,8},{1,9},{2,10},{3,11},{4,12},{5,13},{6,14},{7,15},{8,0},{9,1},... | collective-permute-start | bytes 110600 | tf_op jit(solution)/shard_map/ppermute | solution.py:434
  87.9 5.1 %collective-permute-start.11 = (bf16[1,144,128]{2,1,0:T(8,128)(2,1)S(1)}, bf16[1,144,128]{2,1,0:T(8,128)(2,1)S(1)}, u32[]{:S(2)}, u32[]{:S(2)}) collective-permute-start(bf16[1,144,128]{2,1,0:T(8,128)(2,1)S(1)} %add_convert_fusion.4), channel_id=1, source_target_pairs={{0,4},{1,5},{2,6},{3,7},{4,0},{5,1},{6,2},{7,3},{8,12},{9,13},{10,... | collective-permute-start | bytes 110600 | tf_op jit(solution)/shard_map/ppermute | solution.py:434
  93.0 6.6 %copy-start.1 = (s32[2]{0:T(128)S(1)}, s32[2]{0:T(128)}, u32[]{:S(2)}) copy-start(s32[2]{0:T(128)} %pad_add_fusion.pos_ref) | copy-start | bytes 28
  93.1 5.2 %collective-permute-start.14 = (bf16[4,144,128]{2,1,0:T(8,128)(2,1)S(1)}, bf16[4,144,128]{2,1,0:T(8,128)(2,1)S(1)}, u32[]{:S(2)}, u32[]{:S(2)}) collective-permute-start(bf16[4,144,128]{2,1,0:T(8,128)(2,1)S(1)} %pad_maximum_fusion.refs_0_), channel_id=1, source_target_pairs={{0,2},{1,3},{2,0},{3,1},{4,6},{5,7},{6,4},{7,5},{8,10},{9,11},{10,... | collective-permute-start | bytes 442376 | tf_op jit(solution)/shard_map/ppermute | solution.py:434
  94.6 3.7 %collective-permute-start.15 = (bf16[4,144,128]{2,1,0:T(8,128)(2,1)S(1)}, bf16[4,144,128]{2,1,0:T(8,128)(2,1)S(1)}, u32[]{:S(2)}, u32[]{:S(2)}) collective-permute-start(bf16[4,144,128]{2,1,0:T(8,128)(2,1)S(1)} %pad_maximum_fusion.refs_0_), channel_id=1, source_target_pairs={{0,1},{1,0},{2,3},{3,2},{4,5},{5,4},{6,7},{7,6},{8,9},{9,8},{10,11... | collective-permute-start | bytes 442376 | tf_op jit(solution)/shard_map/ppermute | solution.py:434
  98.3 1.4 %collective-permute-start.16 = (bf16[4,144,128]{2,1,0:T(8,128)(2,1)S(1)}, bf16[4,144,128]{2,1,0:T(8,128)(2,1)S(1)}, u32[]{:S(2)}, u32[]{:S(2)}) collective-permute-start(bf16[4,144,128]{2,1,0:T(8,128)(2,1)S(1)} %collective-permute-done.14.refs_1_), channel_id=1, source_target_pairs={{0,1},{1,0},{2,3},{3,2},{4,5},{5,4},{6,7},{7,6},{8,9},{9,8},{10,11... | collective-permute-start | bytes 442376 | tf_op jit(solution)/shard_map/ppermute | solution.py:434

commit v5 on v4

--- a/solution.py
+++ b/solution.py
@@ -226,11 +226,14 @@
         saved = []
         for layer in range(LAYERS):
             xs[layer, :, columns] = x
-            mixed = dot(left_ref[layer], x)
-            projected = jnp.concatenate([mixed[F:]] * PAIR, axis=0)
+            projected = dot(left_ref[layer, F:], x)
+            projected = jnp.concatenate([projected] * PAIR, axis=0)
             projected = jnp.where(same, projected, 0.0).astype(BF)
             paired = dot_nt(x, projected).astype(BF)
-            low = dot(paired, diag_ref[layer])
+            mixed = dot(
+                jnp.concatenate([left_ref[layer, :F], paired], axis=1),
+                jnp.concatenate([x, diag_ref[layer]], axis=0),
+            )
             gain = gain_ref[layer : layer + 1, :]
             saved.append((x, projected, paired))
             yield
@@ -238,7 +241,7 @@
                 lanes = slice(t * E, (t + 1) * E)
                 for r in range(0, F, CHUNK):
                     rows = slice(r, r + CHUNK)
-                    total = x[rows, lanes].astype(F32) + mixed[rows, lanes] + low[rows, lanes]
+                    total = x[rows, lanes].astype(F32) + mixed[rows, lanes]
                     centred = total - jnp.sum(total, axis=-1, keepdims=True) * (1.0 / E)
                     variance = jnp.sum(centred * centred, axis=-1, keepdims=True) * (1.0 / E)
                     inverse = lax.rsqrt(variance + EPS)
@@ -287,18 +290,17 @@
             for t in range(PAIR):
                 wacc[layer] += wide[t * K : (t + 1) * K, t * E : (t + 1) * E]
             rest = jnp.zeros((E - K, PW), BF)
-            upstream = dot(back_ref[layer], total_low) + dot(
-                jnp.concatenate([grad_paired, project_ref[layer]], axis=1),
-                jnp.concatenate([projected, grad_projected, rest], axis=0),
+            upstream = dot(
+                jnp.concatenate([back_ref[layer], grad_paired, project_ref[layer]], axis=1),
+                jnp.concatenate([total_low, projected, grad_projected, rest], axis=0),
             )
             yield
             for t in range(PAIR):
                 lanes = slice(t * E, (t + 1) * E)
                 for r in range(0, F, CHUNK):
                     rows = slice(r, r + CHUNK)
-                    out = (grad_s[p, rows, lanes] + upstream[rows, lanes]).astype(BF)
-                    if layer == 0:
-                        out = (out.astype(F32) * scale_ref[rows]).astype(BF)
+                    out = grad_s[p, rows, lanes] + upstream[rows, lanes]
+                    out = (out * scale_ref[rows] if layer == 0 else out).astype(BF)
                     next_s[p, rows, lanes] = out
 
         slots = dot(held["unperm"][...], next_s[p])

time: 102 us -> 100 us (0.980)
  Pallas kernels: 26.1 us -> 24.8 us
    pallas_call x1, Pallas kernels: 14.4 us -> 13 us  [run_layers(): pl.pallas_call(functools.partial(layers_kernel, f_dev=f_dev, packed=packe...]
where the time goes in v5:
time: 100 us
  waiting for transfers between devices  39.3 us (39%)
  starting transfers between devices  33.6 us (34%)
  Pallas kernels  24.8 us (25%)
    ppermute x13, waiting for transfers between devices, across(): return lax.ppermute(x, ('dp', 'mp'), pairs)  25.5 us
    all_to_all x2, starting transfers between devices, exchange(): return lax.all_to_all(x, 'mp', split_axis=0, concat_axis=0, tiled=True)  14.7 us
    ppermute x13, starting transfers between devices, across(): return lax.ppermute(x, ('dp', 'mp'), pairs)  14.7 us
    pallas_call x1, Pallas kernels, run_layers(): pl.pallas_call(functools.partial(layers_kernel, f_dev=f_dev, packed=packe...  13 us
    ppermute x4, waiting for transfers between devices, per_device(): lax.ppermute(part, 'dp', [(0, 1), (1, 0)])  10.4 us
    ppermute x4, starting transfers between devices, per_device(): lax.ppermute(part, 'dp', [(0, 1), (1, 0)])  4.12 us
    pallas_call x1, Pallas kernels, pool(): pl.pallas_call(pool_kernel, out_shape=jax.ShapeDtypeStruct((bags, E), BF)...  3.78 us
    pallas_call x1, Pallas kernels, prepare(): pl.pallas_call(functools.partial(prepare_kernel, halves=halves), out_shap...  3.68 us
  transfers between devices with their start and end apart: 19, of which 13 were waited for; matrix products, arithmetic and copies ran while one was open for 1% of the time, Pallas kernels for 6%

profile of v5, /device:TPU:0, one launch (start us, length us, event | category | flops | bytes accessed | tf_op | source)
XLA Modules:
  0.0 100.1 jit_solution(4390736885541169063)
XLA Ops:
  0.6 3.8 %pool.1 = bf16[4096,128]{1,0:T(8,128)(2,1)} custom-call(s32[1,4608]{1,0:T(1,128)} %bitcast.12, bf16[4608,128]{1,0:T(8,128)(2,1)} %bitcast.15), custom_call_target="tpu_custom_call" | custom-call | tf_op jit(solution)/shard_map/pool/pallas_call | solution.py:77
  4.4 7.6 %all-to-all-start = ((bf16[16,256,128]{2,1,0:T(8,128)(2,1)}), bf16[16,256,128]{2,1,0:T(8,128)(2,1)}, u32[]{:S(2)}, u32[]{:S(2)}) async-start(bf16[16,256,128]{2,1,0:T(8,128)(2,1)} %bitcast.14), calls=%async_computation | async-start | bytes 2097152 | tf_op jit(solution)/shard_map/all_to_all | solution.py:486
  12.0 1.6 %collective-permute-start.2 = (bf16[2,256,512]{2,1,0:T(8,128)(2,1)S(1)}, bf16[2,256,512]{2,1,0:T(8,128)(2,1)S(1)}, u32[]{:S(2)}, u32[]{:S(2)}) collective-permute-start(bf16[2,256,512]{2,1,0:T(8,128)(2,1)S(1)} %copy-done.3), channel_id=1, source_target_pairs={{0,16},{16,0},{1,17},{17,1},{2,18},{18,2},{3,19},{19,3},{4,20},{20... | collective-permute-start | bytes 1572872 | tf_op jit(solution)/shard_map/ppermute | solution.py:533
  13.6 0.5 collective-permute-start.3
  14.1 1.5 %collective-permute-start.1 = (bf16[2,16,128]{2,1,0:T(8,128)(2,1)S(1)}, bf16[2,16,128]{2,1,0:T(8,128)(2,1)S(1)}, u32[]{:S(2)}, u32[]{:S(2)}) collective-permute-start(bf16[2,16,128]{2,1,0:T(8,128)(2,1)S(1)} %copy-done.7), channel_id=1, source_target_pairs={{0,16},{16,0},{1,17},{17,1},{2,18},{18,2},{3,19},{19,3},{4,20},{20... | collective-permute-start | bytes 24584 | tf_op jit(solution)/shard_map/ppermute | solution.py:533
  15.6 0.5 collective-permute-start
  16.1 0.6 pad_add_fusion.pos_ref
  16.7 10.0 %collective-permute-done.3.refs_7_ = bf16[2,64]{1,0:T(2,128)(2,1)S(1)} collective-permute-done((bf16[2,64]{1,0:T(2,128)(2,1)S(1)}, bf16[2,64]{1,0:T(2,128)(2,1)S(1)}, u32[]{:S(2)}, u32[]{:S(2)}) %collective-permute-start.3) | collective-permute-done | bytes 288 | tf_op jit(solution)/shard_map/ppermute | solution.py:533
  27.1 0.8 copy-done.4
  27.9 3.7 %prepare.1 = (bf16[2,544,512]{2,1,0:T(8,128)(2,1)}, bf16[2,512,512]{2,1,0:T(8,128)(2,1)}, bf16[2,128,512]{2,1,0:T(8,128)(2,1)}, bf16[2,512,128]{2,1,0:T(8,128)(2...) custom-call(s32[2]{0:T(128)} %pad_add_fusion.pos_ref, ...), custom_call_target="tpu_custom_call" | custom-call | tf_op jit(solution)/shard_map/prepare/pallas_call | solution.py:158
  31.6 3.4 %all-to-all-done.recv_hbm = bf16[16,256,128]{2,1,0:T(8,128)(2,1)} async-done(((bf16[16,256,128]{2,1,0:T(8,128)(2,1)}), bf16[16,256,128]{2,1,0:T(8,128)(2,1)}, u32[]{:S(2)}, u32[]{:S(2)}) %all-to-all-start) | async-done | bytes 1048608 | tf_op jit(solution)/shard_map/all_to_all | solution.py:486
  35.0 13.0 %layers.1 = (bf16[8,512,128]{2,1,0:T(8,128)(2,1)}, bf16[16,256,128]{2,1,0:T(8,128)(2,1)}, bf16[16,144,128]{2,1,0:T(8,128)(2,1)}, bf16[16,144,128]{2,1,0:T(8,128)(2,1)}) custom-call(s32[2]{0:T(128)} %pad_add_fusion.pos_ref, f32[2,128]{1,0:T(2,128)} %get-tuple-element.31.gain_ref, bf16[16,256,128]{2,1,0:T(8,128)(2,1)} %all-to-all-done.recv_hbm, ...), custom_call_target="tpu_custom_call" | custom-call | tf_op jit(solution)/shard_map/layers/pallas_call | solution.py:406
  48.0 7.2 %all-to-all-start.1 = ((bf16[16,256,128]{2,1,0:T(8,128)(2,1)}), bf16[16,256,128]{2,1,0:T(8,128)(2,1)S(1)}, u32[]{:S(2)}, u32[]{:S(2)}) async-start(bf16[16,256,128]{2,1,0:T(8,128)(2,1)} %get-tuple-element.42), calls=%async_computation.1 | async-start | bytes 2097152 | tf_op jit(solution)/shard_map/all_to_all | solution.py:486
  55.7 1.6 %collective-permute-done.4 = bf16[16,144,128]{2,1,0:T(8,128)(2,1)S(1)} collective-permute-done((bf16[16,144,128]{2,1,0:T(8,128)(2,1)S(1)}, bf16[16,144,128]{2,1,0:T(8,128)(2,1)S(1)}, u32[]{:S(2)}, u32[]{:S(2)}) %collective-permute-start.4) | collective-permute-done | bytes 589856 | tf_op jit(solution)/shard_map/ppermute | solution.py:436
  57.5 2.9 %collective-permute-start.7 = (bf16[4,144,128]{2,1,0:T(8,128)(2,1)S(1)}, bf16[4,144,128]{2,1,0:T(8,128)(2,1)S(1)}, u32[]{:S(2)}, u32[]{:S(2)}) collective-permute-start(bf16[4,144,128]{2,1,0:T(8,128)(2,1)S(1)} %get-tuple-element.57), channel_id=1, source_target_pairs={{0,18},{1,19},{2,16},{3,17},{4,22},{5,23},{6,20},{7,21},{8,26},{9,... | collective-permute-start | bytes 442376 | tf_op jit(solution)/shard_map/ppermute | solution.py:436
  60.5 0.5 collective-permute-start.5
  61.0 10.3 %collective-permute-done.7 = bf16[4,144,128]{2,1,0:T(8,128)(2,1)S(1)} collective-permute-done((bf16[4,144,128]{2,1,0:T(8,128)(2,1)S(1)}, bf16[4,144,128]{2,1,0:T(8,128)(2,1)S(1)}, u32[]{:S(2)}, u32[]{:S(2)}) %collective-permute-start.7) | collective-permute-done | bytes 147488 | tf_op jit(solution)/shard_map/ppermute | solution.py:436
  71.3 2.4 %collective-permute-done.6 = bf16[4,144,128]{2,1,0:T(8,128)(2,1)S(1)} collective-permute-done((bf16[4,144,128]{2,1,0:T(8,128)(2,1)S(1)}, bf16[4,144,128]{2,1,0:T(8,128)(2,1)S(1)}, u32[]{:S(2)}, u32[]{:S(2)}) %collective-permute-start.6) | collective-permute-done | bytes 147488 | tf_op jit(solution)/shard_map/ppermute | solution.py:436
  73.8 0.9 collective-permute-start.8
  74.7 3.3 %collective-permute-start.10 = (bf16[1,144,128]{2,1,0:T(8,128)(2,1)S(1)}, bf16[1,144,128]{2,1,0:T(8,128)(2,1)S(1)}, u32[]{:S(2)}, u32[]{:S(2)}) collective-permute-start(bf16[1,144,128]{2,1,0:T(8,128)(2,1)S(1)} %get-tuple-element.61), channel_id=1, source_target_pairs={{0,12},{1,13},{2,14},{3,15},{4,8},{5,9},{6,10},{7,11},{8,4},{9,5},... | collective-permute-start | bytes 110600 | tf_op jit(solution)/shard_map/ppermute | solution.py:436
  78.4 1.5 %collective-permute-done.8 = bf16[1,144,128]{2,1,0:T(8,128)(2,1)S(1)} collective-permute-done((bf16[1,144,128]{2,1,0:T(8,128)(2,1)S(1)}, bf16[1,144,128]{2,1,0:T(8,128)(2,1)S(1)}, u32[]{:S(2)}, u32[]{:S(2)}) %collective-permute-start.8) | collective-permute-done | bytes 36896 | tf_op jit(solution)/shard_map/ppermute | solution.py:436
  79.9 0.6 collective-permute-done.10
  80.6 4.4 %collective-permute-done.9 = bf16[1,144,128]{2,1,0:T(8,128)(2,1)S(1)} collective-permute-done((bf16[1,144,128]{2,1,0:T(8,128)(2,1)S(1)}, bf16[1,144,128]{2,1,0:T(8,128)(2,1)S(1)}, u32[]{:S(2)}, u32[]{:S(2)}) %collective-permute-start.9) | collective-permute-done | bytes 36896 | tf_op jit(solution)/shard_map/ppermute | solution.py:436
  85.0 1.5 %collective-permute-start.13 = (bf16[1,144,128]{2,1,0:T(8,128)(2,1)S(1)}, bf16[1,144,128]{2,1,0:T(8,128)(2,1)S(1)}, u32[]{:S(2)}, u32[]{:S(2)}) collective-permute-start(bf16[1,144,128]{2,1,0:T(8,128)(2,1)S(1)} %add_convert_fusion.4), channel_id=1, source_target_pairs={{0,12},{1,13},{2,14},{3,15},{4,8},{5,9},{6,10},{7,11},{8,4},{9,5},... | collective-permute-start | bytes 110600 | tf_op jit(solution)/shard_map/ppermute | solution.py:436
  86.7 2.8 %collective-permute-start.11 = (bf16[1,144,128]{2,1,0:T(8,128)(2,1)S(1)}, bf16[1,144,128]{2,1,0:T(8,128)(2,1)S(1)}, u32[]{:S(2)}, u32[]{:S(2)}) collective-permute-start(bf16[1,144,128]{2,1,0:T(8,128)(2,1)S(1)} %add_convert_fusion.4), channel_id=1, source_target_pairs={{0,4},{1,5},{2,6},{3,7},{4,0},{5,1},{6,2},{7,3},{8,12},{9,13},{10,... | collective-permute-start | bytes 110600 | tf_op jit(solution)/shard_map/ppermute | solution.py:436
  89.4 1.6 %collective-permute-done.13 = bf16[1,144,128]{2,1,0:T(8,128)(2,1)S(1)} collective-permute-done((bf16[1,144,128]{2,1,0:T(8,128)(2,1)S(1)}, bf16[1,144,128]{2,1,0:T(8,128)(2,1)S(1)}, u32[]{:S(2)}, u32[]{:S(2)}) %collective-permute-start.13) | collective-permute-done | bytes 36896 | tf_op jit(solution)/shard_map/ppermute | solution.py:436
  91.0 0.8 collective-permute-done.12
  91.9 1.5 %collective-permute-start.14 = (bf16[4,144,128]{2,1,0:T(8,128)(2,1)S(1)}, bf16[4,144,128]{2,1,0:T(8,128)(2,1)S(1)}, u32[]{:S(2)}, u32[]{:S(2)}) collective-permute-start(bf16[4,144,128]{2,1,0:T(8,128)(2,1)S(1)} %pad_maximum_fusion.refs_0_), channel_id=1, source_target_pairs={{0,2},{1,3},{2,0},{3,1},{4,6},{5,7},{6,4},{7,5},{8,10},{9,11},{10,... | collective-permute-start | bytes 442376 | tf_op jit(solution)/shard_map/ppermute | solution.py:436
  93.4 2.7 %expand.1 = bf16[4608,128]{1,0:T(8,128)(2,1)} custom-call(s32[1,4608]{1,0:T(1,128)S(1)} %bitcast.13, bf16[4096,128]{1,0:T(8,128)(2,1)S(1)} %bitcast.11), custom_call_target="tpu_custom_call" | custom-call | tf_op jit(solution)/shard_map/expand/pallas_call | solution.py:101
  96.1 1.0 collective-permute-done.14.refs_1_
  97.1 1.4 %collective-permute-done.16.refs_3_ = bf16[4,144,128]{2,1,0:T(8,128)(2,1)S(1)} collective-permute-done((bf16[4,144,128]{2,1,0:T(8,128)(2,1)S(1)}, bf16[4,144,128]{2,1,0:T(8,128)(2,1)S(1)}, u32[]{:S(2)}, u32[]{:S(2)}) %collective-permute-start.16) | collective-permute-done | bytes 147488 | tf_op jit(solution)/shard_map/ppermute | solution.py:436
  98.4 1.6 %finish.1 = (f32[2,256,512]{2,1,0:T(8,128)}, f32[2,32,256]{2,1,0:T(8,128)}, f32[2,16,128]{2,1,0:T(8,128)}, f32[2,64]{1,0:T(2,128)}) custom-call(s32[2]{0:T(128)S(1)} %copy-done.1, bf16[4,144,128]{2,1,0:T(8,128)(2,1)S(1)} %pad_maximum_fusion.refs_0_, bf16[4,144,128]{2,1,0:T(8,128)(2,1)S(1)} %collective-permute-done.14.refs_1_, ...), custom_call_target="tpu_custom_call" | custom-call | tf_op jit(solution)/shard_map/finish/pallas_call | solution.py:469
  (40 shorter events, 2.0 us)
Async XLA Ops:
  4.4 7.6 %copy-start.3 = (bf16[2,256,512]{2,1,0:T(8,128)(2,1)S(1)}, bf16[2,256,512]{2,1,0:T(8,128)(2,1)}, u32[]{:S(2)}) copy-start(bf16[2,256,512]{2,1,0:T(8,128)(2,1)} %refs_4_.1) | copy-start | bytes 1572868
  4.4 9.2 %copy-start.9 = (bf16[2,64]{1,0:T(2,128)(2,1)S(1)}, bf16[2,64]{1,0:T(2,128)(2,1)}, u32[]{:S(2)}) copy-start(bf16[2,64]{1,0:T(2,128)(2,1)} %refs_6_.1) | copy-start | bytes 772
  4.4 9.7 %copy-start.7 = (bf16[2,16,128]{2,1,0:T(8,128)(2,1)S(1)}, bf16[2,16,128]{2,1,0:T(8,128)(2,1)}, u32[]{:S(2)}) copy-start(bf16[2,16,128]{2,1,0:T(8,128)(2,1)} %refs_2_.1) | copy-start | bytes 24580
  4.4 11.2 %copy-start.5 = (bf16[2,256,32]{1,2,0:T(8,128)(2,1)S(1)}, bf16[2,256,32]{1,2,0:T(8,128)(2,1)}, u32[]{:S(2)}) copy-start(bf16[2,256,32]{1,2,0:T(8,128)(2,1)} %param.13) | copy-start | bytes 98308
  4.4 30.6 %all-to-all-start = ((bf16[16,256,128]{2,1,0:T(8,128)(2,1)}), bf16[16,256,128]{2,1,0:T(8,128)(2,1)}, u32[]{:S(2)}, u32[]{:S(2)}) async-start(bf16[16,256,128]{2,1,0:T(8,128)(2,1)} %bitcast.14), calls=%async_computation | async-start | bytes 2097152 | tf_op jit(solution)/shard_map/all_to_all | solution.py:486
  12.0 15.1 %collective-permute-start.2 = (bf16[2,256,512]{2,1,0:T(8,128)(2,1)S(1)}, bf16[2,256,512]{2,1,0:T(8,128)(2,1)S(1)}, u32[]{:S(2)}, u32[]{:S(2)}) collective-permute-start(bf16[2,256,512]{2,1,0:T(8,128)(2,1)S(1)} %copy-done.3), channel_id=1, source_target_pairs={{0,16},{16,0},{1,17},{17,1},{2,18},{18,2},{3,19},{19,3},{4,20},{20... | collective-permute-start | bytes 1572872 | tf_op jit(solution)/shard_map/ppermute | solution.py:533
  13.6 13.2 %collective-permute-start.3 = (bf16[2,64]{1,0:T(2,128)(2,1)S(1)}, bf16[2,64]{1,0:T(2,128)(2,1)S(1)}, u32[]{:S(2)}, u32[]{:S(2)}) collective-permute-start(bf16[2,64]{1,0:T(2,128)(2,1)S(1)} %copy-done.9), channel_id=1, source_target_pairs={{0,16},{16,0},{1,17},{17,1},{2,18},{18,2},{3,19},{19,3},{4,20},{20... | collective-permute-start | bytes 776 | tf_op jit(solution)/shard_map/ppermute | solution.py:533
  14.1 12.7 %collective-permute-start.1 = (bf16[2,16,128]{2,1,0:T(8,128)(2,1)S(1)}, bf16[2,16,128]{2,1,0:T(8,128)(2,1)S(1)}, u32[]{:S(2)}, u32[]{:S(2)}) collective-permute-start(bf16[2,16,128]{2,1,0:T(8,128)(2,1)S(1)} %copy-done.7), channel_id=1, source_target_pairs={{0,16},{16,0},{1,17},{17,1},{2,18},{18,2},{3,19},{19,3},{4,20},{20... | collective-permute-start | bytes 24584 | tf_op jit(solution)/shard_map/ppermute | solution.py:533
  15.6 11.5 %collective-permute-start = (bf16[2,32,256]{2,1,0:T(8,128)(2,1)S(1)}, bf16[2,32,256]{2,1,0:T(8,128)(2,1)S(1)}, u32[]{:S(2)}, u32[]{:S(2)}) collective-permute-start(bf16[2,32,256]{2,1,0:T(8,128)(2,1)S(1)} %bitcast.18), channel_id=1, source_target_pairs={{0,16},{16,0},{1,17},{17,1},{2,18},{18,2},{3,19},{19,3},{4,20},{20... | collective-permute-start | bytes 98312 | tf_op jit(solution)/shard_map/ppermute | solution.py:533
  26.7 1.2 %copy-start.10 = (bf16[2,64]{1,0:T(2,128)(2,1)}, bf16[2,64]{1,0:T(2,128)(2,1)S(1)}, u32[]{:S(2)}) copy-start(bf16[2,64]{1,0:T(2,128)(2,1)S(1)} %collective-permute-done.3.refs_7_) | copy-start | bytes 772
  26.8 1.2 %copy-start.8 = (bf16[2,16,128]{2,1,0:T(8,128)(2,1)}, bf16[2,16,128]{2,1,0:T(8,128)(2,1)S(1)}, u32[]{:S(2)}) copy-start(bf16[2,16,128]{2,1,0:T(8,128)(2,1)S(1)} %collective-permute-done.1.refs_3_) | copy-start | bytes 24580
  27.1 0.8 copy-start.6
  27.1 0.8 copy-start.4
  48.0 7.2 %copy-start.11 = (bf16[16,144,128]{2,1,0:T(8,128)(2,1)S(1)}, bf16[16,144,128]{2,1,0:T(8,128)(2,1)}, u32[]{:S(2)}) copy-start(bf16[16,144,128]{2,1,0:T(8,128)(2,1)} %get-tuple-element.41) | copy-start | bytes 1769476
  48.0 9.3 %copy-start.2 = (bf16[16,144,128]{2,1,0:T(8,128)(2,1)S(1)}, bf16[16,144,128]{2,1,0:T(8,128)(2,1)}, u32[]{:S(2)}) copy-start(bf16[16,144,128]{2,1,0:T(8,128)(2,1)} %get-tuple-element.40) | copy-start | bytes 1769476
  48.0 43.9 %all-to-all-start.1 = ((bf16[16,256,128]{2,1,0:T(8,128)(2,1)}), bf16[16,256,128]{2,1,0:T(8,128)(2,1)S(1)}, u32[]{:S(2)}, u32[]{:S(2)}) async-start(bf16[16,256,128]{2,1,0:T(8,128)(2,1)} %get-tuple-element.42), calls=%async_computation.1 | async-start | bytes 2097152 | tf_op jit(solution)/shard_map/all_to_all | solution.py:486
  55.2 2.1 %collective-permute-start.4 = (bf16[16,144,128]{2,1,0:T(8,128)(2,1)S(1)}, bf16[16,144,128]{2,1,0:T(8,128)(2,1)S(1)}, u32[]{:S(2)}, u32[]{:S(2)}) collective-permute-start(bf16[16,144,128]{2,1,0:T(8,128)(2,1)S(1)} %copy-done.11), channel_id=1, source_target_pairs={{0,1},{1,0},{2,3},{3,2},{4,5},{5,4},{6,7},{7,6},{8,9},{9,8},{10,11... | collective-permute-start | bytes 1769480 | tf_op jit(solution)/shard_map/ppermute | solution.py:436
  57.3 36.1 %copy-start = (s32[1,1,4608]{2,1,0:T(1,128)S(1)}, s32[1,1,4608]{2,1,0:T(1,128)}, u32[]{:S(2)}) copy-start(s32[1,1,4608]{2,1,0:T(1,128)} %param.10) | copy-start | bytes 55300
  57.5 13.9 %collective-permute-start.7 = (bf16[4,144,128]{2,1,0:T(8,128)(2,1)S(1)}, bf16[4,144,128]{2,1,0:T(8,128)(2,1)S(1)}, u32[]{:S(2)}, u32[]{:S(2)}) collective-permute-start(bf16[4,144,128]{2,1,0:T(8,128)(2,1)S(1)} %get-tuple-element.57), channel_id=1, source_target_pairs={{0,18},{1,19},{2,16},{3,17},{4,22},{5,23},{6,20},{7,21},{8,26},{9,... | collective-permute-start | bytes 442376 | tf_op jit(solution)/shard_map/ppermute | solution.py:436
  60.4 13.3 %collective-permute-start.6 = (bf16[4,144,128]{2,1,0:T(8,128)(2,1)S(1)}, bf16[4,144,128]{2,1,0:T(8,128)(2,1)S(1)}, u32[]{:S(2)}, u32[]{:S(2)}) collective-permute-start(bf16[4,144,128]{2,1,0:T(8,128)(2,1)S(1)} %get-tuple-element.58), channel_id=1, source_target_pairs={{0,2},{1,3},{2,0},{3,1},{4,6},{5,7},{6,4},{7,5},{8,10},{9,11},{10,... | collective-permute-start | bytes 442376 | tf_op jit(solution)/shard_map/ppermute | solution.py:436
  60.5 13.2 %collective-permute-start.5 = (bf16[4,144,128]{2,1,0:T(8,128)(2,1)S(1)}, bf16[4,144,128]{2,1,0:T(8,128)(2,1)S(1)}, u32[]{:S(2)}, u32[]{:S(2)}) collective-permute-start(bf16[4,144,128]{2,1,0:T(8,128)(2,1)S(1)} %get-tuple-element.59), channel_id=1, source_target_pairs={{0,16},{1,17},{2,18},{3,19},{4,20},{5,21},{6,22},{7,23},{8,24},{9,... | collective-permute-start | bytes 442376 | tf_op jit(solution)/shard_map/ppermute | solution.py:436
  73.8 6.1 %collective-permute-start.8 = (bf16[1,144,128]{2,1,0:T(8,128)(2,1)S(1)}, bf16[1,144,128]{2,1,0:T(8,128)(2,1)S(1)}, u32[]{:S(2)}, u32[]{:S(2)}) collective-permute-start(bf16[1,144,128]{2,1,0:T(8,128)(2,1)S(1)} %get-tuple-element.60), channel_id=1, source_target_pairs={{0,4},{1,5},{2,6},{3,7},{4,0},{5,1},{6,2},{7,3},{8,12},{9,13},{10,... | collective-permute-start | bytes 110600 | tf_op jit(solution)/shard_map/ppermute | solution.py:436
  74.7 5.9 %collective-permute-start.10 = (bf16[1,144,128]{2,1,0:T(8,128)(2,1)S(1)}, bf16[1,144,128]{2,1,0:T(8,128)(2,1)S(1)}, u32[]{:S(2)}, u32[]{:S(2)}) collective-permute-start(bf16[1,144,128]{2,1,0:T(8,128)(2,1)S(1)} %get-tuple-element.61), channel_id=1, source_target_pairs={{0,12},{1,13},{2,14},{3,15},{4,8},{5,9},{6,10},{7,11},{8,4},{9,5},... | collective-permute-start | bytes 110600 | tf_op jit(solution)/shard_map/ppermute | solution.py:436
  78.0 7.0 %collective-permute-start.9 = (bf16[1,144,128]{2,1,0:T(8,128)(2,1)S(1)}, bf16[1,144,128]{2,1,0:T(8,128)(2,1)S(1)}, u32[]{:S(2)}, u32[]{:S(2)}) collective-permute-start(bf16[1,144,128]{2,1,0:T(8,128)(2,1)S(1)} %get-tuple-element.62), channel_id=1, source_target_pairs={{0,8},{1,9},{2,10},{3,11},{4,12},{5,13},{6,14},{7,15},{8,0},{9,1},... | collective-permute-start | bytes 110600 | tf_op jit(solution)/shard_map/ppermute | solution.py:436
  85.0 6.0 %collective-permute-start.13 = (bf16[1,144,128]{2,1,0:T(8,128)(2,1)S(1)}, bf16[1,144,128]{2,1,0:T(8,128)(2,1)S(1)}, u32[]{:S(2)}, u32[]{:S(2)}) collective-permute-start(bf16[1,144,128]{2,1,0:T(8,128)(2,1)S(1)} %add_convert_fusion.4), channel_id=1, source_target_pairs={{0,12},{1,13},{2,14},{3,15},{4,8},{5,9},{6,10},{7,11},{8,4},{9,5},... | collective-permute-start | bytes 110600 | tf_op jit(solution)/shard_map/ppermute | solution.py:436
  86.5 5.3 %collective-permute-start.12 = (bf16[1,144,128]{2,1,0:T(8,128)(2,1)S(1)}, bf16[1,144,128]{2,1,0:T(8,128)(2,1)S(1)}, u32[]{:S(2)}, u32[]{:S(2)}) collective-permute-start(bf16[1,144,128]{2,1,0:T(8,128)(2,1)S(1)} %add_convert_fusion.4), channel_id=1, source_target_pairs={{0,8},{1,9},{2,10},{3,11},{4,12},{5,13},{6,14},{7,15},{8,0},{9,1},... | collective-permute-start | bytes 110600 | tf_op jit(solution)/shard_map/ppermute | solution.py:436
  86.7 5.1 %collective-permute-start.11 = (bf16[1,144,128]{2,1,0:T(8,128)(2,1)S(1)}, bf16[1,144,128]{2,1,0:T(8,128)(2,1)S(1)}, u32[]{:S(2)}, u32[]{:S(2)}) collective-permute-start(bf16[1,144,128]{2,1,0:T(8,128)(2,1)S(1)} %add_convert_fusion.4), channel_id=1, source_target_pairs={{0,4},{1,5},{2,6},{3,7},{4,0},{5,1},{6,2},{7,3},{8,12},{9,13},{10,... | collective-permute-start | bytes 110600 | tf_op jit(solution)/shard_map/ppermute | solution.py:436
  91.8 6.6 %copy-start.1 = (s32[2]{0:T(128)S(1)}, s32[2]{0:T(128)}, u32[]{:S(2)}) copy-start(s32[2]{0:T(128)} %pad_add_fusion.pos_ref) | copy-start | bytes 28
  91.9 5.2 %collective-permute-start.14 = (bf16[4,144,128]{2,1,0:T(8,128)(2,1)S(1)}, bf16[4,144,128]{2,1,0:T(8,128)(2,1)S(1)}, u32[]{:S(2)}, u32[]{:S(2)}) collective-permute-start(bf16[4,144,128]{2,1,0:T(8,128)(2,1)S(1)} %pad_maximum_fusion.refs_0_), channel_id=1, source_target_pairs={{0,2},{1,3},{2,0},{3,1},{4,6},{5,7},{6,4},{7,5},{8,10},{9,11},{10,... | collective-permute-start | bytes 442376 | tf_op jit(solution)/shard_map/ppermute | solution.py:436
  93.4 3.7 %collective-permute-start.15 = (bf16[4,144,128]{2,1,0:T(8,128)(2,1)S(1)}, bf16[4,144,128]{2,1,0:T(8,128)(2,1)S(1)}, u32[]{:S(2)}, u32[]{:S(2)}) collective-permute-start(bf16[4,144,128]{2,1,0:T(8,128)(2,1)S(1)} %pad_maximum_fusion.refs_0_), channel_id=1, source_target_pairs={{0,1},{1,0},{2,3},{3,2},{4,5},{5,4},{6,7},{7,6},{8,9},{9,8},{10,11... | collective-permute-start | bytes 442376 | tf_op jit(solution)/shard_map/ppermute | solution.py:436
  97.1 1.4 %collective-permute-start.16 = (bf16[4,144,128]{2,1,0:T(8,128)(2,1)S(1)}, bf16[4,144,128]{2,1,0:T(8,128)(2,1)S(1)}, u32[]{:S(2)}, u32[]{:S(2)}) collective-permute-start(bf16[4,144,128]{2,1,0:T(8,128)(2,1)S(1)} %collective-permute-done.14.refs_1_), channel_id=1, source_target_pairs={{0,1},{1,0},{2,3},{3,2},{4,5},{5,4},{6,7},{7,6},{8,9},{9,8},{10,11... | collective-permute-start | bytes 442376 | tf_op jit(solution)/shard_map/ppermute | solution.py:436

commit v6 on v5

--- a/solution.py
+++ b/solution.py
@@ -110,7 +110,7 @@
 def prepare_kernel(pos_ref, slot_ref, expo_ref, *refs, halves):
     weights, outs = refs[: 4 * halves], refs[4 * halves :]
     projects, outputs, mixes, gains = (weights[n * halves : (n + 1) * halves] for n in range(4))
-    left_ref, back_ref, diag_ref, project_ref, gain_ref, scale_ref, perm_ref, unperm_ref = outs
+    left_ref, back_ref, diag_ref, project_ref, gain_ref, scale_ref, unperm_ref = outs
     first = pos_ref[0] == 0
 
     def joined(parts, axis):
@@ -148,7 +148,6 @@
     ).astype(BF)
     scale_ref[...] = dot_tn(small, spread)
     hot = jnp.where(slot_ref[...] == lax.broadcasted_iota(jnp.int32, (F, F), 0), 1.0, 0.0)
-    perm_ref[...] = hot.astype(BF)
     unperm_ref[...] = hot.T.astype(BF)
 
 
@@ -165,10 +164,9 @@
             jax.ShapeDtypeStruct((LAYERS, E), F32),
             jax.ShapeDtypeStruct((F, E), F32),
             jax.ShapeDtypeStruct((F, F), BF),
-            jax.ShapeDtypeStruct((F, F), BF),
         ),
         in_specs=[pl.BlockSpec(memory_space=pltpu.SMEM)] + [VMEM] * (2 + len(flat)),
-        out_specs=(VMEM,) * 8,
+        out_specs=(VMEM,) * 7,
         compiler_params=params(FULL),
         name="prepare",
     )(pos, slot_feature.reshape(1, F), block_exponent.T, *flat)
@@ -181,10 +179,10 @@
     return jnp.concatenate(parts, axis=1).astype(BF)
 
 
-CONSTANTS = ("perm", "scale", "left", "diag", "back", "project", "unperm")
-
-
-def layers_kernel(pos_ref, gain_ref, recv_hbm, cot_hbm, *refs, f_dev, packed):
+CONSTANTS = ("scale", "left", "diag", "back", "project", "unperm")
+
+
+def layers_kernel(pos_ref, gain_ref, slot_ref, recv_hbm, cot_hbm, *refs, f_dev, packed):
     sources, refs = dict(zip(CONSTANTS, refs)), refs[len(CONSTANTS) :]
     feats_hbm, slots_hbm = refs[:2]
     grads = 2 if packed else 4
@@ -204,18 +202,20 @@
         copies.start(name, sources[name], held[name])
 
     copies.start("recv", recv_hbm, recv_ref)
-    for name in ("perm", "scale", "left", "diag"):
+    for name in ("scale", "left", "diag"):
         fetch(name)
     copies.start("cot", cot_hbm, cot_ref)
     for name in ("back", "project", "unperm"):
         fetch(name)
+    hot = slot_ref[...] == lax.broadcasted_iota(jnp.int32, (F, F), 0)
+    perm = jnp.where(hot, 1.0, 0.0).astype(BF)
 
     wacc[...] = jnp.zeros_like(wacc)
     gacc[...] = jnp.zeros_like(gacc)
 
     def pair_steps(p):
         columns = slice(p * PW, (p + 1) * PW)
-        x = dot(held["perm"][...], unslot(recv_ref[:, slot_rows(p)], f_dev))
+        x = dot(perm, unslot(recv_ref[:, slot_rows(p)], f_dev))
         scale = scale_ref[...]
         x = (x * jnp.concatenate([scale] * PAIR, axis=1)).astype(BF)
         yield
@@ -357,7 +357,7 @@
     phases = 4 * LAYERS + 2
     for tick in range(phases):
         if tick == 0:
-            copies.wait("recv", "perm", "scale")
+            copies.wait("recv", "scale")
         if tick == 1:
             copies.wait("left", "diag")
         if tick == 2 * LAYERS + 1:
@@ -375,8 +375,8 @@
     copies.drain()
 
 
-def run_layers(pos, recv, cotangent, operands, f_dev, packed):
-    left, back, diag, project, gain, scale, perm, unperm = operands
+def run_layers(pos, slot_feature, recv, cotangent, operands, f_dev, packed):
+    left, back, diag, project, gain, scale, unperm = operands
     tables = F // f_dev
 
     def shape(dims, dtype=F32):
@@ -392,7 +392,7 @@
             shape((LAYERS, E)),
         ]
     given = dict(
-        perm=perm, scale=scale, left=left, diag=diag, back=back, project=project, unperm=unperm
+        scale=scale, left=left, diag=diag, back=back, project=project, unperm=unperm
     )
     constants = [given[name] for name in CONSTANTS]
     width = SAMP_DEV * E
@@ -406,7 +406,7 @@
     return pl.pallas_call(
         functools.partial(layers_kernel, f_dev=f_dev, packed=packed),
         out_shape=outs,
-        in_specs=[pl.BlockSpec(memory_space=pltpu.SMEM), VMEM]
+        in_specs=[pl.BlockSpec(memory_space=pltpu.SMEM), VMEM, VMEM]
         + [HBM] * (2 + len(constants)),
         out_specs=[HBM] * len(outs),
         scratch_shapes=[scratch(x) for x in constants]
@@ -428,7 +428,7 @@
         ],
         compiler_params=params(WHOLE),
         name="layers",
-    )(pos, gain, recv, cotangent, *constants)
+    )(pos, gain, slot_feature.reshape(1, F), recv, cotangent, *constants)
 
 
 def across(x, d, m):
@@ -489,10 +489,11 @@
 def return_packed(pos, slots, keep, send, ids, factor):
     rows, bags = ids.shape[1], slots.shape[0] * slots.shape[1]
     other = across(send, 0, 1)
-    own, to_y, to_x, to_xy = [
-        added([part[4 * r : 4 * r + 4] for part in (keep, other)]) for r in range(4)
-    ]
-    parts = [own, across(to_y, 1, 0), across(to_x, 0, 2), across(to_xy, 1, 2)]
+    both = [part.reshape(2, 2, 4, PIECE, E) for part in (keep, other)]
+    to_y, own = (added([part[:, ry] for part in both]) for ry in (1, 0))
+    both = [own, across(to_y, 1, 0)]
+    to_x, own = (added([part[rx] for part in both]) for rx in (1, 0))
+    parts = [own, across(to_x, 0, 2)]
     owner = exchange(slots)
     quarters = [added([part[r : r + 1] for part in parts]) for r in range(4)]
     parts = [quarters[0]] + [across(quarters[r], 0, 4 * r) for r in range(1, 4)]
@@ -538,7 +539,7 @@
         ]
     operands = prepare(pos, slot_feature, block_exponent, weights)
     packed = (groups, tables) == (2, 16)
-    feats, slots, *grads = run_layers(pos, recv, out_cotangent, operands, f_dev, packed)
+    feats, slots, *grads = run_layers(pos, slot_feature, recv, out_cotangent, operands, f_dev, packed)
     if packed:
         row_grads, shares = return_packed(pos, slots, *grads, ids, factor)
         project_t, output_g, mix_g, gain_g = shares[1], shares[2], shares[0], shares[3]

time: 100 us -> 100 us (level)
  starting transfers between devices: 33.6 us -> 32.1 us
  waiting for transfers between devices: 39.3 us -> 40.8 us
    ppermute x13 -> x12, waiting for transfers between devices: 25.5 us -> 26.9 us  [across(): return lax.ppermute(x, ('dp', 'mp'), pairs)]
    ppermute x13 -> x12, starting transfers between devices: 14.7 us -> 13.9 us  [across(): return lax.ppermute(x, ('dp', 'mp'), pairs)]
  transfers between devices with their start and end apart: 19 -> 18, of which waited for: 13 -> 12; matrix products, arithmetic and copies ran while one was open for 1% -> 1% of each run, Pallas kernels for 6% -> 6%
where the time goes in v6:
time: 100 us; the launch traced here: 99.9 us
  waiting for transfers between devices  40.8 us (41%)
  starting transfers between devices  32.1 us (32%)
  Pallas kernels  24.4 us (24%)
    ppermute x12, waiting for transfers between devices, across(): return lax.ppermute(x, ('dp', 'mp'), pairs)  26.9 us
    all_to_all x2, starting transfers between devices, exchange(): return lax.all_to_all(x, 'mp', split_axis=0, concat_axis=0, tiled=True)  14.1 us
    ppermute x12, starting transfers between devices, across(): return lax.ppermute(x, ('dp', 'mp'), pairs)  13.9 us
    pallas_call x1, Pallas kernels, run_layers(): pl.pallas_call(functools.partial(layers_kernel, f_dev=f_dev, packed=packe...  12.8 us
    ppermute x4, waiting for transfers between devices, per_device(): lax.ppermute(part, 'dp', [(0, 1), (1, 0)])  10.4 us
    ppermute x4, starting transfers between devices, per_device(): lax.ppermute(part, 'dp', [(0, 1), (1, 0)])  4.12 us
    pallas_call x1, Pallas kernels, pool(): pl.pallas_call(pool_kernel, out_shape=jax.ShapeDtypeStruct((bags, E), BF)...  3.78 us
    all_to_all x2, waiting for transfers between devices, exchange(): return lax.all_to_all(x, 'mp', split_axis=0, concat_axis=0, tiled=True)  3.54 us
  transfers between devices with their start and end apart: 18, of which 12 were waited for; matrix products, arithmetic and copies ran while one was open for 1% of the time, Pallas kernels for 6%

profile of v6, /device:TPU:0, one launch (start us, length us, event | category | flops | bytes accessed | tf_op | source)
XLA Modules:
  0.0 99.9 jit_solution(13639063193575838714)
XLA Ops:
  0.6 3.8 %pool.1 = bf16[4096,128]{1,0:T(8,128)(2,1)} custom-call(s32[1,4608]{1,0:T(1,128)} %bitcast.48, bf16[4608,128]{1,0:T(8,128)(2,1)} %bitcast.51), custom_call_target="tpu_custom_call" | custom-call | tf_op jit(solution)/shard_map/pool/pallas_call | solution.py:77
  4.4 7.6 %all-to-all-start = ((bf16[16,256,128]{2,1,0:T(8,128)(2,1)}), bf16[16,256,128]{2,1,0:T(8,128)(2,1)}, u32[]{:S(2)}, u32[]{:S(2)}) async-start(bf16[16,256,128]{2,1,0:T(8,128)(2,1)} %bitcast.50), calls=%async_computation | async-start | bytes 2097152 | tf_op jit(solution)/shard_map/all_to_all | solution.py:486
  12.0 1.6 %collective-permute-start.2 = (bf16[2,256,512]{2,1,0:T(8,128)(2,1)S(1)}, bf16[2,256,512]{2,1,0:T(8,128)(2,1)S(1)}, u32[]{:S(2)}, u32[]{:S(2)}) collective-permute-start(bf16[2,256,512]{2,1,0:T(8,128)(2,1)S(1)} %copy-done.3), channel_id=1, source_target_pairs={{0,16},{16,0},{1,17},{17,1},{2,18},{18,2},{3,19},{19,3},{4,20},{20... | collective-permute-start | bytes 1572872 | tf_op jit(solution)/shard_map/ppermute | solution.py:534
  13.6 0.5 collective-permute-start.3
  14.1 1.5 %collective-permute-start.1 = (bf16[2,16,128]{2,1,0:T(8,128)(2,1)S(1)}, bf16[2,16,128]{2,1,0:T(8,128)(2,1)S(1)}, u32[]{:S(2)}, u32[]{:S(2)}) collective-permute-start(bf16[2,16,128]{2,1,0:T(8,128)(2,1)S(1)} %copy-done.7), channel_id=1, source_target_pairs={{0,16},{16,0},{1,17},{17,1},{2,18},{18,2},{3,19},{19,3},{4,20},{20... | collective-permute-start | bytes 24584 | tf_op jit(solution)/shard_map/ppermute | solution.py:534
  15.6 0.5 collective-permute-start
  16.1 0.7 pad_add_fusion.pos_ref
  16.8 10.0 %collective-permute-done.3.refs_7_ = bf16[2,64]{1,0:T(2,128)(2,1)S(1)} collective-permute-done((bf16[2,64]{1,0:T(2,128)(2,1)S(1)}, bf16[2,64]{1,0:T(2,128)(2,1)S(1)}, u32[]{:S(2)}, u32[]{:S(2)}) %collective-permute-start.3) | collective-permute-done | bytes 288 | tf_op jit(solution)/shard_map/ppermute | solution.py:534
  27.1 0.8 copy-done.4
  27.9 3.5 %prepare.1 = (bf16[2,544,512]{2,1,0:T(8,128)(2,1)}, bf16[2,512,512]{2,1,0:T(8,128)(2,1)}, bf16[2,128,512]{2,1,0:T(8,128)(2,1)}, bf16[2,512,128]{2,1,0:T(8,128)(2...) custom-call(s32[2]{0:T(128)} %pad_add_fusion.pos_ref, s32[1,512]{1,0:T(1,128)} %bitcast.58, ...), custom_call_target="tpu_custom_call" | custom-call | tf_op jit(solution)/shard_map/prepare/pallas_call | solution.py:157
  31.4 3.5 %all-to-all-done.recv_hbm = bf16[16,256,128]{2,1,0:T(8,128)(2,1)} async-done(((bf16[16,256,128]{2,1,0:T(8,128)(2,1)}), bf16[16,256,128]{2,1,0:T(8,128)(2,1)}, u32[]{:S(2)}, u32[]{:S(2)}) %all-to-all-start) | async-done | bytes 1048608 | tf_op jit(solution)/shard_map/all_to_all | solution.py:486
  35.0 12.8 %layers.1 = (bf16[8,512,128]{2,1,0:T(8,128)(2,1)}, bf16[16,256,128]{2,1,0:T(8,128)(2,1)}, bf16[16,144,128]{2,1,0:T(8,128)(2,1)}, bf16[16,144,128]{2,1,0:T(8,128)(2,1)}) custom-call(s32[2]{0:T(128)} %pad_add_fusion.pos_ref, f32[2,128]{1,0:T(2,128)} %get-tuple-element.30.gain_ref, s32[1,512]{1,0:T(1,128)} %bitcast.59, ...), custom_call_target="tpu_custom_call" | custom-call | tf_op jit(solution)/shard_map/layers/pallas_call | solution.py:406
  47.8 0.7 collective-permute-start.4
  48.5 6.6 %all-to-all-start.1 = ((bf16[16,256,128]{2,1,0:T(8,128)(2,1)}), bf16[16,256,128]{2,1,0:T(8,128)(2,1)S(1)}, u32[]{:S(2)}, u32[]{:S(2)}) async-start(bf16[16,256,128]{2,1,0:T(8,128)(2,1)} %get-tuple-element.40), calls=%async_computation.1 | async-start | bytes 2097152 | tf_op jit(solution)/shard_map/all_to_all | solution.py:486
  55.3 1.6 %collective-permute-start.5 = (bf16[2,4,144,128]{3,2,1,0:T(8,128)(2,1)S(1)}, bf16[2,4,144,128]{3,2,1,0:T(8,128)(2,1)S(1)}, u32[]{:S(2)}, u32[]{:S(2)}) collective-permute-start(bf16[2,4,144,128]{3,2,1,0:T(8,128)(2,1)S(1)} %get-tuple-element.55), channel_id=1, source_target_pairs={{0,16},{1,17},{2,18},{3,19},{4,20},{5,21},{6,22},{7,23},{8,24},{9,... | collective-permute-start | bytes 884744 | tf_op jit(solution)/shard_map/ppermute | solution.py:436
  56.9 7.8 %collective-permute-done.5 = bf16[2,4,144,128]{3,2,1,0:T(8,128)(2,1)S(1)} collective-permute-done((bf16[2,4,144,128]{3,2,1,0:T(8,128)(2,1)S(1)}, bf16[2,4,144,128]{3,2,1,0:T(8,128)(2,1)S(1)}, u32[]{:S(2)}, u32[]{:S(2)}) %collective-permute-start.5) | collective-permute-done | bytes 294944 | tf_op jit(solution)/shard_map/ppermute | solution.py:436
  64.8 1.7 %collective-permute-start.6 = (bf16[4,144,128]{2,1,0:T(8,128)(2,1)S(1)}, bf16[4,144,128]{2,1,0:T(8,128)(2,1)S(1)}, u32[]{:S(2)}, u32[]{:S(2)}) collective-permute-start(bf16[4,144,128]{2,1,0:T(8,128)(2,1)S(1)} %get-tuple-element.57), channel_id=1, source_target_pairs={{0,2},{1,3},{2,0},{3,1},{4,6},{5,7},{6,4},{7,5},{8,10},{9,11},{10,... | collective-permute-start | bytes 442376 | tf_op jit(solution)/shard_map/ppermute | solution.py:436
  66.5 6.1 %collective-permute-done.6 = bf16[4,144,128]{2,1,0:T(8,128)(2,1)S(1)} collective-permute-done((bf16[4,144,128]{2,1,0:T(8,128)(2,1)S(1)}, bf16[4,144,128]{2,1,0:T(8,128)(2,1)S(1)}, u32[]{:S(2)}, u32[]{:S(2)}) %collective-permute-start.6) | collective-permute-done | bytes 147488 | tf_op jit(solution)/shard_map/ppermute | solution.py:436
  72.6 1.2 %collective-permute-start.7 = (bf16[1,144,128]{2,1,0:T(8,128)(2,1)S(1)}, bf16[1,144,128]{2,1,0:T(8,128)(2,1)S(1)}, u32[]{:S(2)}, u32[]{:S(2)}) collective-permute-start(bf16[1,144,128]{2,1,0:T(8,128)(2,1)S(1)} %get-tuple-element.58), channel_id=1, source_target_pairs={{0,4},{1,5},{2,6},{3,7},{4,0},{5,1},{6,2},{7,3},{8,12},{9,13},{10,... | collective-permute-start | bytes 110600 | tf_op jit(solution)/shard_map/ppermute | solution.py:436
  73.8 2.3 %collective-permute-start.9 = (bf16[1,144,128]{2,1,0:T(8,128)(2,1)S(1)}, bf16[1,144,128]{2,1,0:T(8,128)(2,1)S(1)}, u32[]{:S(2)}, u32[]{:S(2)}) collective-permute-start(bf16[1,144,128]{2,1,0:T(8,128)(2,1)S(1)} %get-tuple-element.59), channel_id=1, source_target_pairs={{0,12},{1,13},{2,14},{3,15},{4,8},{5,9},{6,10},{7,11},{8,4},{9,5},... | collective-permute-start | bytes 110600 | tf_op jit(solution)/shard_map/ppermute | solution.py:436
  76.6 1.8 %collective-permute-done.7 = bf16[1,144,128]{2,1,0:T(8,128)(2,1)S(1)} collective-permute-done((bf16[1,144,128]{2,1,0:T(8,128)(2,1)S(1)}, bf16[1,144,128]{2,1,0:T(8,128)(2,1)S(1)}, u32[]{:S(2)}, u32[]{:S(2)}) %collective-permute-start.7) | collective-permute-done | bytes 36896 | tf_op jit(solution)/shard_map/ppermute | solution.py:436
  78.4 1.3 %collective-permute-done.9 = bf16[1,144,128]{2,1,0:T(8,128)(2,1)S(1)} collective-permute-done((bf16[1,144,128]{2,1,0:T(8,128)(2,1)S(1)}, bf16[1,144,128]{2,1,0:T(8,128)(2,1)S(1)}, u32[]{:S(2)}, u32[]{:S(2)}) %collective-permute-start.9) | collective-permute-done | bytes 36896 | tf_op jit(solution)/shard_map/ppermute | solution.py:436
  79.6 5.2 %collective-permute-done.8 = bf16[1,144,128]{2,1,0:T(8,128)(2,1)S(1)} collective-permute-done((bf16[1,144,128]{2,1,0:T(8,128)(2,1)S(1)}, bf16[1,144,128]{2,1,0:T(8,128)(2,1)S(1)}, u32[]{:S(2)}, u32[]{:S(2)}) %collective-permute-start.8) | collective-permute-done | bytes 36896 | tf_op jit(solution)/shard_map/ppermute | solution.py:436
  84.9 1.5 %collective-permute-start.12 = (bf16[1,144,128]{2,1,0:T(8,128)(2,1)S(1)}, bf16[1,144,128]{2,1,0:T(8,128)(2,1)S(1)}, u32[]{:S(2)}, u32[]{:S(2)}) collective-permute-start(bf16[1,144,128]{2,1,0:T(8,128)(2,1)S(1)} %add_convert_fusion.2), channel_id=1, source_target_pairs={{0,12},{1,13},{2,14},{3,15},{4,8},{5,9},{6,10},{7,11},{8,4},{9,5},... | collective-permute-start | bytes 110600 | tf_op jit(solution)/shard_map/ppermute | solution.py:436
  86.6 2.8 %collective-permute-start.10 = (bf16[1,144,128]{2,1,0:T(8,128)(2,1)S(1)}, bf16[1,144,128]{2,1,0:T(8,128)(2,1)S(1)}, u32[]{:S(2)}, u32[]{:S(2)}) collective-permute-start(bf16[1,144,128]{2,1,0:T(8,128)(2,1)S(1)} %add_convert_fusion.2), channel_id=1, source_target_pairs={{0,4},{1,5},{2,6},{3,7},{4,0},{5,1},{6,2},{7,3},{8,12},{9,13},{10,... | collective-permute-start | bytes 110600 | tf_op jit(solution)/shard_map/ppermute | solution.py:436
  89.3 1.6 %collective-permute-done.12 = bf16[1,144,128]{2,1,0:T(8,128)(2,1)S(1)} collective-permute-done((bf16[1,144,128]{2,1,0:T(8,128)(2,1)S(1)}, bf16[1,144,128]{2,1,0:T(8,128)(2,1)S(1)}, u32[]{:S(2)}, u32[]{:S(2)}) %collective-permute-start.12) | collective-permute-done | bytes 36896 | tf_op jit(solution)/shard_map/ppermute | solution.py:436
  90.9 0.8 collective-permute-done.11
  91.7 1.5 %collective-permute-start.13 = (bf16[4,144,128]{2,1,0:T(8,128)(2,1)S(1)}, bf16[4,144,128]{2,1,0:T(8,128)(2,1)S(1)}, u32[]{:S(2)}, u32[]{:S(2)}) collective-permute-start(bf16[4,144,128]{2,1,0:T(8,128)(2,1)S(1)} %pad_maximum_fusion.refs_0_), channel_id=1, source_target_pairs={{0,2},{1,3},{2,0},{3,1},{4,6},{5,7},{6,4},{7,5},{8,10},{9,11},{10,... | collective-permute-start | bytes 442376 | tf_op jit(solution)/shard_map/ppermute | solution.py:436
  93.3 2.7 %expand.1 = bf16[4608,128]{1,0:T(8,128)(2,1)} custom-call(s32[1,4608]{1,0:T(1,128)S(1)} %bitcast.49, bf16[4096,128]{1,0:T(8,128)(2,1)S(1)} %bitcast.47), custom_call_target="tpu_custom_call" | custom-call | tf_op jit(solution)/shard_map/expand/pallas_call | solution.py:101
  95.9 1.0 collective-permute-done.13.refs_1_
  96.9 1.4 %collective-permute-done.15.refs_3_ = bf16[4,144,128]{2,1,0:T(8,128)(2,1)S(1)} collective-permute-done((bf16[4,144,128]{2,1,0:T(8,128)(2,1)S(1)}, bf16[4,144,128]{2,1,0:T(8,128)(2,1)S(1)}, u32[]{:S(2)}, u32[]{:S(2)}) %collective-permute-start.15) | collective-permute-done | bytes 147488 | tf_op jit(solution)/shard_map/ppermute | solution.py:436
  98.3 1.6 %finish.1 = (f32[2,256,512]{2,1,0:T(8,128)}, f32[2,32,256]{2,1,0:T(8,128)}, f32[2,16,128]{2,1,0:T(8,128)}, f32[2,64]{1,0:T(2,128)}) custom-call(s32[2]{0:T(128)S(1)} %copy-done.1, bf16[4,144,128]{2,1,0:T(8,128)(2,1)S(1)} %pad_maximum_fusion.refs_0_, bf16[4,144,128]{2,1,0:T(8,128)(2,1)S(1)} %collective-permute-done.13.refs_1_, ...), custom_call_target="tpu_custom_call" | custom-call | tf_op jit(solution)/shard_map/finish/pallas_call | solution.py:469
  (37 shorter events, 1.5 us)
Async XLA Ops:
  4.4 7.6 %copy-start.3 = (bf16[2,256,512]{2,1,0:T(8,128)(2,1)S(1)}, bf16[2,256,512]{2,1,0:T(8,128)(2,1)}, u32[]{:S(2)}) copy-start(bf16[2,256,512]{2,1,0:T(8,128)(2,1)} %refs_4_.1) | copy-start | bytes 1572868
  4.4 9.2 %copy-start.9 = (bf16[2,64]{1,0:T(2,128)(2,1)S(1)}, bf16[2,64]{1,0:T(2,128)(2,1)}, u32[]{:S(2)}) copy-start(bf16[2,64]{1,0:T(2,128)(2,1)} %refs_6_.1) | copy-start | bytes 772
  4.4 9.7 %copy-start.7 = (bf16[2,16,128]{2,1,0:T(8,128)(2,1)S(1)}, bf16[2,16,128]{2,1,0:T(8,128)(2,1)}, u32[]{:S(2)}) copy-start(bf16[2,16,128]{2,1,0:T(8,128)(2,1)} %refs_2_.1) | copy-start | bytes 24580
  4.4 11.2 %copy-start.5 = (bf16[2,256,32]{1,2,0:T(8,128)(2,1)S(1)}, bf16[2,256,32]{1,2,0:T(8,128)(2,1)}, u32[]{:S(2)}) copy-start(bf16[2,256,32]{1,2,0:T(8,128)(2,1)} %param.13) | copy-start | bytes 98308
  4.4 30.6 %all-to-all-start = ((bf16[16,256,128]{2,1,0:T(8,128)(2,1)}), bf16[16,256,128]{2,1,0:T(8,128)(2,1)}, u32[]{:S(2)}, u32[]{:S(2)}) async-start(bf16[16,256,128]{2,1,0:T(8,128)(2,1)} %bitcast.50), calls=%async_computation | async-start | bytes 2097152 | tf_op jit(solution)/shard_map/all_to_all | solution.py:486
  12.0 15.1 %collective-permute-start.2 = (bf16[2,256,512]{2,1,0:T(8,128)(2,1)S(1)}, bf16[2,256,512]{2,1,0:T(8,128)(2,1)S(1)}, u32[]{:S(2)}, u32[]{:S(2)}) collective-permute-start(bf16[2,256,512]{2,1,0:T(8,128)(2,1)S(1)} %copy-done.3), channel_id=1, source_target_pairs={{0,16},{16,0},{1,17},{17,1},{2,18},{18,2},{3,19},{19,3},{4,20},{20... | collective-permute-start | bytes 1572872 | tf_op jit(solution)/shard_map/ppermute | solution.py:534
  13.6 13.2 %collective-permute-start.3 = (bf16[2,64]{1,0:T(2,128)(2,1)S(1)}, bf16[2,64]{1,0:T(2,128)(2,1)S(1)}, u32[]{:S(2)}, u32[]{:S(2)}) collective-permute-start(bf16[2,64]{1,0:T(2,128)(2,1)S(1)} %copy-done.9), channel_id=1, source_target_pairs={{0,16},{16,0},{1,17},{17,1},{2,18},{18,2},{3,19},{19,3},{4,20},{20... | collective-permute-start | bytes 776 | tf_op jit(solution)/shard_map/ppermute | solution.py:534
  14.1 12.7 %collective-permute-start.1 = (bf16[2,16,128]{2,1,0:T(8,128)(2,1)S(1)}, bf16[2,16,128]{2,1,0:T(8,128)(2,1)S(1)}, u32[]{:S(2)}, u32[]{:S(2)}) collective-permute-start(bf16[2,16,128]{2,1,0:T(8,128)(2,1)S(1)} %copy-done.7), channel_id=1, source_target_pairs={{0,16},{16,0},{1,17},{17,1},{2,18},{18,2},{3,19},{19,3},{4,20},{20... | collective-permute-start | bytes 24584 | tf_op jit(solution)/shard_map/ppermute | solution.py:534
  15.6 11.5 %collective-permute-start = (bf16[2,32,256]{2,1,0:T(8,128)(2,1)S(1)}, bf16[2,32,256]{2,1,0:T(8,128)(2,1)S(1)}, u32[]{:S(2)}, u32[]{:S(2)}) collective-permute-start(bf16[2,32,256]{2,1,0:T(8,128)(2,1)S(1)} %bitcast.56), channel_id=1, source_target_pairs={{0,16},{16,0},{1,17},{17,1},{2,18},{18,2},{3,19},{19,3},{4,20},{20... | collective-permute-start | bytes 98312 | tf_op jit(solution)/shard_map/ppermute | solution.py:534
  26.7 1.2 %copy-start.10 = (bf16[2,64]{1,0:T(2,128)(2,1)}, bf16[2,64]{1,0:T(2,128)(2,1)S(1)}, u32[]{:S(2)}) copy-start(bf16[2,64]{1,0:T(2,128)(2,1)S(1)} %collective-permute-done.3.refs_7_) | copy-start | bytes 772
  26.8 1.2 %copy-start.8 = (bf16[2,16,128]{2,1,0:T(8,128)(2,1)}, bf16[2,16,128]{2,1,0:T(8,128)(2,1)S(1)}, u32[]{:S(2)}) copy-start(bf16[2,16,128]{2,1,0:T(8,128)(2,1)S(1)} %collective-permute-done.1.refs_3_) | copy-start | bytes 24580
  27.1 0.8 copy-start.6
  27.1 0.8 copy-start.4
  47.8 7.3 %copy-start.2 = (bf16[16,144,128]{2,1,0:T(8,128)(2,1)S(1)}, bf16[16,144,128]{2,1,0:T(8,128)(2,1)}, u32[]{:S(2)}) copy-start(bf16[16,144,128]{2,1,0:T(8,128)(2,1)} %get-tuple-element.38) | copy-start | bytes 1769476
  47.8 7.2 %collective-permute-start.4 = (bf16[16,144,128]{2,1,0:T(8,128)(2,1)}, bf16[16,144,128]{2,1,0:T(8,128)(2,1)S(1)}, u32[]{:S(2)}, u32[]{:S(2)}) collective-permute-start(bf16[16,144,128]{2,1,0:T(8,128)(2,1)} %get-tuple-element.39), channel_id=1, source_target_pairs={{0,1},{1,0},{2,3},{3,2},{4,5},{5,4},{6,7},{7,6},{8,9},{9,8},{10,11... | collective-permute-start | bytes 1769480 | tf_op jit(solution)/shard_map/ppermute | solution.py:436
  48.5 43.2 %all-to-all-start.1 = ((bf16[16,256,128]{2,1,0:T(8,128)(2,1)}), bf16[16,256,128]{2,1,0:T(8,128)(2,1)S(1)}, u32[]{:S(2)}, u32[]{:S(2)}) async-start(bf16[16,256,128]{2,1,0:T(8,128)(2,1)} %get-tuple-element.40), calls=%async_computation.1 | async-start | bytes 2097152 | tf_op jit(solution)/shard_map/all_to_all | solution.py:486
  55.3 38.0 %copy-start = (s32[1,1,4608]{2,1,0:T(1,128)S(1)}, s32[1,1,4608]{2,1,0:T(1,128)}, u32[]{:S(2)}) copy-start(s32[1,1,4608]{2,1,0:T(1,128)} %param.10) | copy-start | bytes 55300
  55.3 9.4 %collective-permute-start.5 = (bf16[2,4,144,128]{3,2,1,0:T(8,128)(2,1)S(1)}, bf16[2,4,144,128]{3,2,1,0:T(8,128)(2,1)S(1)}, u32[]{:S(2)}, u32[]{:S(2)}) collective-permute-start(bf16[2,4,144,128]{3,2,1,0:T(8,128)(2,1)S(1)} %get-tuple-element.55), channel_id=1, source_target_pairs={{0,16},{1,17},{2,18},{3,19},{4,20},{5,21},{6,22},{7,23},{8,24},{9,... | collective-permute-start | bytes 884744 | tf_op jit(solution)/shard_map/ppermute | solution.py:436
  64.8 7.8 %collective-permute-start.6 = (bf16[4,144,128]{2,1,0:T(8,128)(2,1)S(1)}, bf16[4,144,128]{2,1,0:T(8,128)(2,1)S(1)}, u32[]{:S(2)}, u32[]{:S(2)}) collective-permute-start(bf16[4,144,128]{2,1,0:T(8,128)(2,1)S(1)} %get-tuple-element.57), channel_id=1, source_target_pairs={{0,2},{1,3},{2,0},{3,1},{4,6},{5,7},{6,4},{7,5},{8,10},{9,11},{10,... | collective-permute-start | bytes 442376 | tf_op jit(solution)/shard_map/ppermute | solution.py:436
  72.6 5.8 %collective-permute-start.7 = (bf16[1,144,128]{2,1,0:T(8,128)(2,1)S(1)}, bf16[1,144,128]{2,1,0:T(8,128)(2,1)S(1)}, u32[]{:S(2)}, u32[]{:S(2)}) collective-permute-start(bf16[1,144,128]{2,1,0:T(8,128)(2,1)S(1)} %get-tuple-element.58), channel_id=1, source_target_pairs={{0,4},{1,5},{2,6},{3,7},{4,0},{5,1},{6,2},{7,3},{8,12},{9,13},{10,... | collective-permute-start | bytes 110600 | tf_op jit(solution)/shard_map/ppermute | solution.py:436
  73.8 5.9 %collective-permute-start.9 = (bf16[1,144,128]{2,1,0:T(8,128)(2,1)S(1)}, bf16[1,144,128]{2,1,0:T(8,128)(2,1)S(1)}, u32[]{:S(2)}, u32[]{:S(2)}) collective-permute-start(bf16[1,144,128]{2,1,0:T(8,128)(2,1)S(1)} %get-tuple-element.59), channel_id=1, source_target_pairs={{0,12},{1,13},{2,14},{3,15},{4,8},{5,9},{6,10},{7,11},{8,4},{9,5},... | collective-permute-start | bytes 110600 | tf_op jit(solution)/shard_map/ppermute | solution.py:436
  76.1 8.7 %collective-permute-start.8 = (bf16[1,144,128]{2,1,0:T(8,128)(2,1)S(1)}, bf16[1,144,128]{2,1,0:T(8,128)(2,1)S(1)}, u32[]{:S(2)}, u32[]{:S(2)}) collective-permute-start(bf16[1,144,128]{2,1,0:T(8,128)(2,1)S(1)} %get-tuple-element.60), channel_id=1, source_target_pairs={{0,8},{1,9},{2,10},{3,11},{4,12},{5,13},{6,14},{7,15},{8,0},{9,1},... | collective-permute-start | bytes 110600 | tf_op jit(solution)/shard_map/ppermute | solution.py:436
  84.9 6.0 %collective-permute-start.12 = (bf16[1,144,128]{2,1,0:T(8,128)(2,1)S(1)}, bf16[1,144,128]{2,1,0:T(8,128)(2,1)S(1)}, u32[]{:S(2)}, u32[]{:S(2)}) collective-permute-start(bf16[1,144,128]{2,1,0:T(8,128)(2,1)S(1)} %add_convert_fusion.2), channel_id=1, source_target_pairs={{0,12},{1,13},{2,14},{3,15},{4,8},{5,9},{6,10},{7,11},{8,4},{9,5},... | collective-permute-start | bytes 110600 | tf_op jit(solution)/shard_map/ppermute | solution.py:436
  86.3 5.3 %collective-permute-start.11 = (bf16[1,144,128]{2,1,0:T(8,128)(2,1)S(1)}, bf16[1,144,128]{2,1,0:T(8,128)(2,1)S(1)}, u32[]{:S(2)}, u32[]{:S(2)}) collective-permute-start(bf16[1,144,128]{2,1,0:T(8,128)(2,1)S(1)} %add_convert_fusion.2), channel_id=1, source_target_pairs={{0,8},{1,9},{2,10},{3,11},{4,12},{5,13},{6,14},{7,15},{8,0},{9,1},... | collective-permute-start | bytes 110600 | tf_op jit(solution)/shard_map/ppermute | solution.py:436
  86.6 5.1 %collective-permute-start.10 = (bf16[1,144,128]{2,1,0:T(8,128)(2,1)S(1)}, bf16[1,144,128]{2,1,0:T(8,128)(2,1)S(1)}, u32[]{:S(2)}, u32[]{:S(2)}) collective-permute-start(bf16[1,144,128]{2,1,0:T(8,128)(2,1)S(1)} %add_convert_fusion.2), channel_id=1, source_target_pairs={{0,4},{1,5},{2,6},{3,7},{4,0},{5,1},{6,2},{7,3},{8,12},{9,13},{10,... | collective-permute-start | bytes 110600 | tf_op jit(solution)/shard_map/ppermute | solution.py:436
  91.7 6.6 %copy-start.1 = (s32[2]{0:T(128)S(1)}, s32[2]{0:T(128)}, u32[]{:S(2)}) copy-start(s32[2]{0:T(128)} %pad_add_fusion.pos_ref) | copy-start | bytes 28
  91.7 5.2 %collective-permute-start.13 = (bf16[4,144,128]{2,1,0:T(8,128)(2,1)S(1)}, bf16[4,144,128]{2,1,0:T(8,128)(2,1)S(1)}, u32[]{:S(2)}, u32[]{:S(2)}) collective-permute-start(bf16[4,144,128]{2,1,0:T(8,128)(2,1)S(1)} %pad_maximum_fusion.refs_0_), channel_id=1, source_target_pairs={{0,2},{1,3},{2,0},{3,1},{4,6},{5,7},{6,4},{7,5},{8,10},{9,11},{10,... | collective-permute-start | bytes 442376 | tf_op jit(solution)/shard_map/ppermute | solution.py:436
  93.2 3.7 %collective-permute-start.14 = (bf16[4,144,128]{2,1,0:T(8,128)(2,1)S(1)}, bf16[4,144,128]{2,1,0:T(8,128)(2,1)S(1)}, u32[]{:S(2)}, u32[]{:S(2)}) collective-permute-start(bf16[4,144,128]{2,1,0:T(8,128)(2,1)S(1)} %pad_maximum_fusion.refs_0_), channel_id=1, source_target_pairs={{0,1},{1,0},{2,3},{3,2},{4,5},{5,4},{6,7},{7,6},{8,9},{9,8},{10,11... | collective-permute-start | bytes 442376 | tf_op jit(solution)/shard_map/ppermute | solution.py:436
  96.9 1.4 %collective-permute-start.15 = (bf16[4,144,128]{2,1,0:T(8,128)(2,1)S(1)}, bf16[4,144,128]{2,1,0:T(8,128)(2,1)S(1)}, u32[]{:S(2)}, u32[]{:S(2)}) collective-permute-start(bf16[4,144,128]{2,1,0:T(8,128)(2,1)S(1)} %collective-permute-done.13.refs_1_), channel_id=1, source_target_pairs={{0,1},{1,0},{2,3},{3,2},{4,5},{5,4},{6,7},{7,6},{8,9},{9,8},{10,11... | collective-permute-start | bytes 442376 | tf_op jit(solution)/shard_map/ppermute | solution.py:436

commit v7 on v6

--- a/solution.py
+++ b/solution.py
@@ -495,9 +495,11 @@
     to_x, own = (added([part[rx] for part in both]) for rx in (1, 0))
     parts = [own, across(to_x, 0, 2)]
     owner = exchange(slots)
-    quarters = [added([part[r : r + 1] for part in parts]) for r in range(4)]
-    parts = [quarters[0]] + [across(quarters[r], 0, 4 * r) for r in range(1, 4)]
-    piece = added(parts)
+    both = [part.reshape(2, 2, PIECE, E) for part in parts]
+    to_near, own = (added([part[:, near] for part in both]) for near in (1, 0))
+    both = [own, across(to_near, 0, 4)]
+    to_far, own = (added([part[far : far + 1] for part in both]) for far in (1, 0))
+    piece = added([own, across(to_far, 0, 8)])
     column = jnp.concatenate([piece] + [across(piece, 0, 4 * r) for r in range(1, 4)], axis=0)
     column, owner = lax.optimization_barrier((column, owner))
     beside = across(column, 0, 2)

time: 100 us -> 99.8 us (level)
  starting transfers between devices: 32.1 us -> 30 us
  waiting for transfers between devices: 40.8 us -> 42.4 us
    ppermute x12 -> x11, starting transfers between devices: 13.9 us -> 11.8 us  [across(): return lax.ppermute(x, ('dp', 'mp'), pairs)]
    ppermute x12 -> x11, waiting for transfers between devices: 26.9 us -> 28.5 us  [across(): return lax.ppermute(x, ('dp', 'mp'), pairs)]
  transfers between devices with their start and end apart: 18 -> 17, of which waited for: 12 -> 12; matrix products, arithmetic and copies ran while one was open for 1% -> 1% of each run, Pallas kernels for 6% -> 6%
where the time goes in v7:
time: 99.8 us; the launch traced here: 99.5 us
  waiting for transfers between devices  42.4 us (42%)
  starting transfers between devices  30 us (30%)
  Pallas kernels  24.4 us (24%)
    ppermute x11, waiting for transfers between devices, across(): return lax.ppermute(x, ('dp', 'mp'), pairs)  28.5 us
    all_to_all x2, starting transfers between devices, exchange(): return lax.all_to_all(x, 'mp', split_axis=0, concat_axis=0, tiled=True)  14.1 us
    pallas_call x1, Pallas kernels, run_layers(): pl.pallas_call(functools.partial(layers_kernel, f_dev=f_dev, packed=packe...  12.9 us
    ppermute x11, starting transfers between devices, across(): return lax.ppermute(x, ('dp', 'mp'), pairs)  11.8 us
    ppermute x4, waiting for transfers between devices, per_device(): lax.ppermute(part, 'dp', [(0, 1), (1, 0)])  10.4 us
    ppermute x4, starting transfers between devices, per_device(): lax.ppermute(part, 'dp', [(0, 1), (1, 0)])  4.12 us
    pallas_call x1, Pallas kernels, pool(): pl.pallas_call(pool_kernel, out_shape=jax.ShapeDtypeStruct((bags, E), BF)...  3.78 us
    all_to_all x2, waiting for transfers between devices, exchange(): return lax.all_to_all(x, 'mp', split_axis=0, concat_axis=0, tiled=True)  3.53 us
  transfers between devices with their start and end apart: 17, of which 12 were waited for; matrix products, arithmetic and copies ran while one was open for 1% of the time, Pallas kernels for 6%

profile of v7, /device:TPU:0, one launch (start us, length us, event | category | flops | bytes accessed | tf_op | source)
XLA Modules:
  0.0 99.5 jit_solution(16470762482145590011)
XLA Ops:
  0.6 3.8 %pool.1 = bf16[4096,128]{1,0:T(8,128)(2,1)} custom-call(s32[1,4608]{1,0:T(1,128)} %bitcast.42, bf16[4608,128]{1,0:T(8,128)(2,1)} %bitcast.45), custom_call_target="tpu_custom_call" | custom-call | tf_op jit(solution)/shard_map/pool/pallas_call | solution.py:77
  4.4 7.6 %all-to-all-start = ((bf16[16,256,128]{2,1,0:T(8,128)(2,1)}), bf16[16,256,128]{2,1,0:T(8,128)(2,1)}, u32[]{:S(2)}, u32[]{:S(2)}) async-start(bf16[16,256,128]{2,1,0:T(8,128)(2,1)} %bitcast.44), calls=%async_computation | async-start | bytes 2097152 | tf_op jit(solution)/shard_map/all_to_all | solution.py:486
  12.0 1.6 %collective-permute-start.2 = (bf16[2,256,512]{2,1,0:T(8,128)(2,1)S(1)}, bf16[2,256,512]{2,1,0:T(8,128)(2,1)S(1)}, u32[]{:S(2)}, u32[]{:S(2)}) collective-permute-start(bf16[2,256,512]{2,1,0:T(8,128)(2,1)S(1)} %copy-done.3), channel_id=1, source_target_pairs={{0,16},{16,0},{1,17},{17,1},{2,18},{18,2},{3,19},{19,3},{4,20},{20... | collective-permute-start | bytes 1572872 | tf_op jit(solution)/shard_map/ppermute | solution.py:536
  13.6 0.5 collective-permute-start.3
  14.1 1.5 %collective-permute-start.1 = (bf16[2,16,128]{2,1,0:T(8,128)(2,1)S(1)}, bf16[2,16,128]{2,1,0:T(8,128)(2,1)S(1)}, u32[]{:S(2)}, u32[]{:S(2)}) collective-permute-start(bf16[2,16,128]{2,1,0:T(8,128)(2,1)S(1)} %copy-done.7), channel_id=1, source_target_pairs={{0,16},{16,0},{1,17},{17,1},{2,18},{18,2},{3,19},{19,3},{4,20},{20... | collective-permute-start | bytes 24584 | tf_op jit(solution)/shard_map/ppermute | solution.py:536
  15.6 0.5 collective-permute-start
  16.1 0.6 pad_add_fusion.pos_ref
  16.7 10.0 %collective-permute-done.3.refs_7_ = bf16[2,64]{1,0:T(2,128)(2,1)S(1)} collective-permute-done((bf16[2,64]{1,0:T(2,128)(2,1)S(1)}, bf16[2,64]{1,0:T(2,128)(2,1)S(1)}, u32[]{:S(2)}, u32[]{:S(2)}) %collective-permute-start.3) | collective-permute-done | bytes 288 | tf_op jit(solution)/shard_map/ppermute | solution.py:536
  26.8 0.3 collective-permute-done.refs_1_
  27.1 0.8 copy-done.4
  27.9 3.5 %prepare.1 = (bf16[2,544,512]{2,1,0:T(8,128)(2,1)}, bf16[2,512,512]{2,1,0:T(8,128)(2,1)}, bf16[2,128,512]{2,1,0:T(8,128)(2,1)}, bf16[2,512,128]{2,1,0:T(8,128)(2...) custom-call(s32[2]{0:T(128)} %pad_add_fusion.pos_ref, s32[1,512]{1,0:T(1,128)} %bitcast.54, ...), custom_call_target="tpu_custom_call" | custom-call | tf_op jit(solution)/shard_map/prepare/pallas_call | solution.py:157
  31.4 3.5 %all-to-all-done.recv_hbm = bf16[16,256,128]{2,1,0:T(8,128)(2,1)} async-done(((bf16[16,256,128]{2,1,0:T(8,128)(2,1)}), bf16[16,256,128]{2,1,0:T(8,128)(2,1)}, u32[]{:S(2)}, u32[]{:S(2)}) %all-to-all-start) | async-done | bytes 1048608 | tf_op jit(solution)/shard_map/all_to_all | solution.py:486
  35.0 12.9 %layers.1 = (bf16[8,512,128]{2,1,0:T(8,128)(2,1)}, bf16[16,256,128]{2,1,0:T(8,128)(2,1)}, bf16[16,144,128]{2,1,0:T(8,128)(2,1)}, bf16[16,144,128]{2,1,0:T(8,128)(2,1)}) custom-call(s32[2]{0:T(128)} %pad_add_fusion.pos_ref, f32[2,128]{1,0:T(2,128)} %get-tuple-element.30.gain_ref, s32[1,512]{1,0:T(1,128)} %bitcast.55, ...), custom_call_target="tpu_custom_call" | custom-call | tf_op jit(solution)/shard_map/layers/pallas_call | solution.py:406
  47.9 0.7 collective-permute-start.4
  48.5 6.6 %all-to-all-start.1 = ((bf16[16,256,128]{2,1,0:T(8,128)(2,1)}), bf16[16,256,128]{2,1,0:T(8,128)(2,1)S(1)}, u32[]{:S(2)}, u32[]{:S(2)}) async-start(bf16[16,256,128]{2,1,0:T(8,128)(2,1)} %get-tuple-element.40), calls=%async_computation.1 | async-start | bytes 2097152 | tf_op jit(solution)/shard_map/all_to_all | solution.py:486
  55.1 0.2 add_convert_fusion.1
  55.3 1.6 %collective-permute-start.5 = (bf16[2,4,144,128]{3,2,1,0:T(8,128)(2,1)S(1)}, bf16[2,4,144,128]{3,2,1,0:T(8,128)(2,1)S(1)}, u32[]{:S(2)}, u32[]{:S(2)}) collective-permute-start(bf16[2,4,144,128]{3,2,1,0:T(8,128)(2,1)S(1)} %get-tuple-element.55), channel_id=1, source_target_pairs={{0,16},{1,17},{2,18},{3,19},{4,20},{5,21},{6,22},{7,23},{8,24},{9,... | collective-permute-start | bytes 884744 | tf_op jit(solution)/shard_map/ppermute | solution.py:436
  56.9 7.8 %collective-permute-done.5 = bf16[2,4,144,128]{3,2,1,0:T(8,128)(2,1)S(1)} collective-permute-done((bf16[2,4,144,128]{3,2,1,0:T(8,128)(2,1)S(1)}, bf16[2,4,144,128]{3,2,1,0:T(8,128)(2,1)S(1)}, u32[]{:S(2)}, u32[]{:S(2)}) %collective-permute-start.5) | collective-permute-done | bytes 294944 | tf_op jit(solution)/shard_map/ppermute | solution.py:436
  64.8 1.7 %collective-permute-start.6 = (bf16[4,144,128]{2,1,0:T(8,128)(2,1)S(1)}, bf16[4,144,128]{2,1,0:T(8,128)(2,1)S(1)}, u32[]{:S(2)}, u32[]{:S(2)}) collective-permute-start(bf16[4,144,128]{2,1,0:T(8,128)(2,1)S(1)} %get-tuple-element.57), channel_id=1, source_target_pairs={{0,2},{1,3},{2,0},{3,1},{4,6},{5,7},{6,4},{7,5},{8,10},{9,11},{10,... | collective-permute-start | bytes 442376 | tf_op jit(solution)/shard_map/ppermute | solution.py:436
  66.5 6.1 %collective-permute-done.6 = bf16[4,144,128]{2,1,0:T(8,128)(2,1)S(1)} collective-permute-done((bf16[4,144,128]{2,1,0:T(8,128)(2,1)S(1)}, bf16[4,144,128]{2,1,0:T(8,128)(2,1)S(1)}, u32[]{:S(2)}, u32[]{:S(2)}) %collective-permute-start.6) | collective-permute-done | bytes 147488 | tf_op jit(solution)/shard_map/ppermute | solution.py:436
  72.6 1.2 %collective-permute-start.7 = (bf16[2,144,128]{2,1,0:T(8,128)(2,1)S(1)}, bf16[2,144,128]{2,1,0:T(8,128)(2,1)S(1)}, u32[]{:S(2)}, u32[]{:S(2)}) collective-permute-start(bf16[2,144,128]{2,1,0:T(8,128)(2,1)S(1)} %get-tuple-element.59), channel_id=1, source_target_pairs={{0,4},{1,5},{2,6},{3,7},{4,0},{5,1},{6,2},{7,3},{8,12},{9,13},{10,... | collective-permute-start | bytes 221192 | tf_op jit(solution)/shard_map/ppermute | solution.py:436
  73.8 5.7 %collective-permute-done.7 = bf16[2,144,128]{2,1,0:T(8,128)(2,1)S(1)} collective-permute-done((bf16[2,144,128]{2,1,0:T(8,128)(2,1)S(1)}, bf16[2,144,128]{2,1,0:T(8,128)(2,1)S(1)}, u32[]{:S(2)}, u32[]{:S(2)}) %collective-permute-start.7) | collective-permute-done | bytes 73760 | tf_op jit(solution)/shard_map/ppermute | solution.py:436
  79.6 4.8 %collective-permute-done.8 = bf16[1,144,128]{2,1,0:T(8,128)(2,1)S(1)} collective-permute-done((bf16[1,144,128]{2,1,0:T(8,128)(2,1)S(1)}, bf16[1,144,128]{2,1,0:T(8,128)(2,1)S(1)}, u32[]{:S(2)}, u32[]{:S(2)}) %collective-permute-start.8) | collective-permute-done | bytes 36896 | tf_op jit(solution)/shard_map/ppermute | solution.py:436
  84.5 1.4 %collective-permute-start.11 = (bf16[1,144,128]{2,1,0:T(8,128)(2,1)S(1)}, bf16[1,144,128]{2,1,0:T(8,128)(2,1)S(1)}, u32[]{:S(2)}, u32[]{:S(2)}) collective-permute-start(bf16[1,144,128]{2,1,0:T(8,128)(2,1)S(1)} %add_convert_fusion.4), channel_id=1, source_target_pairs={{0,12},{1,13},{2,14},{3,15},{4,8},{5,9},{6,10},{7,11},{8,4},{9,5},... | collective-permute-start | bytes 110600 | tf_op jit(solution)/shard_map/ppermute | solution.py:436
  85.9 3.0 %collective-permute-start.9 = (bf16[1,144,128]{2,1,0:T(8,128)(2,1)S(1)}, bf16[1,144,128]{2,1,0:T(8,128)(2,1)S(1)}, u32[]{:S(2)}, u32[]{:S(2)}) collective-permute-start(bf16[1,144,128]{2,1,0:T(8,128)(2,1)S(1)} %add_convert_fusion.4), channel_id=1, source_target_pairs={{0,4},{1,5},{2,6},{3,7},{4,0},{5,1},{6,2},{7,3},{8,12},{9,13},{10,... | collective-permute-start | bytes 110600 | tf_op jit(solution)/shard_map/ppermute | solution.py:436
  88.9 1.4 %collective-permute-done.11 = bf16[1,144,128]{2,1,0:T(8,128)(2,1)S(1)} collective-permute-done((bf16[1,144,128]{2,1,0:T(8,128)(2,1)S(1)}, bf16[1,144,128]{2,1,0:T(8,128)(2,1)S(1)}, u32[]{:S(2)}, u32[]{:S(2)}) %collective-permute-start.11) | collective-permute-done | bytes 36896 | tf_op jit(solution)/shard_map/ppermute | solution.py:436
  90.3 0.9 collective-permute-done.10
  91.3 2.1 %collective-permute-start.12 = (bf16[4,144,128]{2,1,0:T(8,128)(2,1)S(1)}, bf16[4,144,128]{2,1,0:T(8,128)(2,1)S(1)}, u32[]{:S(2)}, u32[]{:S(2)}) collective-permute-start(bf16[4,144,128]{2,1,0:T(8,128)(2,1)S(1)} %pad_maximum_fusion.refs_0_), channel_id=1, source_target_pairs={{0,2},{1,3},{2,0},{3,1},{4,6},{5,7},{6,4},{7,5},{8,10},{9,11},{10,... | collective-permute-start | bytes 442376 | tf_op jit(solution)/shard_map/ppermute | solution.py:436
  93.4 2.7 %expand.1 = bf16[4608,128]{1,0:T(8,128)(2,1)} custom-call(s32[1,4608]{1,0:T(1,128)S(1)} %bitcast.43, bf16[4096,128]{1,0:T(8,128)(2,1)S(1)} %bitcast.41), custom_call_target="tpu_custom_call" | custom-call | tf_op jit(solution)/shard_map/expand/pallas_call | solution.py:101
  96.0 0.4 collective-permute-done.12.refs_1_
  96.6 1.3 %collective-permute-done.14.refs_3_ = bf16[4,144,128]{2,1,0:T(8,128)(2,1)S(1)} collective-permute-done((bf16[4,144,128]{2,1,0:T(8,128)(2,1)S(1)}, bf16[4,144,128]{2,1,0:T(8,128)(2,1)S(1)}, u32[]{:S(2)}, u32[]{:S(2)}) %collective-permute-start.14) | collective-permute-done | bytes 147488 | tf_op jit(solution)/shard_map/ppermute | solution.py:436
  97.9 1.6 %finish.1 = (f32[2,256,512]{2,1,0:T(8,128)}, f32[2,32,256]{2,1,0:T(8,128)}, f32[2,16,128]{2,1,0:T(8,128)}, f32[2,64]{1,0:T(2,128)}) custom-call(s32[2]{0:T(128)S(1)} %copy-done.1, bf16[4,144,128]{2,1,0:T(8,128)(2,1)S(1)} %pad_maximum_fusion.refs_0_, bf16[4,144,128]{2,1,0:T(8,128)(2,1)S(1)} %collective-permute-done.12.refs_1_, ...), custom_call_target="tpu_custom_call" | custom-call | tf_op jit(solution)/shard_map/finish/pallas_call | solution.py:469
  (36 shorter events, 0.5 us)
Async XLA Ops:
  4.4 7.6 %copy-start.3 = (bf16[2,256,512]{2,1,0:T(8,128)(2,1)S(1)}, bf16[2,256,512]{2,1,0:T(8,128)(2,1)}, u32[]{:S(2)}) copy-start(bf16[2,256,512]{2,1,0:T(8,128)(2,1)} %refs_4_.1) | copy-start | bytes 1572868
  4.4 9.2 %copy-start.9 = (bf16[2,64]{1,0:T(2,128)(2,1)S(1)}, bf16[2,64]{1,0:T(2,128)(2,1)}, u32[]{:S(2)}) copy-start(bf16[2,64]{1,0:T(2,128)(2,1)} %refs_6_.1) | copy-start | bytes 772
  4.4 9.7 %copy-start.7 = (bf16[2,16,128]{2,1,0:T(8,128)(2,1)S(1)}, bf16[2,16,128]{2,1,0:T(8,128)(2,1)}, u32[]{:S(2)}) copy-start(bf16[2,16,128]{2,1,0:T(8,128)(2,1)} %refs_2_.1) | copy-start | bytes 24580
  4.4 11.2 %copy-start.5 = (bf16[2,256,32]{1,2,0:T(8,128)(2,1)S(1)}, bf16[2,256,32]{1,2,0:T(8,128)(2,1)}, u32[]{:S(2)}) copy-start(bf16[2,256,32]{1,2,0:T(8,128)(2,1)} %param.13) | copy-start | bytes 98308
  4.4 30.6 %all-to-all-start = ((bf16[16,256,128]{2,1,0:T(8,128)(2,1)}), bf16[16,256,128]{2,1,0:T(8,128)(2,1)}, u32[]{:S(2)}, u32[]{:S(2)}) async-start(bf16[16,256,128]{2,1,0:T(8,128)(2,1)} %bitcast.44), calls=%async_computation | async-start | bytes 2097152 | tf_op jit(solution)/shard_map/all_to_all | solution.py:486
  12.0 15.1 %collective-permute-start.2 = (bf16[2,256,512]{2,1,0:T(8,128)(2,1)S(1)}, bf16[2,256,512]{2,1,0:T(8,128)(2,1)S(1)}, u32[]{:S(2)}, u32[]{:S(2)}) collective-permute-start(bf16[2,256,512]{2,1,0:T(8,128)(2,1)S(1)} %copy-done.3), channel_id=1, source_target_pairs={{0,16},{16,0},{1,17},{17,1},{2,18},{18,2},{3,19},{19,3},{4,20},{20... | collective-permute-start | bytes 1572872 | tf_op jit(solution)/shard_map/ppermute | solution.py:536
  13.6 13.2 %collective-permute-start.3 = (bf16[2,64]{1,0:T(2,128)(2,1)S(1)}, bf16[2,64]{1,0:T(2,128)(2,1)S(1)}, u32[]{:S(2)}, u32[]{:S(2)}) collective-permute-start(bf16[2,64]{1,0:T(2,128)(2,1)S(1)} %copy-done.9), channel_id=1, source_target_pairs={{0,16},{16,0},{1,17},{17,1},{2,18},{18,2},{3,19},{19,3},{4,20},{20... | collective-permute-start | bytes 776 | tf_op jit(solution)/shard_map/ppermute | solution.py:536
  14.1 12.7 %collective-permute-start.1 = (bf16[2,16,128]{2,1,0:T(8,128)(2,1)S(1)}, bf16[2,16,128]{2,1,0:T(8,128)(2,1)S(1)}, u32[]{:S(2)}, u32[]{:S(2)}) collective-permute-start(bf16[2,16,128]{2,1,0:T(8,128)(2,1)S(1)} %copy-done.7), channel_id=1, source_target_pairs={{0,16},{16,0},{1,17},{17,1},{2,18},{18,2},{3,19},{19,3},{4,20},{20... | collective-permute-start | bytes 24584 | tf_op jit(solution)/shard_map/ppermute | solution.py:536
  15.6 11.5 %collective-permute-start = (bf16[2,32,256]{2,1,0:T(8,128)(2,1)S(1)}, bf16[2,32,256]{2,1,0:T(8,128)(2,1)S(1)}, u32[]{:S(2)}, u32[]{:S(2)}) collective-permute-start(bf16[2,32,256]{2,1,0:T(8,128)(2,1)S(1)} %bitcast.52), channel_id=1, source_target_pairs={{0,16},{16,0},{1,17},{17,1},{2,18},{18,2},{3,19},{19,3},{4,20},{20... | collective-permute-start | bytes 98312 | tf_op jit(solution)/shard_map/ppermute | solution.py:536
  26.7 1.2 %copy-start.10 = (bf16[2,64]{1,0:T(2,128)(2,1)}, bf16[2,64]{1,0:T(2,128)(2,1)S(1)}, u32[]{:S(2)}) copy-start(bf16[2,64]{1,0:T(2,128)(2,1)S(1)} %collective-permute-done.3.refs_7_) | copy-start | bytes 772
  26.8 1.2 %copy-start.8 = (bf16[2,16,128]{2,1,0:T(8,128)(2,1)}, bf16[2,16,128]{2,1,0:T(8,128)(2,1)S(1)}, u32[]{:S(2)}) copy-start(bf16[2,16,128]{2,1,0:T(8,128)(2,1)S(1)} %collective-permute-done.1.refs_3_) | copy-start | bytes 24580
  27.1 0.8 copy-start.6
  27.1 0.8 copy-start.4
  47.8 7.3 %copy-start.2 = (bf16[16,144,128]{2,1,0:T(8,128)(2,1)S(1)}, bf16[16,144,128]{2,1,0:T(8,128)(2,1)}, u32[]{:S(2)}) copy-start(bf16[16,144,128]{2,1,0:T(8,128)(2,1)} %get-tuple-element.38) | copy-start | bytes 1769476
  47.9 7.2 %collective-permute-start.4 = (bf16[16,144,128]{2,1,0:T(8,128)(2,1)}, bf16[16,144,128]{2,1,0:T(8,128)(2,1)S(1)}, u32[]{:S(2)}, u32[]{:S(2)}) collective-permute-start(bf16[16,144,128]{2,1,0:T(8,128)(2,1)} %get-tuple-element.39), channel_id=1, source_target_pairs={{0,1},{1,0},{2,3},{3,2},{4,5},{5,4},{6,7},{7,6},{8,9},{9,8},{10,11... | collective-permute-start | bytes 1769480 | tf_op jit(solution)/shard_map/ppermute | solution.py:436
  48.5 42.8 %all-to-all-start.1 = ((bf16[16,256,128]{2,1,0:T(8,128)(2,1)}), bf16[16,256,128]{2,1,0:T(8,128)(2,1)S(1)}, u32[]{:S(2)}, u32[]{:S(2)}) async-start(bf16[16,256,128]{2,1,0:T(8,128)(2,1)} %get-tuple-element.40), calls=%async_computation.1 | async-start | bytes 2097152 | tf_op jit(solution)/shard_map/all_to_all | solution.py:486
  55.3 38.1 %copy-start = (s32[1,1,4608]{2,1,0:T(1,128)S(1)}, s32[1,1,4608]{2,1,0:T(1,128)}, u32[]{:S(2)}) copy-start(s32[1,1,4608]{2,1,0:T(1,128)} %param.10) | copy-start | bytes 55300
  55.3 9.4 %collective-permute-start.5 = (bf16[2,4,144,128]{3,2,1,0:T(8,128)(2,1)S(1)}, bf16[2,4,144,128]{3,2,1,0:T(8,128)(2,1)S(1)}, u32[]{:S(2)}, u32[]{:S(2)}) collective-permute-start(bf16[2,4,144,128]{3,2,1,0:T(8,128)(2,1)S(1)} %get-tuple-element.55), channel_id=1, source_target_pairs={{0,16},{1,17},{2,18},{3,19},{4,20},{5,21},{6,22},{7,23},{8,24},{9,... | collective-permute-start | bytes 884744 | tf_op jit(solution)/shard_map/ppermute | solution.py:436
  64.8 7.8 %collective-permute-start.6 = (bf16[4,144,128]{2,1,0:T(8,128)(2,1)S(1)}, bf16[4,144,128]{2,1,0:T(8,128)(2,1)S(1)}, u32[]{:S(2)}, u32[]{:S(2)}) collective-permute-start(bf16[4,144,128]{2,1,0:T(8,128)(2,1)S(1)} %get-tuple-element.57), channel_id=1, source_target_pairs={{0,2},{1,3},{2,0},{3,1},{4,6},{5,7},{6,4},{7,5},{8,10},{9,11},{10,... | collective-permute-start | bytes 442376 | tf_op jit(solution)/shard_map/ppermute | solution.py:436
  72.6 6.9 %collective-permute-start.7 = (bf16[2,144,128]{2,1,0:T(8,128)(2,1)S(1)}, bf16[2,144,128]{2,1,0:T(8,128)(2,1)S(1)}, u32[]{:S(2)}, u32[]{:S(2)}) collective-permute-start(bf16[2,144,128]{2,1,0:T(8,128)(2,1)S(1)} %get-tuple-element.59), channel_id=1, source_target_pairs={{0,4},{1,5},{2,6},{3,7},{4,0},{5,1},{6,2},{7,3},{8,12},{9,13},{10,... | collective-permute-start | bytes 221192 | tf_op jit(solution)/shard_map/ppermute | solution.py:436
  79.5 4.9 %collective-permute-start.8 = (bf16[1,144,128]{2,1,0:T(8,128)(2,1)S(1)}, bf16[1,144,128]{2,1,0:T(8,128)(2,1)S(1)}, u32[]{:S(2)}, u32[]{:S(2)}) collective-permute-start(bf16[1,144,128]{2,1,0:T(8,128)(2,1)S(1)} %fusion.5), channel_id=1, source_target_pairs={{0,8},{1,9},{2,10},{3,11},{4,12},{5,13},{6,14},{7,15},{8,0},{9,1},... | collective-permute-start | bytes 110600 | tf_op jit(solution)/shard_map/ppermute | solution.py:436
  84.5 5.8 %collective-permute-start.11 = (bf16[1,144,128]{2,1,0:T(8,128)(2,1)S(1)}, bf16[1,144,128]{2,1,0:T(8,128)(2,1)S(1)}, u32[]{:S(2)}, u32[]{:S(2)}) collective-permute-start(bf16[1,144,128]{2,1,0:T(8,128)(2,1)S(1)} %add_convert_fusion.4), channel_id=1, source_target_pairs={{0,12},{1,13},{2,14},{3,15},{4,8},{5,9},{6,10},{7,11},{8,4},{9,5},... | collective-permute-start | bytes 110600 | tf_op jit(solution)/shard_map/ppermute | solution.py:436
  85.9 5.3 %collective-permute-start.10 = (bf16[1,144,128]{2,1,0:T(8,128)(2,1)S(1)}, bf16[1,144,128]{2,1,0:T(8,128)(2,1)S(1)}, u32[]{:S(2)}, u32[]{:S(2)}) collective-permute-start(bf16[1,144,128]{2,1,0:T(8,128)(2,1)S(1)} %add_convert_fusion.4), channel_id=1, source_target_pairs={{0,8},{1,9},{2,10},{3,11},{4,12},{5,13},{6,14},{7,15},{8,0},{9,1},... | collective-permute-start | bytes 110600 | tf_op jit(solution)/shard_map/ppermute | solution.py:436
  85.9 5.3 %collective-permute-start.9 = (bf16[1,144,128]{2,1,0:T(8,128)(2,1)S(1)}, bf16[1,144,128]{2,1,0:T(8,128)(2,1)S(1)}, u32[]{:S(2)}, u32[]{:S(2)}) collective-permute-start(bf16[1,144,128]{2,1,0:T(8,128)(2,1)S(1)} %add_convert_fusion.4), channel_id=1, source_target_pairs={{0,4},{1,5},{2,6},{3,7},{4,0},{5,1},{6,2},{7,3},{8,12},{9,13},{10,... | collective-permute-start | bytes 110600 | tf_op jit(solution)/shard_map/ppermute | solution.py:436
  91.3 6.6 %copy-start.1 = (s32[2]{0:T(128)S(1)}, s32[2]{0:T(128)}, u32[]{:S(2)}) copy-start(s32[2]{0:T(128)} %pad_add_fusion.pos_ref) | copy-start | bytes 28
  91.3 5.2 %collective-permute-start.12 = (bf16[4,144,128]{2,1,0:T(8,128)(2,1)S(1)}, bf16[4,144,128]{2,1,0:T(8,128)(2,1)S(1)}, u32[]{:S(2)}, u32[]{:S(2)}) collective-permute-start(bf16[4,144,128]{2,1,0:T(8,128)(2,1)S(1)} %pad_maximum_fusion.refs_0_), channel_id=1, source_target_pairs={{0,2},{1,3},{2,0},{3,1},{4,6},{5,7},{6,4},{7,5},{8,10},{9,11},{10,... | collective-permute-start | bytes 442376 | tf_op jit(solution)/shard_map/ppermute | solution.py:436
  93.4 3.2 %collective-permute-start.13 = (bf16[4,144,128]{2,1,0:T(8,128)(2,1)S(1)}, bf16[4,144,128]{2,1,0:T(8,128)(2,1)S(1)}, u32[]{:S(2)}, u32[]{:S(2)}) collective-permute-start(bf16[4,144,128]{2,1,0:T(8,128)(2,1)S(1)} %pad_maximum_fusion.refs_0_), channel_id=1, source_target_pairs={{0,1},{1,0},{2,3},{3,2},{4,5},{5,4},{6,7},{7,6},{8,9},{9,8},{10,11... | collective-permute-start | bytes 442376 | tf_op jit(solution)/shard_map/ppermute | solution.py:436
  96.5 1.4 %collective-permute-start.14 = (bf16[4,144,128]{2,1,0:T(8,128)(2,1)S(1)}, bf16[4,144,128]{2,1,0:T(8,128)(2,1)S(1)}, u32[]{:S(2)}, u32[]{:S(2)}) collective-permute-start(bf16[4,144,128]{2,1,0:T(8,128)(2,1)S(1)} %collective-permute-done.12.refs_1_), channel_id=1, source_target_pairs={{0,1},{1,0},{2,3},{3,2},{4,5},{5,4},{6,7},{7,6},{8,9},{9,8},{10,11... | collective-permute-start | bytes 442376 | tf_op jit(solution)/shard_map/ppermute | solution.py:436
